TPU v7x, 32 devices: a whole 2x2x4 slice. The times are simulated.
32 devices in a mesh: seq: 32 (over z, y, x, core).
Axes of the slice: x: 2, y: 2, z: 4, core: 2. Of those that a mesh axis runs over, the one named last changes fastest.
Arguments:
- tokens: bfloat16 [4096, 256], P('seq'), may hold values from -6 to 6
- cotangent: bfloat16 [4096, 256], P('seq'), may hold values from -6 to 6
- weight_in: bfloat16 [512, 1024], replicated, may hold values from -0.25 to 0.25
- bias_in: float32 [1024], replicated, may hold values from -4 to 4
- norm_gain: float32 [1024], replicated, may hold values from 0.1 to 1.9
- weight_out: bfloat16 [512, 1024], replicated, may hold values from -0.1875 to 0.1875
- bias_out: float32 [512], replicated, may hold values from -3 to 3
- gate_logit: float32 [512], replicated, may hold values from -1 to 3
Outputs:
- final_rows: bfloat16 [4096, 256], P('seq')
- grad_tokens: bfloat16 [4096, 256], P('seq')
- grad_weight_in: bfloat16 [512, 1024], replicated
- grad_weight_out: bfloat16 [512, 1024], replicated
- grad_bias_in: float32 [1024], replicated
- grad_norm_gain: float32 [1024], replicated
- grad_bias_out: float32 [512], replicated
- grad_gate_logit: float32 [512], replicated
All inputs are finite; a program needn't handle non-finite values.
Results may differ from a plain program's by a relative error of at most 0.0075.
Values may be sent and summed in bfloat16 or wider, within the bound.
No kernel may reach another device: no remote copies, remote signals or barrier semaphores. Data moves between devices by JAX's collectives and lax.ppermute only.
A program may use at most 64 MiB of HBM per device.

v0:
```python
import jax
import jax.numpy as jnp
from jax import lax
from jax.sharding import PartitionSpec as P

D = 256
HID = 1024
LAYERS = 4


epsilon = 1e-05
branch_scale = 0.25


def partner(shard, axis, distance):
    return lax.ppermute(shard, axis, [(i, i ^ 1 << distance) for i in range(lax.axis_size(axis))])


def layer_forward(paired, params):
    weight_in, bias_in, norm_gain, weight_out, bias_out, gates_on = params
    pre_norm = jnp.dot(paired, weight_in, preferred_element_type=jnp.float32) + bias_in
    row_mean = jnp.mean(pre_norm, axis=-1, keepdims=True)
    centred = pre_norm - row_mean
    variance = jnp.mean(centred * centred, axis=-1, keepdims=True)
    inv_std = lax.rsqrt(variance + epsilon)
    normed = centred * inv_std
    scaled = normed * norm_gain
    hidden = jax.nn.gelu(scaled).astype(jnp.bfloat16)
    mixed = (
        lax.dot_general(
            hidden, weight_out, (((1,), (1,)), ((), ())), preferred_element_type=jnp.float32
        )
        + bias_out
    )
    result = (gates_on * paired.astype(jnp.float32) + branch_scale * mixed).astype(jnp.bfloat16)
    return (result, (normed, inv_std, scaled, hidden))


def layer_backward(paired, stored, grad_out, params):
    weight_in, bias_in, norm_gain, weight_out, bias_out, gates_on = params
    normed, inv_std, scaled, hidden = stored
    out_grads = grad_out.astype(jnp.float32)
    gate_terms = out_grads * paired.astype(jnp.float32)
    mix_grads = branch_scale * out_grads
    mix_cast = mix_grads.astype(jnp.bfloat16)
    hidden_grads = jnp.dot(mix_cast, weight_out, preferred_element_type=jnp.float32)
    slope = jax.vjp(jax.nn.gelu, scaled)[1]
    scaled_grads = slope(hidden_grads)[0]
    gain_terms = scaled_grads * normed
    normed_grads = scaled_grads * norm_gain
    pre_grads = inv_std * (
        normed_grads
        - jnp.mean(normed_grads, axis=-1, keepdims=True)
        - normed * jnp.mean(normed_grads * normed, axis=-1, keepdims=True)
    )
    pre_cast = pre_grads.astype(jnp.bfloat16)
    back_in = lax.dot_general(
        pre_cast, weight_in, (((1,), (1,)), ((), ())), preferred_element_type=jnp.float32
    )
    pair_grads = (gates_on * out_grads + back_in).astype(jnp.bfloat16)
    return (pair_grads, (pre_grads, pre_cast, mix_grads, mix_cast, gain_terms, gate_terms))


def make_pairs(current, distance):
    rows_dev, row_width = current.shape
    viewed = current.reshape(rows_dev // (2 * distance), 2, distance, row_width)
    return jnp.concatenate([viewed[:, 0], viewed[:, 1]], axis=-1).reshape(
        rows_dev // 2, 2 * row_width
    )


def split_pairs(joined, distance):
    pair_rows, pair_width = joined.shape
    row_width = pair_width // 2
    viewed = joined.reshape(pair_rows // distance, distance, pair_width)
    return jnp.stack([viewed[:, :, :row_width], viewed[:, :, row_width:]], axis=1).reshape(
        2 * pair_rows, row_width
    )


def flip_bits(values, dev_index, top_bit, inward):
    stacks, rows_dev, row_width = values.shape
    block_rows = rows_dev // 2**LAYERS
    for bit_pos in range(LAYERS):
        bit_num = top_bit - LAYERS + bit_pos
        is_upper = dev_index // 2**bit_num % 2 == 1
        viewed = values.reshape(
            stacks, 2**LAYERS // 2 ** (bit_pos + 1), 2, 2**bit_pos * block_rows, row_width
        )
        lower_half = viewed[:, :, 0]
        upper_half = viewed[:, :, 1]
        given_half = jnp.where(is_upper, lower_half, upper_half)
        if inward:
            received = partner(given_half, "seq", bit_num)
        else:
            received = partner(given_half, "seq", bit_num)
        first_half = jnp.where(is_upper, received, lower_half)
        second_half = jnp.where(is_upper, upper_half, received)
        values = jnp.stack([first_half, second_half], axis=2).reshape(stacks, rows_dev, row_width)
    return values


def per_device(tokens, cotangent, weight_in, bias_in, norm_gain, weight_out, bias_out, gate_logit):
    rows_dev, row_width = tokens.shape
    devices = lax.axis_size("seq")
    top_bit = devices.bit_length() - 1
    dev_index = lax.axis_index("seq")
    gates_on = jax.nn.sigmoid(gate_logit)
    params = (weight_in, bias_in, norm_gain, weight_out, bias_out, gates_on)
    block_rows = rows_dev // 2**LAYERS
    both_local = flip_bits(jnp.stack([tokens, cotangent], axis=0), dev_index, top_bit, True)
    current = both_local[0]
    grads_rows = both_local[1]
    layer_pairs = []
    layer_stored = []
    for layer_num in range(LAYERS):
        distance = 2**layer_num * block_rows
        paired = make_pairs(current, distance)
        result, stored = layer_forward(paired, params)
        current = split_pairs(result, distance)
        layer_pairs.append(paired)
        layer_stored.append(stored)
    final_rows = flip_bits(current[None], dev_index, top_bit, False)[0]
    kept_pairs = []
    kept_pre = []
    kept_mix = []
    kept_hidden = []
    totals = (
        jnp.zeros((HID,), jnp.float32),
        jnp.zeros((HID,), jnp.float32),
        jnp.zeros((2 * D,), jnp.float32),
        jnp.zeros((2 * D,), jnp.float32),
    )
    for layer_num in reversed(range(LAYERS)):
        paired = layer_pairs[layer_num]
        stored = layer_stored[layer_num]
        distance = 2**layer_num * block_rows
        grad_out = make_pairs(grads_rows, distance)
        pair_grads, terms = layer_backward(paired, stored, grad_out, params)
        grads_rows = split_pairs(pair_grads, distance)
        pre_grads, pre_cast, mix_grads, mix_cast, gain_terms, gate_terms = terms
        kept_pairs.append(paired)
        kept_pre.append(pre_cast)
        kept_mix.append(mix_cast)
        kept_hidden.append(stored[3])
        totals = (
            totals[0] + jnp.sum(pre_grads, axis=0),
            totals[1] + jnp.sum(gain_terms, axis=0),
            totals[2] + jnp.sum(mix_grads, axis=0),
            totals[3] + jnp.sum(gate_terms, axis=0),
        )
    grads_rows = flip_bits(grads_rows[None], dev_index, top_bit, False)[0]
    pairs_stack = jnp.stack(kept_pairs, axis=0)
    pre_stack = jnp.stack(kept_pre, axis=0)
    mix_stack = jnp.stack(kept_mix, axis=0)
    hidden_stack = jnp.stack(kept_hidden, axis=0)
    grad_first = jnp.einsum(
        "lrc,lrh->ch", pairs_stack, pre_stack, preferred_element_type=jnp.float32
    )
    grad_second = jnp.einsum(
        "lrc,lrh->ch", mix_stack, hidden_stack, preferred_element_type=jnp.float32
    )
    both_grads = lax.psum_scatter(
        jnp.concatenate([grad_first, grad_second], axis=1), "seq", scatter_dimension=0, tiled=True
    )
    summed = lax.psum((totals[0], totals[1], totals[2], totals[3]), "seq")
    scaling = float(rows_dev * devices // 2) ** (-0.5)
    owned_cast = (both_grads * scaling).astype(jnp.bfloat16)
    whole_grads = lax.all_gather(owned_cast, "seq", axis=0, tiled=True)
    grad_weight_in = whole_grads[:, :HID]
    grad_weight_out = whole_grads[:, HID:]
    return (
        final_rows,
        grads_rows,
        grad_weight_in,
        grad_weight_out,
        summed[0] * scaling,
        summed[1] * scaling,
        summed[2] * scaling,
        summed[3] * gates_on * (1.0 - gates_on) * scaling,
    )


def solution(mesh):
    placed = (P("seq", None), P("seq", None), P(), P(), P(), P(), P(), P())
    return jax.shard_map(
        per_device,
        mesh=mesh,
        in_specs=placed,
        out_specs=(P("seq", None), P("seq", None), P(), P(), P(), P(), P(), P()),
        check_vma=False,
    )
```

profile of v0, /device:TPU:0, one launch (start us, length us, event | category | flops | bytes accessed | tf_op | source)
XLA Modules:
  0.0 250.5 jit_solution(9286799474599238168)
XLA Ops:
  7.3 0.9 broadcast_select_fusion
  8.2 3.0 %collective-permute-start = (bf16[2,8,8,256]{3,2,1,0:T(8,128)(2,1)S(1)}, bf16[2,8,8,256]{3,2,1,0:T(8,128)(2,1)S(1)}, u32[]{:S(2)}, u32[]{:S(2)}) collective-permute-start(bf16[2,8,8,256]{3,2,1,0:T(8,128)(2,1)S(1)} %broadcast_select_fusion), channel_id=1, source_target_pairs={{0,2},{1,3},{2,0},{3,1},{4,6},{5,7},{6,4},{7,5},{8,10},{9,11},{10,... | collective-permute-start | bytes 196616 | tf_op jit(solution)/shard_map/ppermute | solution.py:16
  11.2 2.2 collective-permute-done
  13.4 0.8 select_bitcast_fusion.7
  14.3 2.1 collective-permute-start.1
  16.4 2.2 collective-permute-done.1
  18.8 2.1 collective-permute-start.2
  20.9 2.2 collective-permute-done.2
  23.3 3.5 %collective-permute-start.3 = (bf16[2,1,64,256]{3,2,0,1:T(8,128)(2,1)S(1)}, bf16[2,1,64,256]{3,2,0,1:T(8,128)(2,1)S(1)}, u32[]{:S(2)}, u32[]{:S(2)}) collective-permute-start(bf16[2,1,64,256]{3,2,0,1:T(8,128)(2,1)S(1)} %broadcast_select_fusion.3), channel_id=1, source_target_pairs={{0,16},{1,17},{2,18},{3,19},{4,20},{5,21},{6,22},{7,23},{8,24},{9,... | collective-permute-start | bytes 196616 | tf_op jit(solution)/shard_map/ppermute | solution.py:16
  26.8 2.2 collective-permute-done.3
  33.8 0.5 multiply_reduce_fusion.3
  36.3 0.5 multiply_reduce_fusion.1
  39.2 2.4 pad_maximum_fusion
  42.2 1.6 collective-permute-start.4
  44.3 0.6 collective-permute-start.8
  45.1 41.5 %all-reduce = (f32[1024]{0:T(1024)S(1)}, f32[1024]{0:T(1024)S(1)}, f32[512]{0:T(512)S(1)}, f32[512]{0:T(512)S(1)}) all-reduce(f32[1024]{0:T(1024)S(1)} %add_add_fusion.1, f32[1024]{0:T(1024)S(1)} %add_add_fusion, f32[512]{0:T(512)S(1)} %add_add_fusion.3, f32[512]{0:T(512)S(1)} %add_add_fusion.2), channel_id=1, replica_groups=mesh['seq'=32] {'seq'}, use_global_device_ids=true, to_apply=%region_21.22 | all-reduce | flops 3072 | bytes 24576 | tf_op jit(solution)/shard_map/psum | solution.py:166
  86.6 0.6 broadcast_multiply_fusion.2
  87.2 0.6 multiply_multiply_fusion.8
  87.7 0.6 broadcast_multiply_fusion.1
  88.3 0.6 broadcast_multiply_fusion
  88.9 95.9 %reduce-scatter.2.cloned.1.call-done = f32[16,2048]{1,0:T(8,128)} async-done(((f32[512,2048]{1,0:T(8,128)}), f32[16,2048]{1,0:T(8,128)}) %reduce-scatter.2.cloned.1.call-update) | async-done | bytes 131088 | tf_op jit(solution)/shard_map/reduce_scatter | solution.py:163
  184.9 1.5 multiply_convert_fusion.4
  186.7 2.1 collective-permute-start.9
  188.7 1.8 collective-permute-done.5
  190.9 1.9 collective-permute-start.10
  192.8 1.8 collective-permute-done.6
  195.0 2.8 %collective-permute-start.11 = (bf16[1,1,64,256]{3,2,1,0:T(8,128)(2,1)S(1)}, bf16[1,1,64,256]{3,2,1,0:T(8,128)(2,1)S(1)}, u32[]{:S(2)}, u32[]{:S(2)}) collective-permute-start(bf16[1,1,64,256]{3,2,1,0:T(8,128)(2,1)S(1)} %broadcast_select_fusion.10), channel_id=1, source_target_pairs={{0,16},{1,17},{2,18},{3,19},{4,20},{5,21},{6,22},{7,23},{8,24},{9,... | collective-permute-start | bytes 98312 | tf_op jit(solution)/shard_map/ppermute | solution.py:16
  197.7 1.8 collective-permute-done.7
  199.6 0.6 pad_maximum_fusion.16
  200.2 0.6 pad_maximum_fusion.26
  200.8 39.8 %all-gather.2.cloned.1.call-done = bf16[512,2048]{1,0:T(8,128)(2,1)} async-done(((bf16[16,2048]{1,0:T(8,128)(2,1)}), bf16[512,2048]{1,0:T(8,128)(2,1)}) %all-gather.2.cloned.1.call-update) | async-done | bytes 2097168 | tf_op jit(solution)/shard_map/all_gather | solution.py:169
  240.7 3.0 %fusion.140 = (bf16[512,1024]{1,0:T(8,128)(2,1)}, bf16[512,1024]{1,0:T(8,128)(2,1)}) fusion(bf16[512,2048]{1,0:T(8,128)(2,1)} %all-gather.2.cloned.1.call-done), kind=kLoop, calls=%fused_computation.346 | loop fusion | bytes 4194304 | tf_op jit(solution)/shard_map/slice | solution.py:171
  (143 shorter events, 11.1 us)
Async XLA Ops:
  7.2 22.7 %copy-start = (bf16[512,1024]{1,0:T(8,128)(2,1)S(1)}, bf16[512,1024]{1,0:T(8,128)(2,1)}, u32[]{:S(2)}) copy-start(bf16[512,1024]{1,0:T(8,128)(2,1)} %param.13) | copy-start | bytes 3145732
  7.2 19.6 %copy-start.4 = (f32[512]{0:T(512)S(1)}, f32[512]{0:T(512)}, u32[]{:S(2)}) copy-start(f32[512]{0:T(512)} %param.15) | copy-start | bytes 6148
  7.2 177.7 %reduce-scatter.2.cloned.1.call-start = ((), (), s32[]{:S(2)}) async-start(), calls=%async_computation.1 | async-start | bytes 4325376 | tf_op jit(solution)/shard_map/reduce_scatter | solution.py:163
  8.2 20.9 %copy-start.1 = (bf16[512,1024]{1,0:T(8,128)(2,1)S(1)}, bf16[512,1024]{1,0:T(8,128)(2,1)}, u32[]{:S(2)}) copy-start(bf16[512,1024]{1,0:T(8,128)(2,1)} %param.10) | copy-start | bytes 3145732
  8.2 20.9 %copy-start.3 = (f32[1024]{0:T(1024)S(1)}, f32[1024]{0:T(1024)}, u32[]{:S(2)}) copy-start(f32[1024]{0:T(1024)} %param.11) | copy-start | bytes 12292
  8.2 5.2 %collective-permute-start = (bf16[2,8,8,256]{3,2,1,0:T(8,128)(2,1)S(1)}, bf16[2,8,8,256]{3,2,1,0:T(8,128)(2,1)S(1)}, u32[]{:S(2)}, u32[]{:S(2)}) collective-permute-start(bf16[2,8,8,256]{3,2,1,0:T(8,128)(2,1)S(1)} %broadcast_select_fusion), channel_id=1, source_target_pairs={{0,2},{1,3},{2,0},{3,1},{4,6},{5,7},{6,4},{7,5},{8,10},{9,11},{10,... | collective-permute-start | bytes 196616 | tf_op jit(solution)/shard_map/ppermute | solution.py:16
  14.3 4.4 %collective-permute-start.1 = (bf16[2,4,16,256]{3,2,1,0:T(8,128)(2,1)S(1)}, bf16[2,4,16,256]{3,2,1,0:T(8,128)(2,1)S(1)}, u32[]{:S(2)}, u32[]{:S(2)}) collective-permute-start(bf16[2,4,16,256]{3,2,1,0:T(8,128)(2,1)S(1)} %broadcast_select_fusion.1), channel_id=1, source_target_pairs={{0,4},{1,5},{2,6},{3,7},{4,0},{5,1},{6,2},{7,3},{8,12},{9,13},{10,... | collective-permute-start | bytes 196616 | tf_op jit(solution)/shard_map/ppermute | solution.py:16
  18.7 11.0 %copy-start.2 = (f32[1024]{0:T(1024)S(1)}, f32[1024]{0:T(1024)}, u32[]{:S(2)}) copy-start(f32[1024]{0:T(1024)} %param.12) | copy-start | bytes 12292
  18.8 11.2 %copy-start.5 = (f32[512]{0:T(512)S(1)}, f32[512]{0:T(512)}, u32[]{:S(2)}) copy-start(f32[512]{0:T(512)} %param.14) | copy-start | bytes 6148
  18.8 4.4 %collective-permute-start.2 = (bf16[2,2,32,256]{3,2,1,0:T(8,128)(2,1)S(1)}, bf16[2,2,32,256]{3,2,1,0:T(8,128)(2,1)S(1)}, u32[]{:S(2)}, u32[]{:S(2)}) collective-permute-start(bf16[2,2,32,256]{3,2,1,0:T(8,128)(2,1)S(1)} %broadcast_select_fusion.2), channel_id=1, source_target_pairs={{0,8},{1,9},{2,10},{3,11},{4,12},{5,13},{6,14},{7,15},{8,0},{9,1},... | collective-permute-start | bytes 196616 | tf_op jit(solution)/shard_map/ppermute | solution.py:16
  23.3 5.8 %collective-permute-start.3 = (bf16[2,1,64,256]{3,2,0,1:T(8,128)(2,1)S(1)}, bf16[2,1,64,256]{3,2,0,1:T(8,128)(2,1)S(1)}, u32[]{:S(2)}, u32[]{:S(2)}) collective-permute-start(bf16[2,1,64,256]{3,2,0,1:T(8,128)(2,1)S(1)} %broadcast_select_fusion.3), channel_id=1, source_target_pairs={{0,16},{1,17},{2,18},{3,19},{4,20},{5,21},{6,22},{7,23},{8,24},{9,... | collective-permute-start | bytes 196616 | tf_op jit(solution)/shard_map/ppermute | solution.py:16
  41.7 199.0 %all-gather.2.cloned.1.call-start = ((), (), s32[]{:S(2)}) async-start(), calls=%async_computation.2 | async-start | bytes 2162688 | tf_op jit(solution)/shard_map/all_gather | solution.py:169
  42.2 144.2 %collective-permute-start.4 = (bf16[1,8,8,256]{3,2,1,0:T(8,128)(2,1)S(1)}, bf16[1,8,8,256]{3,2,1,0:T(8,128)(2,1)S(1)}, u32[]{:S(2)}, u32[]{:S(2)}) collective-permute-start(bf16[1,8,8,256]{3,2,1,0:T(8,128)(2,1)S(1)} %broadcast_select_fusion.5), channel_id=1, source_target_pairs={{0,2},{1,3},{2,0},{3,1},{4,6},{5,7},{6,4},{7,5},{8,10},{9,11},{10,... | collective-permute-start | bytes 98312 | tf_op jit(solution)/shard_map/ppermute | solution.py:16
  44.3 142.3 %collective-permute-start.8 = (bf16[1,8,8,256]{3,2,1,0:T(8,128)(2,1)S(1)}, bf16[1,8,8,256]{3,2,1,0:T(8,128)(2,1)S(1)}, u32[]{:S(2)}, u32[]{:S(2)}) collective-permute-start(bf16[1,8,8,256]{3,2,1,0:T(8,128)(2,1)S(1)} %broadcast_select_fusion.4), channel_id=1, source_target_pairs={{0,2},{1,3},{2,0},{3,1},{4,6},{5,7},{6,4},{7,5},{8,10},{9,11},{10,... | collective-permute-start | bytes 98312 | tf_op jit(solution)/shard_map/ppermute | solution.py:16
  186.5 4.0 %collective-permute-start.5 = (bf16[1,4,16,256]{3,2,1,0:T(8,128)(2,1)S(1)}, bf16[1,4,16,256]{3,2,1,0:T(8,128)(2,1)S(1)}, u32[]{:S(2)}, u32[]{:S(2)}) collective-permute-start(bf16[1,4,16,256]{3,2,1,0:T(8,128)(2,1)S(1)} %broadcast_select_fusion.7), channel_id=1, source_target_pairs={{0,4},{1,5},{2,6},{3,7},{4,0},{5,1},{6,2},{7,3},{8,12},{9,13},{10,... | collective-permute-start | bytes 98312 | tf_op jit(solution)/shard_map/ppermute | solution.py:16
  186.7 4.2 %collective-permute-start.9 = (bf16[1,4,16,256]{3,2,1,0:T(8,128)(2,1)S(1)}, bf16[1,4,16,256]{3,2,1,0:T(8,128)(2,1)S(1)}, u32[]{:S(2)}, u32[]{:S(2)}) collective-permute-start(bf16[1,4,16,256]{3,2,1,0:T(8,128)(2,1)S(1)} %broadcast_select_fusion.6), channel_id=1, source_target_pairs={{0,4},{1,5},{2,6},{3,7},{4,0},{5,1},{6,2},{7,3},{8,12},{9,13},{10,... | collective-permute-start | bytes 98312 | tf_op jit(solution)/shard_map/ppermute | solution.py:16
  190.6 4.0 %collective-permute-start.6 = (bf16[1,2,32,256]{3,2,1,0:T(8,128)(2,1)S(1)}, bf16[1,2,32,256]{3,2,1,0:T(8,128)(2,1)S(1)}, u32[]{:S(2)}, u32[]{:S(2)}) collective-permute-start(bf16[1,2,32,256]{3,2,1,0:T(8,128)(2,1)S(1)} %broadcast_select_fusion.9), channel_id=1, source_target_pairs={{0,8},{1,9},{2,10},{3,11},{4,12},{5,13},{6,14},{7,15},{8,0},{9,1},... | collective-permute-start | bytes 98312 | tf_op jit(solution)/shard_map/ppermute | solution.py:16
  190.9 4.0 %collective-permute-start.10 = (bf16[1,2,32,256]{3,2,1,0:T(8,128)(2,1)S(1)}, bf16[1,2,32,256]{3,2,1,0:T(8,128)(2,1)S(1)}, u32[]{:S(2)}, u32[]{:S(2)}) collective-permute-start(bf16[1,2,32,256]{3,2,1,0:T(8,128)(2,1)S(1)} %broadcast_select_fusion.8), channel_id=1, source_target_pairs={{0,8},{1,9},{2,10},{3,11},{4,12},{5,13},{6,14},{7,15},{8,0},{9,1},... | collective-permute-start | bytes 98312 | tf_op jit(solution)/shard_map/ppermute | solution.py:16
  194.6 4.9 %collective-permute-start.7 = (bf16[1,1,64,256]{3,2,1,0:T(8,128)(2,1)S(1)}, bf16[1,1,64,256]{3,2,1,0:T(8,128)(2,1)S(1)}, u32[]{:S(2)}, u32[]{:S(2)}) collective-permute-start(bf16[1,1,64,256]{3,2,1,0:T(8,128)(2,1)S(1)} %broadcast_select_fusion.11), channel_id=1, source_target_pairs={{0,16},{1,17},{2,18},{3,19},{4,20},{5,21},{6,22},{7,23},{8,24},{9,... | collective-permute-start | bytes 98312 | tf_op jit(solution)/shard_map/ppermute | solution.py:16
  195.0 5.2 %collective-permute-start.11 = (bf16[1,1,64,256]{3,2,1,0:T(8,128)(2,1)S(1)}, bf16[1,1,64,256]{3,2,1,0:T(8,128)(2,1)S(1)}, u32[]{:S(2)}, u32[]{:S(2)}) collective-permute-start(bf16[1,1,64,256]{3,2,1,0:T(8,128)(2,1)S(1)} %broadcast_select_fusion.10), channel_id=1, source_target_pairs={{0,16},{1,17},{2,18},{3,19},{4,20},{5,21},{6,22},{7,23},{8,24},{9,... | collective-permute-start | bytes 98312 | tf_op jit(solution)/shard_map/ppermute | solution.py:16
Sparse Core Ops, SparseCore 0:
  41.8 143.0 reduce-scatter.1
  188.3 52.3 all-gather.1
where the time goes:
time: 251 us
  waiting for transfers between devices  151 us (60%)
  blocking collectives  41.5 us (17%)
  starting transfers between devices  19.9 us (8%)
  between operations  14.9 us (6%)
  other arithmetic  12.1 us (5%)
  matrix products  8.39 us (3%)
  local copies, waits for them, and re-layouts  3.24 us (1%)
    reduce_scatter x1, waiting for transfers between devices, per_device(): lax.psum_scatter(jnp.concatenate([grad_first, grad_second], axis=1), 'seq...  95.9 us
    psum x1, blocking collectives, per_device(): summed = lax.psum((totals[0], totals[1], totals[2], totals[3]), 'seq')  41.5 us
    all_gather x1, waiting for transfers between devices, per_device(): whole_grads = lax.all_gather(owned_cast, 'seq', axis=0, tiled=True)  39.8 us
    ppermute x12, starting transfers between devices, partner(): lax.ppermute(shard, axis, [(i, i ^ 1 << distance) for i in range(lax.axis...  19.8 us
    ppermute x12, waiting for transfers between devices, partner(): lax.ppermute(shard, axis, [(i, i ^ 1 << distance) for i in range(lax.axis...  14.7 us
  transfers between devices with their start and end apart: 14, of which 11 were waited for; matrix products, arithmetic and copies ran while one was open for 3% of the time, Pallas kernels for 0%

commit v1 on v0

v1 whole, which is shorter than its diff:
```python
import functools

import jax
import jax.numpy as jnp
from jax import lax
from jax.experimental import pallas as pl
from jax.experimental.pallas import tpu as pltpu
from jax.sharding import PartitionSpec as P

LAYERS = 4
LANES = 128
CHUNK = 16

epsilon = 1e-05
branch_scale = 0.25
GELU_IN = 0.7978845608028654
GELU_CUBE = 0.044715

BF16 = jnp.bfloat16
F32 = jnp.float32


def split_small(total):
    high = total.astype(BF16).astype(F32)
    return jnp.concatenate([high, total - high], axis=0).astype(BF16)


def join_small(packed):
    wide = packed.astype(F32)
    rows = wide.shape[0] // 2
    return wide[:rows] + wide[rows:]


def layer_halves(blocks, layer):
    lower = [b for b in range(len(blocks)) if not b >> layer & 1]
    upper = [b for b in range(len(blocks)) if b >> layer & 1]
    left = jnp.concatenate([blocks[b] for b in lower], axis=0)
    right = jnp.concatenate([blocks[b] for b in upper], axis=0)
    return jnp.concatenate([left, right], axis=1), lower, upper


def layer_blocks(joined, lower, upper, height, width):
    blocks = [None] * (2 * len(lower))
    for i, b in enumerate(lower):
        blocks[b] = joined[i * height : (i + 1) * height, :width]
    for i, b in enumerate(upper):
        blocks[b] = joined[i * height : (i + 1) * height, width:]
    return blocks


def switch_kernel(
    place_ref, rows_ref, win_ref, bin_ref, gain_ref, wout_ref, bout_ref, gate_ref, msg_ref,
    pre_s, normed_s, slope_s, inv_s, hidden_s, cast_s, left_s, right_s, small_s,
):
    core = place_ref[0]
    total_rows, double = rows_ref.shape
    width = double // 2
    pairs = total_rows // 2
    count = 2**LAYERS
    height = total_rows // count
    hid = win_ref.shape[1]
    quarters = msg_ref.shape[0]
    gate = 1.0 / (1.0 + jnp.exp(-gate_ref[...]))
    bias_out = bout_ref[...]
    everything = rows_ref[...]
    blocks = [everything[b * height : (b + 1) * height, :width] for b in range(count)]
    grads = [everything[b * height : (b + 1) * height, width:] for b in range(count)]
    for layer in range(LAYERS):
        paired, lower, upper = layer_halves(blocks, layer)
        span = slice(layer * pairs, (layer + 1) * pairs)
        left_s[0, span, :] = paired
        pre_s[...] = jnp.dot(paired, win_ref[...], preferred_element_type=F32)
        for c in range(pairs // CHUNK):
            here = slice(c * CHUNK, (c + 1) * CHUNK)
            there = slice(layer * pairs + c * CHUNK, layer * pairs + (c + 1) * CHUNK)
            pre = pre_s[here, :] + bin_ref[...]
            centred = pre - jnp.mean(pre, axis=-1, keepdims=True)
            variance = jnp.mean(centred * centred, axis=-1, keepdims=True)
            inv_std = lax.rsqrt(variance + epsilon)
            normed = centred * inv_std
            scaled = normed * gain_ref[...]
            square = scaled * scaled
            bent = jnp.tanh(scaled * (GELU_IN + (GELU_IN * GELU_CUBE) * square))
            half = 0.5 + 0.5 * bent
            hidden_s[there, :] = (scaled * half).astype(BF16)
            slope_s[there, :] = half + (scaled * (0.5 - 0.5 * bent * bent)) * (
                GELU_IN + (3.0 * GELU_IN * GELU_CUBE) * square
            )
            normed_s[there, :] = normed
            inv_s[there, :] = jnp.broadcast_to(inv_std, (CHUNK, LANES))
        mixed = (
            lax.dot_general(
                hidden_s[span, :], wout_ref[...], (((1,), (1,)), ((), ())),
                preferred_element_type=F32,
            )
            + bias_out
        )
        result = (gate * paired.astype(F32) + branch_scale * mixed).astype(BF16)
        blocks = layer_blocks(result, lower, upper, height, width)

    sum_pre = jnp.zeros((1, hid), F32)
    sum_gain = jnp.zeros((1, hid), F32)
    sum_mix = jnp.zeros((1, 2 * width), F32)
    sum_gate = jnp.zeros((1, 2 * width), F32)
    for layer in reversed(range(LAYERS)):
        grad_out, lower, upper = layer_halves(grads, layer)
        span = slice(layer * pairs, (layer + 1) * pairs)
        out_grads = grad_out.astype(F32)
        paired = left_s[0, span, :].astype(F32)
        sum_gate += jnp.sum(out_grads * paired, axis=0, keepdims=True)
        mix_grads = branch_scale * out_grads
        sum_mix += jnp.sum(mix_grads, axis=0, keepdims=True)
        mix_cast = mix_grads.astype(BF16)
        left_s[1, span, :] = mix_cast
        pre_s[...] = jnp.dot(mix_cast, wout_ref[...], preferred_element_type=F32)
        part_pre = jnp.zeros((CHUNK, hid), F32)
        part_gain = jnp.zeros((CHUNK, hid), F32)
        for c in range(pairs // CHUNK):
            here = slice(c * CHUNK, (c + 1) * CHUNK)
            there = slice(layer * pairs + c * CHUNK, layer * pairs + (c + 1) * CHUNK)
            normed = normed_s[there, :]
            scaled_grads = slope_s[there, :] * pre_s[here, :]
            part_gain += scaled_grads * normed
            normed_grads = scaled_grads * gain_ref[...]
            mean_grad = jnp.mean(normed_grads, axis=-1, keepdims=True)
            mean_both = jnp.mean(normed_grads * normed, axis=-1, keepdims=True)
            pre_grads = inv_s[there, :1] * (normed_grads - mean_grad - normed * mean_both)
            part_pre += pre_grads
            cast_s[there, :] = pre_grads.astype(BF16)
        sum_pre += jnp.sum(part_pre, axis=0, keepdims=True)
        sum_gain += jnp.sum(part_gain, axis=0, keepdims=True)
        back_in = lax.dot_general(
            cast_s[span, :], win_ref[...], (((1,), (1,)), ((), ())), preferred_element_type=F32
        )
        result = (gate * out_grads + back_in).astype(BF16)
        grads = layer_blocks(result, lower, upper, height, width)

    @pl.when(core == 0)
    def _():
        right_s[...] = cast_s[...]

    @pl.when(core != 0)
    def _():
        right_s[...] = hidden_s[...]

    part_rows = 2 * width // quarters
    body = part_rows * hid // LANES
    for q in range(quarters):
        here = slice(q * part_rows, (q + 1) * part_rows)
        chosen = jnp.where(core == 0, left_s[0, :, here], left_s[1, :, here])
        part = lax.dot_general(
            chosen, right_s[...], (((0,), (0,)), ((), ())), preferred_element_type=F32
        ).astype(BF16)
        for k in range(hid // LANES):
            msg_ref[q, k * part_rows : (k + 1) * part_rows, :] = part[
                :, k * LANES : (k + 1) * LANES
            ]

    row = 0
    for total in (sum_pre, sum_gain, sum_mix, sum_gate):
        for k in range(total.shape[1] // LANES):
            small_s[row : row + 1, :] = total[:, k * LANES : (k + 1) * LANES]
            row += 1
    packed = split_small(small_s[...])
    own = height // 2
    for b in range(count):
        low, high = b % quarters, b // quarters
        for t, block in enumerate((blocks[b], grads[b])):
            wide = block.astype(F32)
            mine = jnp.where(core == 0, wide[:own], wide[own:])
            tall = jnp.concatenate(
                [mine[:, k * LANES : (k + 1) * LANES] for k in range(width // LANES)], axis=0
            )
            start = body + (high * 2 + t) * tall.shape[0]
            msg_ref[low, start : start + tall.shape[0], :] = tall.astype(BF16)
    for q in range(quarters):
        msg_ref[q, msg_ref.shape[1] - packed.shape[0] :, :] = packed


def plane_kernel(sizes, place_ref, got_ref, *out_refs):
    hid, part_rows, row_tile, small_rows = sizes
    mine = place_ref[2]
    sources = got_ref.shape[0]
    peers = len(out_refs)
    slabs = hid // LANES
    share = part_rows // peers
    body = slabs * part_rows
    small = join_small(got_ref[0, -2 * small_rows :, :])
    for s in range(1, sources):
        small = small + join_small(got_ref[s, -2 * small_rows :, :])
    packed = split_small(small)
    for k, out_ref in enumerate(out_refs):
        peer = mine ^ k
        for b in range(slabs):
            rows = pl.ds(pl.multiple_of(b * part_rows + peer * share, share), share)
            total = got_ref[0, rows, :].astype(F32)
            for s in range(1, sources):
                total = total + got_ref[s, rows, :].astype(F32)
            out_ref[b * share : (b + 1) * share, :] = total.astype(BF16)
        for s in range(sources):
            rows = pl.ds(pl.multiple_of(body + peer * row_tile, row_tile), row_tile)
            start = slabs * share + s * row_tile
            out_ref[start : start + row_tile, :] = got_ref[s, rows, :]
        out_ref[-2 * small_rows :, :] = packed


def column_kernel(sizes, scaling, place_ref, gate_ref, *refs):
    hid, part_rows, row_tile, small_rows, width, sources = sizes
    peers = (len(refs) - 7)
    got = refs[:peers]
    slice_ref, final_ref, grad_ref, pre_ref, gain_ref, mix_ref, gout_ref = refs[peers:]
    mine = place_ref[2]
    slabs = hid // LANES
    share = part_rows // peers

    def add(pick):
        terms = [pick(ref) for ref in got]
        while len(terms) > 1:
            terms = [terms[i] + terms[i + 1] for i in range(0, len(terms), 2)]
        return terms[0]

    for b in range(slabs):
        total = add(lambda ref: ref[b * share : (b + 1) * share, :].astype(F32))
        slice_ref[:, b * LANES : (b + 1) * LANES] = (total * scaling).astype(slice_ref.dtype)
    half = row_tile // 2
    own = half // (width // LANES)
    for k, ref in enumerate(got):
        peer = mine ^ k
        rows = pl.ds(pl.multiple_of(peer * (own * sources), own * sources), own * sources)
        for t, out_ref in enumerate((final_ref, grad_ref)):
            pieces = []
            for s in range(sources):
                start = slabs * share + s * row_tile + t * half
                tall = ref[start : start + half, :].astype(F32)
                pieces.append(
                    jnp.concatenate(
                        [tall[i * own : (i + 1) * own] for i in range(width // LANES)], axis=1
                    )
                )
            out_ref[rows, :] = jnp.concatenate(pieces, axis=0).astype(BF16)
    small = add(lambda ref: join_small(ref[-2 * small_rows :, :])) * scaling
    gate = 1.0 / (1.0 + jnp.exp(-gate_ref[...]))
    first = 0
    for out_ref in (pre_ref, gain_ref, mix_ref, gout_ref):
        count = out_ref.shape[0]
        part = small[first : first + count]
        if out_ref is gout_ref:
            part = part * gate * (1.0 - gate)
        out_ref[...] = part
        first += count


def gather_kernel(place_ref, *refs):
    *got, out_ref = refs
    mine = place_ref[2]
    share = got[0].shape[0]
    for k, ref in enumerate(got):
        rows = pl.ds(pl.multiple_of((mine ^ k) * share, share), share)
        for q in range(out_ref.shape[0]):
            out_ref[q, rows, :] = ref[...]


def order_kernel(place_ref, mine_ref, other_ref, first_ref, second_ref, sems):
    def move(first_src, second_src):
        one = pltpu.make_async_copy(first_src, first_ref, sems.at[0])
        two = pltpu.make_async_copy(second_src, second_ref, sems.at[1])
        one.start()
        two.start()
        one.wait()
        two.wait()

    @pl.when(place_ref[0] == 0)
    def _():
        move(mine_ref, other_ref)

    @pl.when(place_ref[0] != 0)
    def _():
        move(other_ref, mine_ref)


def bit_groups(devices, bits):
    masks = [sum(1 << b for i, b in enumerate(bits) if j >> i & 1) for j in range(2 ** len(bits))]
    every = sum(1 << b for b in bits)
    return [[base | m for m in masks] for base in range(devices) if not base & every]


def exchange(value, devices, bits):
    groups = None if 2 ** len(bits) == devices else bit_groups(devices, bits)
    return lax.all_to_all(value, "seq", 0, 0, axis_index_groups=groups)


def send(value, devices, mask):
    return lax.ppermute(value, "seq", [(i, i ^ mask) for i in range(devices)])


VMEM = pl.BlockSpec(memory_space=pltpu.VMEM)
SMEM = pl.BlockSpec(memory_space=pltpu.SMEM)
PARAMS = pltpu.CompilerParams(vmem_limit_bytes=48 * 1024 * 1024)


def per_device(tokens, cotangent, weight_in, bias_in, norm_gain, weight_out, bias_out, gate_logit):
    rows_dev, width = tokens.shape
    hid = weight_in.shape[1]
    devices = lax.axis_size("seq")
    top_bit = devices.bit_length() - 1
    index = lax.axis_index("seq").astype(jnp.int32)
    count = 2**LAYERS
    block_rows = rows_dev // count
    quarters = 4
    peers = 4
    place = jnp.stack([index & 1, index >> 1 & 3, index >> 3 & 3])
    both = jnp.concatenate(
        [tokens.reshape(count, block_rows, width), cotangent.reshape(count, block_rows, width)],
        axis=-1,
    )
    outgoing = jnp.broadcast_to(both[:, None], (count, 2, block_rows, 2 * width))
    outgoing = outgoing.reshape(2 * count, block_rows, 2 * width)
    top_bits = list(range(top_bit - LAYERS, top_bit))
    rows = exchange(outgoing, devices, [0] + top_bits).reshape(
        2 * count * block_rows, 2 * width
    )

    part_rows = 2 * width // quarters
    small_rows = (2 * hid + 4 * width) // LANES
    row_tile = 2 * block_rows * width // LANES
    pairs = count * block_rows
    msg_rows = part_rows * hid // LANES + (count // quarters) * row_tile + 2 * small_rows
    message = pl.pallas_call(
        switch_kernel,
        out_shape=jax.ShapeDtypeStruct((quarters, msg_rows, LANES), BF16),
        in_specs=[SMEM] + [VMEM] * 7,
        out_specs=VMEM,
        scratch_shapes=[
            pltpu.VMEM((pairs, hid), F32),
            pltpu.VMEM((LAYERS * pairs, hid), F32),
            pltpu.VMEM((LAYERS * pairs, hid), F32),
            pltpu.VMEM((LAYERS * pairs, LANES), F32),
            pltpu.VMEM((LAYERS * pairs, hid), BF16),
            pltpu.VMEM((LAYERS * pairs, hid), BF16),
            pltpu.VMEM((2, LAYERS * pairs, 2 * width), BF16),
            pltpu.VMEM((LAYERS * pairs, hid), BF16),
            pltpu.VMEM((small_rows, LANES), F32),
        ],
        compiler_params=PARAMS,
        name="switch_layers",
    )(
        place, rows, weight_in, bias_in[None], norm_gain[None], weight_out, bias_out[None],
        gate_logit[None],
    )

    got = exchange(message, devices, [1, 2])
    share = part_rows // peers
    out_rows = share * hid // LANES + quarters * row_tile + 2 * small_rows
    piece = jax.ShapeDtypeStruct((out_rows, LANES), BF16)
    pieces = pl.pallas_call(
        functools.partial(plane_kernel, (hid, part_rows, row_tile, small_rows)),
        out_shape=[piece] * peers,
        in_specs=[SMEM, VMEM],
        out_specs=[VMEM] * peers,
        compiler_params=PARAMS,
        name="plane_sum",
    )(place, got)
    arrived = [pieces[0]] + [send(pieces[k], devices, k << 3) for k in range(1, peers)]

    scaling = float(rows_dev * devices // 2) ** (-0.5)
    merged = top_bit == LAYERS + 1
    rows_shape = jax.ShapeDtypeStruct((rows_dev, width), BF16)
    slice_type = BF16 if merged else F32
    outs = pl.pallas_call(
        functools.partial(
            column_kernel,
            (hid, part_rows, row_tile, small_rows, width, quarters),
            scaling,
        ),
        out_shape=[
            jax.ShapeDtypeStruct((share, hid), slice_type),
            rows_shape,
            rows_shape,
            jax.ShapeDtypeStruct((hid // LANES, LANES), F32),
            jax.ShapeDtypeStruct((hid // LANES, LANES), F32),
            jax.ShapeDtypeStruct((2 * width // LANES, LANES), F32),
            jax.ShapeDtypeStruct((2 * width // LANES, LANES), F32),
        ],
        in_specs=[SMEM] + [VMEM] * (peers + 1),
        out_specs=[VMEM] * 7,
        compiler_params=PARAMS,
        name="column_sum",
    )(place, gate_logit.reshape(-1, LANES), *arrived)
    owned, final_rows, grad_rows, *small = outs
    if not merged:
        rest = bit_groups(devices, list(range(LAYERS + 1, top_bit)))
        owned, *small = lax.psum((owned, *small), "seq", axis_index_groups=rest)
        owned = owned.astype(BF16)
        final_rows, grad_rows = outward_rows(
            message, devices, top_bits, rows_dev, width, part_rows * hid // LANES
        )

    slices = [owned] + [send(owned, devices, k << 3) for k in range(1, peers)]
    spread = pl.pallas_call(
        gather_kernel,
        out_shape=jax.ShapeDtypeStruct((quarters, part_rows, hid), BF16),
        in_specs=[SMEM] + [VMEM] * peers,
        out_specs=VMEM,
        compiler_params=PARAMS,
        name="column_gather",
    )(place, *slices)
    whole = exchange(spread, devices, [1, 2]).reshape(2 * width, hid)
    other = send(whole, devices, 1)
    grad_weight = jax.ShapeDtypeStruct((2 * width, hid), BF16)
    grad_weight_in, grad_weight_out = pl.pallas_call(
        order_kernel,
        out_shape=[grad_weight] * 2,
        in_specs=[SMEM, VMEM, VMEM],
        out_specs=[pl.BlockSpec(memory_space=pl.ANY)] * 2,
        scratch_shapes=[pltpu.SemaphoreType.DMA((2,))],
        compiler_params=PARAMS,
        name="weight_order",
    )(place, whole, other)
    return (final_rows, grad_rows, grad_weight_in, grad_weight_out, *(s.reshape(-1) for s in small))


def outward_rows(message, devices, top_bits, rows_dev, width, body):
    quarters = message.shape[0]
    count = 2**LAYERS
    block_rows = rows_dev // count
    tail = count // quarters * 2 * block_rows * width // LANES
    shaped = message[:, body : body + tail].reshape(
        quarters, count // quarters, 2, width // LANES, block_rows, LANES
    )
    blocks = shaped.transpose(1, 0, 2, 4, 3, 5).reshape(count, 2, block_rows, width)
    back = exchange(blocks, devices, top_bits)
    return back[:, 0].reshape(rows_dev, width), back[:, 1].reshape(rows_dev, width)


def solution(mesh):
    placed = (P("seq", None), P("seq", None), P(), P(), P(), P(), P(), P())
    return jax.shard_map(
        per_device,
        mesh=mesh,
        in_specs=placed,
        out_specs=(P("seq", None), P("seq", None), P(), P(), P(), P(), P(), P()),
        check_vma=False,
    )
```

time: 251 us -> 92 us (0.37)
  waiting for transfers between devices: 151 us -> 23.3 us
  between operations: 14.9 us -> 0.7 us
  Pallas kernels: 0 us -> 13.1 us
  other arithmetic: 12.1 us -> 1.05 us
  blocking collectives: 41.5 us -> 32.7 us
  matrix products: 8.39 us -> 0 us
  starting transfers between devices: 19.9 us -> 16.1 us
    reduce_scatter x1 -> x0, waiting for transfers between devices: 95.9 us -> none  [per_device(): lax.psum_scatter(jnp.concatenate([grad_first, grad_second], axis=1), 'seq...]
    psum x1 -> x0, blocking collectives: 41.5 us -> none  [per_device(): summed = lax.psum((totals[0], totals[1], totals[2], totals[3]), 'seq')]
    all_gather x1 -> x0, waiting for transfers between devices: 39.8 us -> none  [per_device(): whole_grads = lax.all_gather(owned_cast, 'seq', axis=0, tiled=True)]
    all_to_all x0 -> x2, blocking collectives: none -> 32.7 us  [exchange(): return lax.all_to_all(value, 'seq', 0, 0, axis_index_groups=groups)]
    pallas_call x0 -> x5, Pallas kernels: none -> 13.1 us  [the longest x1 8.7 us: per_device(): pl.pallas_call(switch_kernel, out_shape=jax.ShapeDtypeStruct((quarters, m...]
    ppermute x12 -> x7, starting transfers between devices: 19.8 us -> 8.84 us  [send(): return lax.ppermute(value, 'seq', [(i, i ^ mask) for i in range(devices)])]
    all_to_all x0 -> x1, waiting for transfers between devices: none -> 10.5 us  [exchange(): return lax.all_to_all(value, 'seq', 0, 0, axis_index_groups=groups)]
    dot_general x18 -> x0, matrix products: 8.39 us -> none  [the longest x4 2.17 us: layer_backward(): jnp.dot(mix_cast, weight_out, preferred_element_type=jnp.float32)]
  transfers between devices with their start and end apart: 14 -> 8, of which waited for: 11 -> 6; matrix products, arithmetic and copies ran while one was open for 3% -> 0% of each run, Pallas kernels for 0% -> 0%
where the time goes in v1:
time: 92 us; the launch traced here: 91.6 us
  blocking collectives  32.7 us (36%)
  waiting for transfers between devices  23.3 us (25%)
  starting transfers between devices  16.1 us (18%)
  Pallas kernels  13.1 us (14%)
  local copies, waits for them, and re-layouts  4.69 us (5%)
  other arithmetic  1.05 us (1%)
    all_to_all x2, blocking collectives, exchange(): return lax.all_to_all(value, 'seq', 0, 0, axis_index_groups=groups)  32.7 us
    ppermute x7, waiting for transfers between devices, send(): return lax.ppermute(value, 'seq', [(i, i ^ mask) for i in range(devices)])  12.8 us
    all_to_all x1, waiting for transfers between devices, exchange(): return lax.all_to_all(value, 'seq', 0, 0, axis_index_groups=groups)  10.5 us
    ppermute x7, starting transfers between devices, send(): return lax.ppermute(value, 'seq', [(i, i ^ mask) for i in range(devices)])  8.84 us
    pallas_call x1, Pallas kernels, per_device(): pl.pallas_call(switch_kernel, out_shape=jax.ShapeDtypeStruct((quarters, m...  8.7 us
    all_to_all x1, starting transfers between devices, exchange(): return lax.all_to_all(value, 'seq', 0, 0, axis_index_groups=groups)  7.3 us
    unnamed x12, local copies, waits for them, and re-layouts  3.96 us
    pallas_call x1, Pallas kernels, per_device(): pl.pallas_call(order_kernel, out_shape=[grad_weight] * 2, in_specs=[SMEM,...  1.87 us
  transfers between devices with their start and end apart: 8, of which 6 were waited for; matrix products, arithmetic and copies ran while one was open for 0% of the time, Pallas kernels for 0%

profile of v1, /device:TPU:0, one launch (start us, length us, event | category | flops | bytes accessed | tf_op | source)
XLA Modules:
  0.0 91.6 jit_solution(17117863487384908567)
XLA Ops:
  0.6 0.0 copy-start
  0.6 1.0 %pad_maximum_fusion = bf16[16,8,512]{2,1,0:T(8,128)(2,1)S(1)} fusion(bf16[16,8,256]{2,1,0:T(8,128)(2,1)} %bitcast.25, bf16[16,8,256]{2,1,0:T(8,128)(2,1)} %bitcast.26), kind=kLoop, calls=%fused_computation | loop fusion | flops 262144 | bytes 262144 | tf_op jit(solution)/shard_map/concatenate | solution.py:312
  1.6 0.7 broadcast_in_dim.18
  2.3 7.3 %all-to-all-start = ((bf16[32,8,512]{2,1,0:T(8,128)(2,1)}), bf16[32,8,512]{2,1,0:T(8,128)(2,1)S(1)}, u32[]{:S(2)}, u32[]{:S(2)}) async-start(bf16[32,8,512]{2,1,0:T(8,128)(2,1)} %bitcast.6), calls=%async_computation | async-start | bytes 524288 | tf_op jit(solution)/shard_map/all_to_all | solution.py:289
  9.7 0.1 pad_add_fusion.place_ref
  9.7 10.5 %all-to-all-done = bf16[32,8,512]{2,1,0:T(8,128)(2,1)S(1)} async-done(((bf16[32,8,512]{2,1,0:T(8,128)(2,1)}), bf16[32,8,512]{2,1,0:T(8,128)(2,1)S(1)}, u32[]{:S(2)}, u32[]{:S(2)}) %all-to-all-start) | async-done | bytes 262176 | tf_op jit(solution)/shard_map/all_to_all | solution.py:289
  20.2 1.2 %copy-done.1 = bf16[512,1024]{1,0:T(8,128)(2,1)S(1)} copy-done((bf16[512,1024]{1,0:T(8,128)(2,1)S(1)}, bf16[512,1024]{1,0:T(8,128)(2,1)}, u32[]{:S(2)}) %copy-start.1) | copy-done | bytes 1048600
  21.5 0.7 copy-done.2
  22.2 0.7 copy-done.3
  22.8 0.7 copy-done.4
  23.5 0.7 copy-done.5
  24.2 8.7 %switch_layers.1 = bf16[4,1200,128]{2,1,0:T(8,128)(2,1)S(1)} custom-call(s32[3]{0:T(128)S(1)} %pad_add_fusion.place_ref, bf16[256,512]{1,0:T(8,128)(2,1)S(1)} %bitcast.19, bf16[512,1024]{1,0:T(8,128)(2,1)S(1)} %copy-done, f32[1,1024]{1,0:T(1,128)S(1)} %bitcast.22, f32[1,1024]{1,0:T(1,128)S(1)} %bitcast.23, bf16[512,1024]{1,0:T(8,128)(2,1)S(1)} %copy-done.1, ...), custom_call_target="tpu_custom_call" | custom-call | tf_op jit(solution)/shard_map/switch_layers/pallas_call | solution.py:328
  32.9 19.1 %all_to_all.15.got_ref = bf16[4,1200,128]{2,1,0:T(8,128)(2,1)S(1)} all-to-all(bf16[4,1200,128]{2,1,0:T(8,128)(2,1)S(1)} %switch_layers.1), channel_id=1, replica_groups={{0,2,4,6},{1,3,5,7},{8,10,12,14},{9,11,13,15},{16,18,20,22},{17,19,21,2..., dimensions={0} | all-to-all | bytes 2457600 | tf_op jit(solution)/shard_map/all_to_all | solution.py:289
  52.0 0.7 plane_sum.1
  52.7 0.1 collective-permute-start
  52.8 1.6 %collective-permute-start.1 = (bf16[432,128]{1,0:T(8,128)(2,1)S(1)}, bf16[432,128]{1,0:T(8,128)(2,1)S(1)}, u32[]{:S(2)}, u32[]{:S(2)}) collective-permute-start(bf16[432,128]{1,0:T(8,128)(2,1)S(1)} %get-tuple-element.23), channel_id=1, source_target_pairs={{0,16},{1,17},{2,18},{3,19},{4,20},{5,21},{6,22},{7,23},{8,24},{9,... | collective-permute-start | bytes 331784 | tf_op jit(solution)/shard_map/ppermute | solution.py:293
  54.5 2.7 %collective-permute-start.2 = (bf16[432,128]{1,0:T(8,128)(2,1)S(1)}, bf16[432,128]{1,0:T(8,128)(2,1)S(1)}, u32[]{:S(2)}, u32[]{:S(2)}) collective-permute-start(bf16[432,128]{1,0:T(8,128)(2,1)S(1)} %get-tuple-element.24), channel_id=1, source_target_pairs={{0,24},{1,25},{2,26},{3,27},{4,28},{5,29},{6,30},{7,31},{8,16},{9,... | collective-permute-start | bytes 331784 | tf_op jit(solution)/shard_map/ppermute | solution.py:293
  57.1 0.5 collective-permute-done.refs_1_
  57.6 5.8 %collective-permute-done.1.refs_2_ = bf16[432,128]{1,0:T(8,128)(2,1)S(1)} collective-permute-done((bf16[432,128]{1,0:T(8,128)(2,1)S(1)}, bf16[432,128]{1,0:T(8,128)(2,1)S(1)}, u32[]{:S(2)}, u32[]{:S(2)}) %collective-permute-start.1) | collective-permute-done | bytes 110624 | tf_op jit(solution)/shard_map/ppermute | solution.py:293
  63.4 0.0 collective-permute-done.2.refs_3_
  63.4 1.2 %column_sum.1 = (bf16[32,1024]{1,0:T(8,128)(2,1)S(1)}, bf16[128,256]{1,0:T(8,128)(2,1)}, bf16[128,256]{1,0:T(8,128)(2,1)}, f32[8,128]{1,0:T(8,128)}, f32[8,128]{...) custom-call(s32[3]{0:T(128)S(1)} %pad_add_fusion.place_ref, f32[4,128]{1,0:T(4,128)S(1)} %bitcast.21, ...), custom_call_target="tpu_custom_call" | custom-call | tf_op jit(solution)/shard_map/column_sum/pallas_call | solution.py:369
  64.6 2.2 %collective-permute-start.5 = (bf16[32,1024]{1,0:T(8,128)(2,1)S(1)}, bf16[32,1024]{1,0:T(8,128)(2,1)S(1)}, u32[]{:S(2)}, u32[]{:S(2)}) collective-permute-start(bf16[32,1024]{1,0:T(8,128)(2,1)S(1)} %get-tuple-element.27.refs_0_), channel_id=1, source_target_pairs={{0,24},{1,25},{2,26},{3,27},{4,28},{5,29},{6,30},{7,31},{8,16},{9,... | collective-permute-start | bytes 196616 | tf_op jit(solution)/shard_map/ppermute | solution.py:293
  66.8 1.0 %collective-permute-start.4 = (bf16[32,1024]{1,0:T(8,128)(2,1)S(1)}, bf16[32,1024]{1,0:T(8,128)(2,1)S(1)}, u32[]{:S(2)}, u32[]{:S(2)}) collective-permute-start(bf16[32,1024]{1,0:T(8,128)(2,1)S(1)} %get-tuple-element.27.refs_0_), channel_id=1, source_target_pairs={{0,16},{1,17},{2,18},{3,19},{4,20},{5,21},{6,22},{7,23},{8,24},{9,... | collective-permute-start | bytes 196616 | tf_op jit(solution)/shard_map/ppermute | solution.py:293
  67.8 1.2 %collective-permute-start.3 = (bf16[32,1024]{1,0:T(8,128)(2,1)S(1)}, bf16[32,1024]{1,0:T(8,128)(2,1)S(1)}, u32[]{:S(2)}, u32[]{:S(2)}) collective-permute-start(bf16[32,1024]{1,0:T(8,128)(2,1)S(1)} %get-tuple-element.27.refs_0_), channel_id=1, source_target_pairs={{0,8},{1,9},{2,10},{3,11},{4,12},{5,13},{6,14},{7,15},{8,0},{9,1},... | collective-permute-start | bytes 196616 | tf_op jit(solution)/shard_map/ppermute | solution.py:293
  69.0 2.4 %collective-permute-done.5.refs_3_ = bf16[32,1024]{1,0:T(8,128)(2,1)S(1)} collective-permute-done((bf16[32,1024]{1,0:T(8,128)(2,1)S(1)}, bf16[32,1024]{1,0:T(8,128)(2,1)S(1)}, u32[]{:S(2)}, u32[]{:S(2)}) %collective-permute-start.5) | collective-permute-done | bytes 65568 | tf_op jit(solution)/shard_map/ppermute | solution.py:293
  71.4 1.4 %collective-permute-done.4.refs_2_ = bf16[32,1024]{1,0:T(8,128)(2,1)S(1)} collective-permute-done((bf16[32,1024]{1,0:T(8,128)(2,1)S(1)}, bf16[32,1024]{1,0:T(8,128)(2,1)S(1)}, u32[]{:S(2)}, u32[]{:S(2)}) %collective-permute-start.4) | collective-permute-done | bytes 65568 | tf_op jit(solution)/shard_map/ppermute | solution.py:293
  72.9 0.0 collective-permute-done.3.refs_1_
  72.9 0.6 column_gather.1
  73.5 13.6 %all_to_all.16 = bf16[4,128,1024]{2,1,0:T(8,128)(2,1)S(1)} all-to-all(bf16[4,128,1024]{2,1,0:T(8,128)(2,1)S(1)} %column_gather.1), channel_id=1, replica_groups={{0,2,4,6},{1,3,5,7},{8,10,12,14},{9,11,13,15},{16,18,20,22},{17,19,21,2..., dimensions={0} | all-to-all | bytes 2097152 | tf_op jit(solution)/shard_map/all_to_all | solution.py:289
  87.1 0.0 collective-permute-start.6
  87.1 2.7 %collective-permute-done.6.other_ref = bf16[512,1024]{1,0:T(8,128)(2,1)S(1)} collective-permute-done((bf16[512,1024]{1,0:T(8,128)(2,1)S(1)}, bf16[512,1024]{1,0:T(8,128)(2,1)S(1)}, u32[]{:S(2)}, u32[]{:S(2)}) %collective-permute-start.6) | collective-permute-done | bytes 1048608 | tf_op jit(solution)/shard_map/ppermute | solution.py:293
  89.8 1.9 %weight_order.1 = (bf16[512,1024]{1,0:T(8,128)(2,1)}, bf16[512,1024]{1,0:T(8,128)(2,1)}) custom-call(s32[3]{0:T(128)S(1)} %pad_add_fusion.place_ref, bf16[512,1024]{1,0:T(8,128)(2,1)S(1)} %bitcast.18, bf16[512,1024]{1,0:T(8,128)(2,1)S(1)} %collective-permute-done.6.other_ref), custom_call_target="tpu_custom_call" | custom-call | tf_op jit(solution)/shard_map/weight_order/pallas_call | solution.py:410
  (6 shorter events, 0.0 us)
Async XLA Ops:
  0.6 19.6 %copy-start = (bf16[512,1024]{1,0:T(8,128)(2,1)S(1)}, bf16[512,1024]{1,0:T(8,128)(2,1)}, u32[]{:S(2)}) copy-start(bf16[512,1024]{1,0:T(8,128)(2,1)} %win_ref.1) | copy-start | bytes 3145732
  2.3 17.9 %all-to-all-start = ((bf16[32,8,512]{2,1,0:T(8,128)(2,1)}), bf16[32,8,512]{2,1,0:T(8,128)(2,1)S(1)}, u32[]{:S(2)}, u32[]{:S(2)}) async-start(bf16[32,8,512]{2,1,0:T(8,128)(2,1)} %bitcast.6), calls=%async_computation | async-start | bytes 524288 | tf_op jit(solution)/shard_map/all_to_all | solution.py:289
  20.2 1.2 %copy-start.1 = (bf16[512,1024]{1,0:T(8,128)(2,1)S(1)}, bf16[512,1024]{1,0:T(8,128)(2,1)}, u32[]{:S(2)}) copy-start(bf16[512,1024]{1,0:T(8,128)(2,1)} %wout_ref.1) | copy-start | bytes 3145732
  21.5 0.7 copy-start.2
  22.2 0.7 copy-start.3
  22.8 0.7 copy-start.4
  23.5 0.7 copy-start.5
  52.7 5.0 %collective-permute-start = (bf16[432,128]{1,0:T(8,128)(2,1)S(1)}, bf16[432,128]{1,0:T(8,128)(2,1)S(1)}, u32[]{:S(2)}, u32[]{:S(2)}) collective-permute-start(bf16[432,128]{1,0:T(8,128)(2,1)S(1)} %get-tuple-element.22), channel_id=1, source_target_pairs={{0,8},{1,9},{2,10},{3,11},{4,12},{5,13},{6,14},{7,15},{8,0},{9,1},... | collective-permute-start | bytes 331784 | tf_op jit(solution)/shard_map/ppermute | solution.py:293
  52.8 10.6 %collective-permute-start.1 = (bf16[432,128]{1,0:T(8,128)(2,1)S(1)}, bf16[432,128]{1,0:T(8,128)(2,1)S(1)}, u32[]{:S(2)}, u32[]{:S(2)}) collective-permute-start(bf16[432,128]{1,0:T(8,128)(2,1)S(1)} %get-tuple-element.23), channel_id=1, source_target_pairs={{0,16},{1,17},{2,18},{3,19},{4,20},{5,21},{6,22},{7,23},{8,24},{9,... | collective-permute-start | bytes 331784 | tf_op jit(solution)/shard_map/ppermute | solution.py:293
  54.5 8.9 %collective-permute-start.2 = (bf16[432,128]{1,0:T(8,128)(2,1)S(1)}, bf16[432,128]{1,0:T(8,128)(2,1)S(1)}, u32[]{:S(2)}, u32[]{:S(2)}) collective-permute-start(bf16[432,128]{1,0:T(8,128)(2,1)S(1)} %get-tuple-element.24), channel_id=1, source_target_pairs={{0,24},{1,25},{2,26},{3,27},{4,28},{5,29},{6,30},{7,31},{8,16},{9,... | collective-permute-start | bytes 331784 | tf_op jit(solution)/shard_map/ppermute | solution.py:293
  64.6 6.8 %collective-permute-start.5 = (bf16[32,1024]{1,0:T(8,128)(2,1)S(1)}, bf16[32,1024]{1,0:T(8,128)(2,1)S(1)}, u32[]{:S(2)}, u32[]{:S(2)}) collective-permute-start(bf16[32,1024]{1,0:T(8,128)(2,1)S(1)} %get-tuple-element.27.refs_0_), channel_id=1, source_target_pairs={{0,24},{1,25},{2,26},{3,27},{4,28},{5,29},{6,30},{7,31},{8,16},{9,... | collective-permute-start | bytes 196616 | tf_op jit(solution)/shard_map/ppermute | solution.py:293
  66.8 6.0 %collective-permute-start.4 = (bf16[32,1024]{1,0:T(8,128)(2,1)S(1)}, bf16[32,1024]{1,0:T(8,128)(2,1)S(1)}, u32[]{:S(2)}, u32[]{:S(2)}) collective-permute-start(bf16[32,1024]{1,0:T(8,128)(2,1)S(1)} %get-tuple-element.27.refs_0_), channel_id=1, source_target_pairs={{0,16},{1,17},{2,18},{3,19},{4,20},{5,21},{6,22},{7,23},{8,24},{9,... | collective-permute-start | bytes 196616 | tf_op jit(solution)/shard_map/ppermute | solution.py:293
  67.8 5.1 %collective-permute-start.3 = (bf16[32,1024]{1,0:T(8,128)(2,1)S(1)}, bf16[32,1024]{1,0:T(8,128)(2,1)S(1)}, u32[]{:S(2)}, u32[]{:S(2)}) collective-permute-start(bf16[32,1024]{1,0:T(8,128)(2,1)S(1)} %get-tuple-element.27.refs_0_), channel_id=1, source_target_pairs={{0,8},{1,9},{2,10},{3,11},{4,12},{5,13},{6,14},{7,15},{8,0},{9,1},... | collective-permute-start | bytes 196616 | tf_op jit(solution)/shard_map/ppermute | solution.py:293
  87.1 2.7 %collective-permute-start.6 = (bf16[512,1024]{1,0:T(8,128)(2,1)S(1)}, bf16[512,1024]{1,0:T(8,128)(2,1)S(1)}, u32[]{:S(2)}, u32[]{:S(2)}) collective-permute-start(bf16[512,1024]{1,0:T(8,128)(2,1)S(1)} %bitcast.17), channel_id=1, source_target_pairs={{0,1},{1,0},{2,3},{3,2},{4,5},{5,4},{6,7},{7,6},{8,9},{9,8},{10,11... | collective-permute-start | bytes 3145736 | tf_op jit(solution)/shard_map/ppermute | solution.py:293

commit v2 on v1

v2 whole, which is shorter than its diff:
```python
import functools

import jax
import jax.numpy as jnp
from jax import lax
from jax.experimental import pallas as pl
from jax.experimental.pallas import tpu as pltpu
from jax.sharding import PartitionSpec as P

LAYERS = 4
LANES = 128
CHUNK = 16

epsilon = 1e-05
branch_scale = 0.25
GELU_IN = 0.7978845608028654
GELU_CUBE = 0.044715

BF16 = jnp.bfloat16
F32 = jnp.float32


def split_small(total):
    high = total.astype(BF16).astype(F32)
    return jnp.concatenate([high, total - high], axis=0).astype(BF16)


def join_small(packed):
    wide = packed.astype(F32)
    rows = wide.shape[0] // 2
    return wide[:rows] + wide[rows:]


def layer_halves(blocks, layer):
    lower = [b for b in range(len(blocks)) if not b >> layer & 1]
    upper = [b for b in range(len(blocks)) if b >> layer & 1]
    left = jnp.concatenate([blocks[b] for b in lower], axis=0)
    right = jnp.concatenate([blocks[b] for b in upper], axis=0)
    return jnp.concatenate([left, right], axis=1), lower, upper


def layer_blocks(joined, lower, upper, height, width):
    blocks = [None] * (2 * len(lower))
    for i, b in enumerate(lower):
        blocks[b] = joined[i * height : (i + 1) * height, :width]
    for i, b in enumerate(upper):
        blocks[b] = joined[i * height : (i + 1) * height, width:]
    return blocks


def entry_kernel(tokens_ref, cotangent_ref, out_ref):
    copies, keys, twins, height, double = out_ref.shape
    for key in range(keys):
        here = slice(key * height, (key + 1) * height)
        both = jnp.concatenate([tokens_ref[here, :], cotangent_ref[here, :]], axis=1)
        for copy in range(copies):
            for twin in range(twins):
                out_ref[copy, key, twin] = both


def keep_kernel(*refs):
    half = len(refs) // 2
    for source, target in zip(refs[:half], refs[half:]):
        target[...] = source[...]


def switch_kernel(
    place_ref, rows_ref, win_ref, bin_ref, gain_ref, wout_ref, bout_ref, gate_ref, msg_ref,
    pre_s, normed_s, slope_s, inv_s, hidden_s, cast_s, paired_s, mix_s, small_s, ends_s,
    left_s, right_s,
):
    core = place_ref[0]
    copy = place_ref[1]
    total_rows, double = rows_ref.shape
    width = double // 2
    pairs = total_rows // 2
    count = 2**LAYERS
    height = total_rows // count
    hid = win_ref.shape[1]
    keys = msg_ref.shape[0]
    gate = 1.0 / (1.0 + jnp.exp(-gate_ref[...]))
    bias_out = bout_ref[...]
    blocks = [rows_ref[b * height : (b + 1) * height, :width] for b in range(count)]
    for layer in range(LAYERS):
        paired, lower, upper = layer_halves(blocks, layer)
        span = slice(layer * pairs, (layer + 1) * pairs)
        paired_s[span, :] = paired
        pre_s[...] = jnp.dot(paired, win_ref[...], preferred_element_type=F32)
        for c in range(pairs // CHUNK):
            here = slice(c * CHUNK, (c + 1) * CHUNK)
            there = slice(layer * pairs + c * CHUNK, layer * pairs + (c + 1) * CHUNK)
            pre = pre_s[here, :] + bin_ref[...]
            centred = pre - jnp.mean(pre, axis=-1, keepdims=True)
            variance = jnp.mean(centred * centred, axis=-1, keepdims=True)
            inv_std = lax.rsqrt(variance + epsilon)
            normed = centred * inv_std
            scaled = normed * gain_ref[...]
            square = scaled * scaled
            bent = jnp.tanh(scaled * (GELU_IN + (GELU_IN * GELU_CUBE) * square))
            half = 0.5 + 0.5 * bent
            hidden_s[there, :] = (scaled * half).astype(BF16)
            slope_s[there, :] = half + (scaled * (0.5 - 0.5 * bent * bent)) * (
                GELU_IN + (3.0 * GELU_IN * GELU_CUBE) * square
            )
            normed_s[there, :] = normed
            inv_s[there, :] = jnp.broadcast_to(inv_std, (CHUNK, LANES))
        mixed = (
            lax.dot_general(
                hidden_s[span, :], wout_ref[...], (((1,), (1,)), ((), ())),
                preferred_element_type=F32,
            )
            + bias_out
        )
        result = (gate * paired.astype(F32) + branch_scale * mixed).astype(BF16)
        blocks = layer_blocks(result, lower, upper, height, width)
    for b in range(count):
        ends_s[0, b * height : (b + 1) * height, :] = blocks[b]

    blocks = [rows_ref[b * height : (b + 1) * height, width:] for b in range(count)]
    sum_pre = jnp.zeros((1, hid), F32)
    sum_gain = jnp.zeros((1, hid), F32)
    sum_mix = jnp.zeros((1, 2 * width), F32)
    sum_gate = jnp.zeros((1, 2 * width), F32)
    for layer in reversed(range(LAYERS)):
        grad_out, lower, upper = layer_halves(blocks, layer)
        span = slice(layer * pairs, (layer + 1) * pairs)
        out_grads = grad_out.astype(F32)
        paired = paired_s[span, :].astype(F32)
        sum_gate += jnp.sum(out_grads * paired, axis=0, keepdims=True)
        mix_grads = branch_scale * out_grads
        sum_mix += jnp.sum(mix_grads, axis=0, keepdims=True)
        mix_cast = mix_grads.astype(BF16)
        mix_s[span, :] = mix_cast
        pre_s[...] = jnp.dot(mix_cast, wout_ref[...], preferred_element_type=F32)
        part_pre = jnp.zeros((CHUNK, hid), F32)
        part_gain = jnp.zeros((CHUNK, hid), F32)
        for c in range(pairs // CHUNK):
            here = slice(c * CHUNK, (c + 1) * CHUNK)
            there = slice(layer * pairs + c * CHUNK, layer * pairs + (c + 1) * CHUNK)
            normed = normed_s[there, :]
            scaled_grads = slope_s[there, :] * pre_s[here, :]
            part_gain += scaled_grads * normed
            normed_grads = scaled_grads * gain_ref[...]
            mean_grad = jnp.mean(normed_grads, axis=-1, keepdims=True)
            mean_both = jnp.mean(normed_grads * normed, axis=-1, keepdims=True)
            pre_grads = inv_s[there, :1] * (normed_grads - mean_grad - normed * mean_both)
            part_pre += pre_grads
            cast_s[there, :] = pre_grads.astype(BF16)
        sum_pre += jnp.sum(part_pre, axis=0, keepdims=True)
        sum_gain += jnp.sum(part_gain, axis=0, keepdims=True)
        back_in = lax.dot_general(
            cast_s[span, :], win_ref[...], (((1,), (1,)), ((), ())), preferred_element_type=F32
        )
        result = (gate * out_grads + back_in).astype(BF16)
        blocks = layer_blocks(result, lower, upper, height, width)
    for b in range(count):
        ends_s[1, b * height : (b + 1) * height, :] = blocks[b]

    share = width // keys

    side = pl.ds(pl.multiple_of(copy * width, width), width)

    @pl.when(core == 0)
    def _():
        left_s[...] = paired_s[:, side]
        right_s[...] = cast_s[...]

    @pl.when(core != 0)
    def _():
        left_s[...] = mix_s[:, side]
        right_s[...] = hidden_s[...]

    for piece in range(width // LANES):
        part = lax.dot_general(
            left_s[:, piece * LANES : (piece + 1) * LANES], right_s[...],
            (((0,), (0,)), ((), ())), preferred_element_type=F32,
        ).astype(BF16)
        for i in range(LANES // share):
            key = piece * (LANES // share) + i
            for k in range(hid // LANES):
                msg_ref[key, k * share : (k + 1) * share, :] = part[
                    i * share : (i + 1) * share, k * LANES : (k + 1) * LANES
                ]

    row = 0
    for total in (sum_pre, sum_gain, sum_mix, sum_gate):
        for k in range(total.shape[1] // LANES):
            small_s[row : row + 1, :] = total[:, k * LANES : (k + 1) * LANES]
            row += 1
    packed = split_small(small_s[...])
    own = height // 2
    for key in range(keys):
        start = share * hid // LANES
        rows = pl.ds(pl.multiple_of((copy * keys + key) * height + core * own, own), own)
        for t in range(2):
            for k in range(width // LANES):
                msg_ref[key, start : start + own, :] = ends_s[
                    t, rows, k * LANES : (k + 1) * LANES
                ]
                start += own
        msg_ref[key, start:, :] = packed


def sum_kernel(
    sizes, scaling, got_ref, gate_ref,
    slice_ref, final_ref, grad_ref, pre_ref, gain_ref, mix_ref, gout_ref,
):
    share, own, width = sizes
    keys = got_ref.shape[0]
    hid = slice_ref.shape[1]
    for k in range(hid // LANES):
        here = slice(k * share, (k + 1) * share)
        total = got_ref[0, here, :].astype(F32)
        for key in range(1, keys):
            total += got_ref[key, here, :].astype(F32)
        slice_ref[:, k * LANES : (k + 1) * LANES] = (total * scaling).astype(slice_ref.dtype)
    start = share * hid // LANES
    for out_ref in (final_ref, grad_ref):
        for k in range(width // LANES):
            for key in range(keys):
                out_ref[key * own : (key + 1) * own, k * LANES : (k + 1) * LANES] = got_ref[
                    key, start : start + own, :
                ]
            start += own
    small = join_small(got_ref[0, start:, :])
    for key in range(1, keys):
        small = small + join_small(got_ref[key, start:, :])
    small = small * scaling
    gate = 1.0 / (1.0 + jnp.exp(-gate_ref[...]))
    first = 0
    for out_ref in (pre_ref, gain_ref, mix_ref, gout_ref):
        count = out_ref.shape[0]
        part = small[first : first + count]
        if out_ref is gout_ref:
            part = part * gate * (1.0 - gate)
        out_ref[...] = part
        first += count


def gather_kernel(place_ref, mine_ref, other_ref, out_ref):
    copy = place_ref[1]
    for key in range(out_ref.shape[0]):
        out_ref[key, copy] = mine_ref[...]
        out_ref[key, 1 - copy] = other_ref[...]


def order_kernel(place_ref, mine_ref, other_ref, first_ref, second_ref, sems):
    copies = mine_ref.shape[1]

    def move(first_src, second_src):
        moves = [
            pltpu.make_async_copy(source.at[:, copy], target.at[copy], sems.at[i, copy])
            for i, (source, target) in enumerate(
                ((first_src, first_ref), (second_src, second_ref))
            )
            for copy in range(copies)
        ]
        for one in moves:
            one.start()
        for one in moves:
            one.wait()

    @pl.when(place_ref[0] == 0)
    def _():
        move(mine_ref, other_ref)

    @pl.when(place_ref[0] != 0)
    def _():
        move(other_ref, mine_ref)


def bit_groups(devices, bits):
    masks = [sum(1 << b for i, b in enumerate(bits) if j >> i & 1) for j in range(2 ** len(bits))]
    every = sum(1 << b for b in bits)
    return [[base | m for m in masks] for base in range(devices) if not base & every]


def exchange(value, devices, bits):
    groups = None if 2 ** len(bits) == devices else bit_groups(devices, bits)
    return lax.all_to_all(value, "seq", 0, 0, axis_index_groups=groups)


def send(value, devices, mask):
    return lax.ppermute(value, "seq", [(i, i ^ mask) for i in range(devices)])


VMEM = pl.BlockSpec(memory_space=pltpu.VMEM)
SMEM = pl.BlockSpec(memory_space=pltpu.SMEM)
HBM = pl.BlockSpec(memory_space=pltpu.HBM)
PARAMS = pltpu.CompilerParams(vmem_limit_bytes=48 * 1024 * 1024)


def per_device(tokens, cotangent, weight_in, bias_in, norm_gain, weight_out, bias_out, gate_logit):
    rows_dev, width = tokens.shape
    hid = weight_in.shape[1]
    devices = lax.axis_size("seq")
    top_bit = devices.bit_length() - 1
    index = lax.axis_index("seq").astype(jnp.int32)
    top_bits = list(range(top_bit - LAYERS, top_bit))
    key_bits, copy_bit = top_bits[:-1], top_bits[-1]
    keys = 2 ** len(key_bits)
    own = rows_dev // keys
    place = jnp.stack([index & 1, index >> copy_bit & 1])

    kept = (weight_in, bias_in[None], norm_gain[None], weight_out, bias_out[None], gate_logit[None])
    kept = pl.pallas_call(
        keep_kernel,
        out_shape=[jax.ShapeDtypeStruct(k.shape, k.dtype) for k in kept],
        in_specs=[VMEM] * len(kept),
        out_specs=[VMEM] * len(kept),
        compiler_params=PARAMS,
        name="keep_weights",
    )(*kept)
    outgoing = pl.pallas_call(
        entry_kernel,
        out_shape=jax.ShapeDtypeStruct((2, keys, 2, own, 2 * width), BF16),
        in_specs=[VMEM] * 2,
        out_specs=VMEM,
        compiler_params=PARAMS,
        name="entry",
    )(tokens, cotangent)
    rows = exchange(outgoing.reshape(4 * keys, own, 2 * width), devices, [0] + top_bits)
    rows = rows.reshape(4 * keys * own, 2 * width)

    pairs = rows.shape[0] // 2
    share = width // keys
    small_rows = (2 * hid + 4 * width) // LANES
    msg_rows = share * hid // LANES + 2 * own * width // LANES + 2 * small_rows
    message = pl.pallas_call(
        switch_kernel,
        out_shape=jax.ShapeDtypeStruct((keys, msg_rows, LANES), BF16),
        in_specs=[SMEM] + [VMEM] * 7,
        out_specs=VMEM,
        scratch_shapes=[
            pltpu.VMEM((pairs, hid), F32),
            pltpu.VMEM((LAYERS * pairs, hid), F32),
            pltpu.VMEM((LAYERS * pairs, hid), F32),
            pltpu.VMEM((LAYERS * pairs, LANES), F32),
            pltpu.VMEM((LAYERS * pairs, hid), BF16),
            pltpu.VMEM((LAYERS * pairs, hid), BF16),
            pltpu.VMEM((LAYERS * pairs, 2 * width), BF16),
            pltpu.VMEM((LAYERS * pairs, 2 * width), BF16),
            pltpu.VMEM((small_rows, LANES), F32),
            pltpu.VMEM((2, 2 * pairs, width), BF16),
            pltpu.VMEM((LAYERS * pairs, width), BF16),
            pltpu.VMEM((LAYERS * pairs, hid), BF16),
        ],
        compiler_params=PARAMS,
        name="switch_layers",
    )(place, rows, *kept)

    got = exchange(message, devices, key_bits)
    scaling = float(rows_dev * devices // 2) ** (-0.5)
    rest = list(range(1, top_bit - LAYERS))
    rows_shape = jax.ShapeDtypeStruct((rows_dev, width), BF16)
    tall, short = hid // LANES, 2 * width // LANES
    owned, final_rows, grad_rows, *small = pl.pallas_call(
        functools.partial(sum_kernel, (share, own, width), scaling),
        out_shape=[jax.ShapeDtypeStruct((share, hid), F32 if rest else BF16)]
        + [rows_shape] * 2
        + [jax.ShapeDtypeStruct((n, LANES), F32) for n in (tall, tall, short, short)],
        in_specs=[VMEM] * 2,
        out_specs=[VMEM] * 7,
        compiler_params=PARAMS,
        name="key_sum",
    )(got, kept[-1].reshape(-1, LANES))
    if rest:
        owned, *small = lax.psum(
            (owned, *small), "seq", axis_index_groups=bit_groups(devices, rest)
        )
        owned = owned.astype(BF16)

    spread = pl.pallas_call(
        gather_kernel,
        out_shape=jax.ShapeDtypeStruct((keys, 2, share, hid), BF16),
        in_specs=[SMEM, VMEM, VMEM],
        out_specs=VMEM,
        compiler_params=PARAMS,
        name="copy_gather",
    )(place, owned, send(owned, devices, 1 << copy_bit))
    whole = exchange(spread, devices, key_bits)
    other = send(whole, devices, 1)
    ordered = jax.ShapeDtypeStruct((2, keys, share, hid), BF16)
    grad_weight_in, grad_weight_out = pl.pallas_call(
        order_kernel,
        out_shape=[ordered] * 2,
        in_specs=[SMEM, VMEM, VMEM],
        out_specs=[HBM] * 2,
        scratch_shapes=[pltpu.SemaphoreType.DMA((2, 2))],
        compiler_params=PARAMS,
        name="weight_order",
    )(place, whole, other)
    return (
        final_rows,
        grad_rows,
        grad_weight_in.reshape(2 * width, hid),
        grad_weight_out.reshape(2 * width, hid),
        *(s.reshape(-1) for s in small),
    )


def solution(mesh):
    placed = (P("seq", None), P("seq", None), P(), P(), P(), P(), P(), P())
    return jax.shard_map(
        per_device,
        mesh=mesh,
        in_specs=placed,
        out_specs=(P("seq", None), P("seq", None), P(), P(), P(), P(), P(), P()),
        check_vma=False,
    )
```

time: 92 us -> 79.7 us (0.87)
  starting transfers between devices: 16.1 us -> 8.86 us
  waiting for transfers between devices: 23.3 us -> 19.4 us
  blocking collectives: 32.7 us -> 29.2 us
  Pallas kernels: 13.1 us -> 15.3 us
  local copies, waits for them, and re-layouts: 4.69 us -> 5.75 us
  other arithmetic: 1.05 us -> 0.07 us
    ppermute x7 -> x2, starting transfers between devices: 8.84 us -> 1.57 us  [send(): return lax.ppermute(value, 'seq', [(i, i ^ mask) for i in range(devices)])]
    ppermute x7 -> x2, waiting for transfers between devices: 12.8 us -> 6.96 us  [send(): return lax.ppermute(value, 'seq', [(i, i ^ mask) for i in range(devices)])]
    all_to_all x2, blocking collectives: 32.7 us -> 29.2 us  [exchange(): return lax.all_to_all(value, 'seq', 0, 0, axis_index_groups=groups)]
    pallas_call x5 -> x6, Pallas kernels: 13.1 us -> 15.3 us  [the longest x1 11.1 us: per_device(): pl.pallas_call(switch_kernel, out_shape=jax.ShapeDtypeStruct((keys, msg_r...]
    all_to_all x1, waiting for transfers between devices: 10.5 us -> 12.4 us  [exchange(): return lax.all_to_all(value, 'seq', 0, 0, axis_index_groups=groups)]
    unnamed x12 -> x20, local copies, waits for them, and re-layouts: 3.96 us -> 5.75 us
    concatenate x1 -> x0, other arithmetic: 0.97 us -> none  [per_device(): jnp.concatenate([tokens.reshape(count, block_rows, width), cotangent.resh...]
  transfers between devices with their start and end apart: 8 -> 3, of which waited for: 6 -> 3; matrix products, arithmetic and copies ran while one was open for 0% -> 0% of each run, Pallas kernels for 0% -> 0%
where the time goes in v2:
time: 79.7 us; the launch traced here: 79.3 us
  blocking collectives  29.2 us (37%)
  waiting for transfers between devices  19.4 us (24%)
  Pallas kernels  15.3 us (19%)
  starting transfers between devices  8.86 us (11%)
  local copies, waits for them, and re-layouts  5.75 us (7%)
    all_to_all x2, blocking collectives, exchange(): return lax.all_to_all(value, 'seq', 0, 0, axis_index_groups=groups)  29.2 us
    all_to_all x1, waiting for transfers between devices, exchange(): return lax.all_to_all(value, 'seq', 0, 0, axis_index_groups=groups)  12.4 us
    pallas_call x1, Pallas kernels, per_device(): pl.pallas_call(switch_kernel, out_shape=jax.ShapeDtypeStruct((keys, msg_r...  11.1 us
    all_to_all x1, starting transfers between devices, exchange(): return lax.all_to_all(value, 'seq', 0, 0, axis_index_groups=groups)  7.3 us
    ppermute x2, waiting for transfers between devices, send(): return lax.ppermute(value, 'seq', [(i, i ^ mask) for i in range(devices)])  6.96 us
    unnamed x20, local copies, waits for them, and re-layouts  5.75 us
    pallas_call x1, Pallas kernels, per_device(): pl.pallas_call(order_kernel, out_shape=[ordered] * 2, in_specs=[SMEM, VME...  1.89 us
  transfers between devices with their start and end apart: 3, of which 3 were waited for; matrix products, arithmetic and copies ran while one was open for 0% of the time, Pallas kernels for 0%

profile of v2, /device:TPU:0, one launch (start us, length us, event | category | flops | bytes accessed | tf_op | source)
XLA Modules:
  0.0 79.3 jit_solution(16768455664231172405)
XLA Ops:
  0.6 0.0 copy-start.4
  0.6 0.8 %copy-done.4 = bf16[128,256]{1,0:T(8,128)(2,1)S(1)} copy-done((bf16[128,256]{1,0:T(8,128)(2,1)S(1)}, bf16[128,256]{1,0:T(8,128)(2,1)}, u32[]{:S(2)}) %copy-start.4) | copy-done | bytes 65560
  1.5 0.0 copy-start.5
  1.5 0.8 %copy-done.5 = bf16[128,256]{1,0:T(8,128)(2,1)S(1)} copy-done((bf16[128,256]{1,0:T(8,128)(2,1)S(1)}, bf16[128,256]{1,0:T(8,128)(2,1)}, u32[]{:S(2)}) %copy-start.5) | copy-done | bytes 65560
  2.3 0.0 copy-start
  2.3 0.8 %entry.1 = bf16[2,8,2,16,512]{4,3,2,1,0:T(8,128)(2,1)} custom-call(bf16[128,256]{1,0:T(8,128)(2,1)S(1)} %copy-done.4, bf16[128,256]{1,0:T(8,128)(2,1)S(1)} %copy-done.5), custom_call_target="tpu_custom_call" | custom-call | tf_op jit(solution)/shard_map/entry/pallas_call | solution.py:314
  3.1 0.0 copy-start.8
  3.1 7.3 %all-to-all-start = ((bf16[32,16,512]{2,1,0:T(8,128)(2,1)}), bf16[32,16,512]{2,1,0:T(8,128)(2,1)S(1)}, u32[]{:S(2)}, u32[]{:S(2)}) async-start(bf16[32,16,512]{2,1,0:T(8,128)(2,1)} %bitcast.2), calls=%async_computation | async-start | bytes 1048576 | tf_op jit(solution)/shard_map/all_to_all | solution.py:280
  10.5 0.0 copy-start.7
  10.5 0.0 copy-start.6
  10.5 0.0 copy-done
  10.5 0.0 copy-done.8
  10.5 0.0 copy-done.9
  10.5 0.6 copy-done.7
  11.1 0.0 copy-done.6
  11.2 1.2 %copy-done.1 = bf16[512,1024]{1,0:T(8,128)(2,1)S(1)} copy-done((bf16[512,1024]{1,0:T(8,128)(2,1)S(1)}, bf16[512,1024]{1,0:T(8,128)(2,1)}, u32[]{:S(2)}) %copy-start.1) | copy-done | bytes 1048600
  12.4 0.1 keep_weights.1
  12.5 0.0 copy-start.2
  12.5 1.0 %copy-done.2 = bf16[512,1024]{1,0:T(8,128)(2,1)} copy-done((bf16[512,1024]{1,0:T(8,128)(2,1)}, bf16[512,1024]{1,0:T(8,128)(2,1)S(1)}, u32[]{:S(2)}) %copy-start.2) | copy-done | bytes 1048600
  13.5 0.1 pad_add_fusion.place_ref
  13.6 12.4 %all-to-all-done = bf16[32,16,512]{2,1,0:T(8,128)(2,1)S(1)} async-done(((bf16[32,16,512]{2,1,0:T(8,128)(2,1)}), bf16[32,16,512]{2,1,0:T(8,128)(2,1)S(1)}, u32[]{:S(2)}, u32[]{:S(2)}) %all-to-all-start) | async-done | bytes 524320 | tf_op jit(solution)/shard_map/all_to_all | solution.py:280
  26.0 1.2 %copy-done.3 = bf16[512,1024]{1,0:T(8,128)(2,1)S(1)} copy-done((bf16[512,1024]{1,0:T(8,128)(2,1)S(1)}, bf16[512,1024]{1,0:T(8,128)(2,1)}, u32[]{:S(2)}) %copy-start.3) | copy-done | bytes 1048600
  27.2 11.1 %switch_layers.1 = bf16[8,368,128]{2,1,0:T(8,128)(2,1)S(1)} custom-call(s32[2]{0:T(128)S(1)} %pad_add_fusion.place_ref, bf16[512,512]{1,0:T(8,128)(2,1)S(1)} %bitcast.15, bf16[512,1024]{1,0:T(8,128)(2,1)S(1)} %get-tuple-element.23.win_ref, f32[1,1024]{1,0:T(1,128)S(1)} %get-tuple-element.24.bin_ref, f32[1,1024]{1,0:T(1,128)S(1)} %get-tuple-element.25.gain_ref, ...), custom_call_target="tpu_custom_call" | custom-call | tf_op jit(solution)/shard_map/switch_layers/pallas_call | solution.py:329
  38.4 14.7 %all_to_all.15.got_ref = bf16[8,368,128]{2,1,0:T(8,128)(2,1)S(1)} all-to-all(bf16[8,368,128]{2,1,0:T(8,128)(2,1)S(1)} %switch_layers.1), channel_id=1, replica_groups={{0,2,4,6,8,10,12,14},{1,3,5,7,9,11,13,15},{16,18,20,22,24,26,28,30},{17..., dimensions={0} | all-to-all | bytes 1507328 | tf_op jit(solution)/shard_map/all_to_all | solution.py:280
  53.1 0.7 key_sum.1
  53.8 1.6 %collective-permute-start = (bf16[32,1024]{1,0:T(8,128)(2,1)S(1)}, bf16[32,1024]{1,0:T(8,128)(2,1)S(1)}, u32[]{:S(2)}, u32[]{:S(2)}) collective-permute-start(bf16[32,1024]{1,0:T(8,128)(2,1)S(1)} %get-tuple-element.31.mine_ref), channel_id=1, source_target_pairs={{0,16},{1,17},{2,18},{3,19},{4,20},{5,21},{6,22},{7,23},{8,24},{9,... | collective-permute-start | bytes 196616 | tf_op jit(solution)/shard_map/ppermute | solution.py:284
  55.3 4.3 %collective-permute-done.other_ref = bf16[32,1024]{1,0:T(8,128)(2,1)S(1)} collective-permute-done((bf16[32,1024]{1,0:T(8,128)(2,1)S(1)}, bf16[32,1024]{1,0:T(8,128)(2,1)S(1)}, u32[]{:S(2)}, u32[]{:S(2)}) %collective-permute-start) | collective-permute-done | bytes 65568 | tf_op jit(solution)/shard_map/ppermute | solution.py:284
  59.6 0.6 copy_gather.1
  60.2 14.5 %all_to_all.16.mine_ref = bf16[8,2,32,1024]{3,2,1,0:T(8,128)(2,1)S(1)} all-to-all(bf16[8,2,32,1024]{3,2,1,0:T(8,128)(2,1)S(1)} %copy_gather.1), channel_id=1, replica_groups={{0,2,4,6,8,10,12,14},{1,3,5,7,9,11,13,15},{16,18,20,22,24,26,28,30},{17..., dimensions={0} | all-to-all | bytes 2097152 | tf_op jit(solution)/shard_map/all_to_all | solution.py:280
  74.7 0.0 collective-permute-start.1
  74.7 2.7 %collective-permute-done.1.other_ref = bf16[8,2,32,1024]{3,2,1,0:T(8,128)(2,1)S(1)} collective-permute-done((bf16[8,2,32,1024]{3,2,1,0:T(8,128)(2,1)S(1)}, bf16[8,2,32,1024]{3,2,1,0:T(8,128)(2,1)S(1)}, u32[]{:S(2)}, u32[]{:S(2)}) %collective-permute-start.1) | collective-permute-done | bytes 1048608 | tf_op jit(solution)/shard_map/ppermute | solution.py:284
  77.4 1.9 %weight_order.1 = (bf16[2,8,32,1024]{3,2,1,0:T(8,128)(2,1)}, bf16[2,8,32,1024]{3,2,1,0:T(8,128)(2,1)}) custom-call(s32[2]{0:T(128)S(1)} %pad_add_fusion.place_ref, bf16[8,2,32,1024]{3,2,1,0:T(8,128)(2,1)S(1)} %all_to_all.16.mine_ref, bf16[8,2,32,1024]{3,2,1,0:T(8,128)(2,1)S(1)} %collective-permute-done.1.other_ref), custom_call_target="tpu_custom_call" | custom-call | tf_op jit(solution)/shard_map/weight_order/pallas_call | solution.py:384
  (3 shorter events, 0.0 us)
Async XLA Ops:
  0.6 0.8 %copy-start.4 = (bf16[128,256]{1,0:T(8,128)(2,1)S(1)}, bf16[128,256]{1,0:T(8,128)(2,1)}, u32[]{:S(2)}) copy-start(bf16[128,256]{1,0:T(8,128)(2,1)} %tokens_ref.1) | copy-start | bytes 196612
  1.5 0.8 %copy-start.5 = (bf16[128,256]{1,0:T(8,128)(2,1)S(1)}, bf16[128,256]{1,0:T(8,128)(2,1)}, u32[]{:S(2)}) copy-start(bf16[128,256]{1,0:T(8,128)(2,1)} %cotangent_ref.1) | copy-start | bytes 196612
  2.3 8.2 %copy-start = (bf16[512,1024]{1,0:T(8,128)(2,1)S(1)}, bf16[512,1024]{1,0:T(8,128)(2,1)}, u32[]{:S(2)}) copy-start(bf16[512,1024]{1,0:T(8,128)(2,1)} %refs_0_.1) | copy-start | bytes 3145732
  3.1 7.4 %copy-start.8 = (f32[512]{0:T(512)S(1)}, f32[512]{0:T(512)}, u32[]{:S(2)}) copy-start(f32[512]{0:T(512)} %param.14) | copy-start | bytes 6148
  3.1 7.4 %copy-start.9 = (f32[512]{0:T(512)S(1)}, f32[512]{0:T(512)}, u32[]{:S(2)}) copy-start(f32[512]{0:T(512)} %param.15) | copy-start | bytes 6148
  3.1 22.9 %all-to-all-start = ((bf16[32,16,512]{2,1,0:T(8,128)(2,1)}), bf16[32,16,512]{2,1,0:T(8,128)(2,1)S(1)}, u32[]{:S(2)}, u32[]{:S(2)}) async-start(bf16[32,16,512]{2,1,0:T(8,128)(2,1)} %bitcast.2), calls=%async_computation | async-start | bytes 1048576 | tf_op jit(solution)/shard_map/all_to_all | solution.py:280
  10.5 0.7 copy-start.7
  10.5 0.7 copy-start.6
  11.2 1.2 %copy-start.1 = (bf16[512,1024]{1,0:T(8,128)(2,1)S(1)}, bf16[512,1024]{1,0:T(8,128)(2,1)}, u32[]{:S(2)}) copy-start(bf16[512,1024]{1,0:T(8,128)(2,1)} %refs_3_.1) | copy-start | bytes 3145732
  12.5 1.0 %copy-start.2 = (bf16[512,1024]{1,0:T(8,128)(2,1)}, bf16[512,1024]{1,0:T(8,128)(2,1)S(1)}, u32[]{:S(2)}) copy-start(bf16[512,1024]{1,0:T(8,128)(2,1)S(1)} %get-tuple-element.26.wout_ref) | copy-start | bytes 3145732
  26.0 1.2 %copy-start.3 = (bf16[512,1024]{1,0:T(8,128)(2,1)S(1)}, bf16[512,1024]{1,0:T(8,128)(2,1)}, u32[]{:S(2)}) copy-start(bf16[512,1024]{1,0:T(8,128)(2,1)} %copy-done.2) | copy-start | bytes 3145732
  53.8 5.9 %collective-permute-start = (bf16[32,1024]{1,0:T(8,128)(2,1)S(1)}, bf16[32,1024]{1,0:T(8,128)(2,1)S(1)}, u32[]{:S(2)}, u32[]{:S(2)}) collective-permute-start(bf16[32,1024]{1,0:T(8,128)(2,1)S(1)} %get-tuple-element.31.mine_ref), channel_id=1, source_target_pairs={{0,16},{1,17},{2,18},{3,19},{4,20},{5,21},{6,22},{7,23},{8,24},{9,... | collective-permute-start | bytes 196616 | tf_op jit(solution)/shard_map/ppermute | solution.py:284
  74.7 2.7 %collective-permute-start.1 = (bf16[8,2,32,1024]{3,2,1,0:T(8,128)(2,1)S(1)}, bf16[8,2,32,1024]{3,2,1,0:T(8,128)(2,1)S(1)}, u32[]{:S(2)}, u32[]{:S(2)}) collective-permute-start(bf16[8,2,32,1024]{3,2,1,0:T(8,128)(2,1)S(1)} %all_to_all.16.mine_ref), channel_id=1, source_target_pairs={{0,1},{1,0},{2,3},{3,2},{4,5},{5,4},{6,7},{7,6},{8,9},{9,8},{10,11... | collective-permute-start | bytes 3145736 | tf_op jit(solution)/shard_map/ppermute | solution.py:284

commit v3 on v2

v3 whole, which is shorter than its diff:
```python
import functools

import jax
import jax.numpy as jnp
from jax import lax
from jax.experimental import pallas as pl
from jax.experimental.pallas import tpu as pltpu
from jax.sharding import PartitionSpec as P

LAYERS = 4
LANES = 128
CHUNK = 16
TILE = 256

epsilon = 1e-05
branch_scale = 0.25
GELU_IN = 0.7978845608028654
GELU_CUBE = 0.044715

BF16 = jnp.bfloat16
F32 = jnp.float32


def split_small(total):
    high = total.astype(BF16).astype(F32)
    return jnp.concatenate([high, total - high], axis=0).astype(BF16)


def join_small(packed):
    wide = packed.astype(F32)
    rows = wide.shape[0] // 2
    return wide[:rows] + wide[rows:]


def layer_halves(blocks, layer):
    lower = [b for b in range(len(blocks)) if not b >> layer & 1]
    upper = [b for b in range(len(blocks)) if b >> layer & 1]
    left = jnp.concatenate([blocks[b] for b in lower], axis=0)
    right = jnp.concatenate([blocks[b] for b in upper], axis=0)
    return jnp.concatenate([left, right], axis=1), lower, upper


def layer_blocks(joined, lower, upper, height, width):
    blocks = [None] * (2 * len(lower))
    for i, b in enumerate(lower):
        blocks[b] = joined[i * height : (i + 1) * height, :width]
    for i, b in enumerate(upper):
        blocks[b] = joined[i * height : (i + 1) * height, width:]
    return blocks


def keep_kernel(*refs):
    half = len(refs) // 2
    for source, target in zip(refs[:half], refs[half:]):
        target[...] = source[...]


def fold_lanes(tile):
    return sum(tile[:, k : k + LANES] for k in range(0, tile.shape[1], LANES))


def widen(stat):
    return jnp.concatenate([stat] * (TILE // LANES), axis=1)


def row_total(folded):
    return jnp.sum(folded, axis=-1, keepdims=True)


def switch_kernel(
    place_ref, rows_ref, win_ref, bin_ref, gain_ref, wout_ref, bout_ref, gate_ref, msg_ref,
    pre_s, normed_s, slope_s, inv_s, stat_s, both_s, side_s, small_s, ends_s,
):
    core = place_ref[0]
    copy = place_ref[1]
    twins, count, own, double = rows_ref.shape
    width = double // 2
    height = twins * own
    pairs = count * height // 2
    hid = win_ref.shape[1]
    keys = msg_ref.shape[0]
    columns = [slice(c, c + TILE) for c in range(0, hid, TILE)]
    chunks = [slice(r, r + CHUNK) for r in range(0, pairs, CHUNK)]
    gate = 1.0 / (1.0 + jnp.exp(-gate_ref[...]))
    bias_out = bout_ref[...]

    def below(layer, here):
        return slice(layer * pairs + here.start, layer * pairs + here.stop)

    blocks = [
        jnp.concatenate([rows_ref[twin, b, :, :width] for twin in range(twins)], axis=0)
        for b in range(count)
    ]
    for layer in range(LAYERS):
        paired, lower, upper = layer_halves(blocks, layer)
        span = slice(layer * pairs, (layer + 1) * pairs)
        for side in range(2):
            side_s[0, side, span, :] = paired[:, side * width : (side + 1) * width]

        def project(column):
            pre_s[:, column] = jnp.dot(
                paired, win_ref[:, column], preferred_element_type=F32
            ) + bin_ref[:, column]

        def gather_stats(column):
            for here in chunks:
                pre = pre_s[here, column]
                if column.start == 0:
                    shift = row_total(fold_lanes(pre)) * (1.0 / TILE)
                    stat_s[0, here, :] = jnp.broadcast_to(shift, (CHUNK, LANES))
                    moved = pre - shift
                    stat_s[1, here, :] = fold_lanes(moved)
                    stat_s[2, here, :] = fold_lanes(moved * moved)
                else:
                    moved = pre - widen(stat_s[0, here, :])
                    stat_s[1, here, :] += fold_lanes(moved)
                    stat_s[2, here, :] += fold_lanes(moved * moved)

        project(columns[0])
        for now, column in zip(columns[1:], columns):
            project(now)
            gather_stats(column)
        gather_stats(columns[-1])
        for here in chunks:
            drift = row_total(stat_s[1, here, :]) * (1.0 / hid)
            square = row_total(stat_s[2, here, :]) * (1.0 / hid)
            inv_std = lax.rsqrt(square - drift * drift + epsilon)
            stat_s[0, here, :] = stat_s[0, here, :] + drift
            inv_s[below(layer, here), :] = jnp.broadcast_to(inv_std, (CHUNK, LANES))
        def activate(column):
            for here in chunks:
                there = below(layer, here)
                normed = (pre_s[here, column] - widen(stat_s[0, here, :])) * widen(
                    inv_s[there, :]
                )
                scaled = normed * gain_ref[:, column]
                square = scaled * scaled
                bent = jnp.tanh(scaled * (GELU_IN + (GELU_IN * GELU_CUBE) * square))
                half = 0.5 + 0.5 * bent
                both_s[1, there, column] = (scaled * half).astype(BF16)
                slope_s[there, column] = half + (scaled * (0.5 - 0.5 * bent * bent)) * (
                    GELU_IN + (3.0 * GELU_IN * GELU_CUBE) * square
                )
                normed_s[there, column] = normed

        activate(columns[0])
        mixed = None
        for i, column in enumerate(columns):
            if i + 1 < len(columns):
                activate(columns[i + 1])
            part = lax.dot_general(
                both_s[1, span, column], wout_ref[:, column], (((1,), (1,)), ((), ())),
                preferred_element_type=F32,
            )
            mixed = part if mixed is None else mixed + part
        result = (
            gate * paired.astype(F32) + branch_scale * (mixed + bias_out)
        ).astype(BF16)
        blocks = layer_blocks(result, lower, upper, height, width)
    for b in range(count):
        ends_s[0, b * height : (b + 1) * height, :] = blocks[b]

    blocks = [
        jnp.concatenate([rows_ref[twin, b, :, width:] for twin in range(twins)], axis=0)
        for b in range(count)
    ]
    sum_pre = [jnp.zeros((1, TILE), F32) for _ in columns]
    sum_gain = [jnp.zeros((1, TILE), F32) for _ in columns]
    sum_mix = jnp.zeros((1, 2 * width), F32)
    sum_gate = jnp.zeros((1, 2 * width), F32)
    for layer in reversed(range(LAYERS)):
        grad_out, lower, upper = layer_halves(blocks, layer)
        span = slice(layer * pairs, (layer + 1) * pairs)
        out_grads = grad_out.astype(F32)
        paired = jnp.concatenate([side_s[0, side, span, :] for side in range(2)], axis=1)
        sum_gate += jnp.sum(out_grads * paired.astype(F32), axis=0, keepdims=True)
        mix_grads = branch_scale * out_grads
        sum_mix += jnp.sum(mix_grads, axis=0, keepdims=True)
        mix_cast = mix_grads.astype(BF16)
        for side in range(2):
            side_s[1, side, span, :] = mix_cast[:, side * width : (side + 1) * width]

        def project(column):
            pre_s[:, column] = jnp.dot(
                mix_cast, wout_ref[:, column], preferred_element_type=F32
            )

        def gather_stats(i, column):
            gains = jnp.zeros((CHUNK, TILE), F32)
            for here in chunks:
                there = below(layer, here)
                normed = normed_s[there, column]
                scaled_grads = slope_s[there, column] * pre_s[here, column]
                gains += scaled_grads * normed
                normed_grads = scaled_grads * gain_ref[:, column]
                pre_s[here, column] = normed_grads
                first = fold_lanes(normed_grads)
                second = fold_lanes(normed_grads * normed)
                if i == 0:
                    stat_s[1, here, :] = first
                    stat_s[2, here, :] = second
                else:
                    stat_s[1, here, :] += first
                    stat_s[2, here, :] += second
            sum_gain[i] += jnp.sum(gains, axis=0, keepdims=True)

        project(columns[0])
        for i, now in enumerate(columns[1:]):
            project(now)
            gather_stats(i, columns[i])
        gather_stats(len(columns) - 1, columns[-1])
        for here in chunks:
            for k in (1, 2):
                mean = row_total(stat_s[k, here, :]) * (1.0 / hid)
                stat_s[k, here, :] = jnp.broadcast_to(mean, (CHUNK, LANES))
        def finish(i, column):
            total = jnp.zeros((CHUNK, TILE), F32)
            for here in chunks:
                there = below(layer, here)
                pre_grads = widen(inv_s[there, :]) * (
                    pre_s[here, column]
                    - widen(stat_s[1, here, :])
                    - normed_s[there, column] * widen(stat_s[2, here, :])
                )
                total += pre_grads
                both_s[0, there, column] = pre_grads.astype(BF16)
            sum_pre[i] += jnp.sum(total, axis=0, keepdims=True)

        finish(0, columns[0])
        back_in = None
        for i, column in enumerate(columns):
            if i + 1 < len(columns):
                finish(i + 1, columns[i + 1])
            part = lax.dot_general(
                both_s[0, span, column], win_ref[:, column], (((1,), (1,)), ((), ())),
                preferred_element_type=F32,
            )
            back_in = part if back_in is None else back_in + part
        result = (gate * out_grads + back_in).astype(BF16)
        blocks = layer_blocks(result, lower, upper, height, width)
    for b in range(count):
        ends_s[1, b * height : (b + 1) * height, :] = blocks[b]

    share = width // keys
    for piece in range(width // LANES):
        part = lax.dot_general(
            side_s[core, copy, :, piece * LANES : (piece + 1) * LANES], both_s[core],
            (((0,), (0,)), ((), ())), preferred_element_type=F32,
        ).astype(BF16)
        for i in range(LANES // share):
            key = piece * (LANES // share) + i
            for k in range(hid // LANES):
                msg_ref[key, k * share : (k + 1) * share, :] = part[
                    i * share : (i + 1) * share, k * LANES : (k + 1) * LANES
                ]

    row = 0
    for total in (*sum_pre, *sum_gain, sum_mix, sum_gate):
        for k in range(total.shape[1] // LANES):
            small_s[row : row + 1, :] = total[:, k * LANES : (k + 1) * LANES]
            row += 1
    packed = split_small(small_s[...])
    for key in range(keys):
        start = share * hid // LANES
        rows = pl.ds(pl.multiple_of((copy * keys + key) * height + core * own, own), own)
        for t in range(2):
            for k in range(width // LANES):
                msg_ref[key, start : start + own, :] = ends_s[
                    t, rows, k * LANES : (k + 1) * LANES
                ]
                start += own
        msg_ref[key, start:, :] = packed


def sum_kernel(
    sizes, scaling, got_ref, gate_ref,
    slice_ref, final_ref, grad_ref, pre_ref, gain_ref, mix_ref, gout_ref,
):
    share, own, width = sizes
    keys = got_ref.shape[0]
    hid = slice_ref.shape[1]
    for k in range(hid // LANES):
        here = slice(k * share, (k + 1) * share)
        total = got_ref[0, here, :].astype(F32)
        for key in range(1, keys):
            total += got_ref[key, here, :].astype(F32)
        slice_ref[:, k * LANES : (k + 1) * LANES] = (total * scaling).astype(slice_ref.dtype)
    start = share * hid // LANES
    for out_ref in (final_ref, grad_ref):
        for k in range(width // LANES):
            for key in range(keys):
                out_ref[key * own : (key + 1) * own, k * LANES : (k + 1) * LANES] = got_ref[
                    key, start : start + own, :
                ]
            start += own
    small = join_small(got_ref[0, start:, :])
    for key in range(1, keys):
        small = small + join_small(got_ref[key, start:, :])
    small = small * scaling
    gate = 1.0 / (1.0 + jnp.exp(-gate_ref[...]))
    first = 0
    for out_ref in (pre_ref, gain_ref, mix_ref, gout_ref):
        count = out_ref.shape[0]
        part = small[first : first + count]
        if out_ref is gout_ref:
            part = part * gate * (1.0 - gate)
        out_ref[...] = part
        first += count


def gather_kernel(place_ref, mine_ref, other_ref, out_ref):
    copy = place_ref[1]
    for key in range(out_ref.shape[0]):
        out_ref[key, copy] = mine_ref[...]
        out_ref[key, 1 - copy] = other_ref[...]


def move_weight(source_ref, target_ref, sems):
    keys, copies = source_ref.shape[:2]
    moves = [
        pltpu.make_async_copy(
            source_ref.at[key, copy], target_ref.at[copy, key], sems.at[copies * key + copy]
        )
        for key in range(keys)
        for copy in range(copies)
    ]
    for move in moves:
        move.start()
    for move in moves:
        move.wait()


def mine_kernel(place_ref, mine_ref, first_ref, second_ref, sems):
    for core, out_ref in enumerate((first_ref, second_ref)):

        @pl.when(place_ref[0] == core)
        def _():
            move_weight(mine_ref, out_ref, sems)


def other_kernel(place_ref, other_ref, first_in, second_in, first_ref, second_ref, sems):
    for core, out_ref in enumerate((second_ref, first_ref)):

        @pl.when(place_ref[0] == core)
        def _():
            move_weight(other_ref, out_ref, sems)


def bit_groups(devices, bits):
    masks = [sum(1 << b for i, b in enumerate(bits) if j >> i & 1) for j in range(2 ** len(bits))]
    every = sum(1 << b for b in bits)
    return [[base | m for m in masks] for base in range(devices) if not base & every]


def exchange(value, devices, bits):
    groups = None if 2 ** len(bits) == devices else bit_groups(devices, bits)
    return lax.all_to_all(value, "seq", 0, 0, axis_index_groups=groups)


def send(value, devices, mask):
    return lax.ppermute(value, "seq", [(i, i ^ mask) for i in range(devices)])


VMEM = pl.BlockSpec(memory_space=pltpu.VMEM)
SMEM = pl.BlockSpec(memory_space=pltpu.SMEM)
HBM = pl.BlockSpec(memory_space=pltpu.HBM)
PARAMS = pltpu.CompilerParams(vmem_limit_bytes=4 * 1024 * 1024)
WIDE = pltpu.CompilerParams(vmem_limit_bytes=32 * 1024 * 1024)


def compute(place, rows, kept):
    hid = kept[0].shape[1]
    twins, count, own, double = rows.shape
    width = double // 2
    keys = count // 2
    pairs = twins * count * own // 2
    share = width // keys
    small_rows = (2 * hid + 4 * width) // LANES
    msg_rows = share * hid // LANES + 2 * own * width // LANES + 2 * small_rows
    return pl.pallas_call(
        switch_kernel,
        out_shape=jax.ShapeDtypeStruct((keys, msg_rows, LANES), BF16),
        in_specs=[SMEM] + [VMEM] * 7,
        out_specs=VMEM,
        scratch_shapes=[
            pltpu.VMEM((pairs, hid), F32),
            pltpu.VMEM((LAYERS * pairs, hid), F32),
            pltpu.VMEM((LAYERS * pairs, hid), F32),
            pltpu.VMEM((LAYERS * pairs, LANES), F32),
            pltpu.VMEM((3, pairs, LANES), F32),
            pltpu.VMEM((2, LAYERS * pairs, hid), BF16),
            pltpu.VMEM((2, 2, LAYERS * pairs, width), BF16),
            pltpu.VMEM((small_rows, LANES), F32),
            pltpu.VMEM((2, 2 * pairs, width), BF16),
        ],
        compiler_params=WIDE,
        name="switch_layers",
    )(place, rows, *kept)


def per_device(tokens, cotangent, weight_in, bias_in, norm_gain, weight_out, bias_out, gate_logit):
    rows_dev, width = tokens.shape
    hid = weight_in.shape[1]
    devices = lax.axis_size("seq")
    top_bit = devices.bit_length() - 1
    index = lax.axis_index("seq").astype(jnp.int32)
    top_bits = list(range(top_bit - LAYERS, top_bit))
    key_bits, copy_bit = top_bits[:-1], top_bits[-1]
    keys = 2 ** len(key_bits)
    own = rows_dev // keys
    place = jnp.stack([index & 1, index >> copy_bit & 1])

    kept = (weight_in, bias_in[None], norm_gain[None], weight_out, bias_out[None], gate_logit[None])
    kept = pl.pallas_call(
        keep_kernel,
        out_shape=[jax.ShapeDtypeStruct(k.shape, k.dtype) for k in kept],
        in_specs=[VMEM] * len(kept),
        out_specs=[VMEM] * len(kept),
        compiler_params=PARAMS,
        name="keep_weights",
    )(*kept)
    both = jnp.concatenate([tokens, cotangent], axis=-1).reshape(keys, own, 2 * width)
    rows = exchange(jnp.concatenate([both, both], axis=0), devices, top_bits)
    rows = lax.all_gather(rows, "seq", axis=0, axis_index_groups=bit_groups(devices, [0]))

    message = compute(place, rows, kept)
    share = width // keys
    got = exchange(message, devices, key_bits)
    scaling = float(rows_dev * devices // 2) ** (-0.5)
    rest = list(range(1, top_bit - LAYERS))
    rows_shape = jax.ShapeDtypeStruct((rows_dev, width), BF16)
    tall, short = hid // LANES, 2 * width // LANES
    owned, final_rows, grad_rows, *small = pl.pallas_call(
        functools.partial(sum_kernel, (share, own, width), scaling),
        out_shape=[jax.ShapeDtypeStruct((share, hid), F32 if rest else BF16)]
        + [rows_shape] * 2
        + [jax.ShapeDtypeStruct((n, LANES), F32) for n in (tall, tall, short, short)],
        in_specs=[VMEM] * 2,
        out_specs=[VMEM] * 7,
        compiler_params=PARAMS,
        name="key_sum",
    )(got, kept[5].reshape(-1, LANES))
    if rest:
        owned, *small = lax.psum(
            (owned, *small), "seq", axis_index_groups=bit_groups(devices, rest)
        )
        owned = owned.astype(BF16)

    spread = pl.pallas_call(
        gather_kernel,
        out_shape=jax.ShapeDtypeStruct((keys, 2, share, hid), BF16),
        in_specs=[SMEM, VMEM, VMEM],
        out_specs=VMEM,
        compiler_params=PARAMS,
        name="copy_gather",
    )(place, owned, send(owned, devices, 1 << copy_bit))
    whole = exchange(spread, devices, key_bits)
    other = send(whole, devices, 1)
    ordered = jax.ShapeDtypeStruct((2, keys, share, hid), BF16)
    weights = pl.pallas_call(
        mine_kernel,
        out_shape=[ordered] * 2,
        in_specs=[SMEM, VMEM],
        out_specs=[HBM] * 2,
        scratch_shapes=[pltpu.SemaphoreType.DMA((2 * keys,))],
        compiler_params=PARAMS,
        name="mine_out",
    )(place, whole)
    grad_weight_in, grad_weight_out = pl.pallas_call(
        other_kernel,
        out_shape=[ordered] * 2,
        in_specs=[SMEM, VMEM, HBM, HBM],
        out_specs=[HBM] * 2,
        scratch_shapes=[pltpu.SemaphoreType.DMA((2 * keys,))],
        input_output_aliases={2: 0, 3: 1},
        compiler_params=PARAMS,
        name="other_out",
    )(place, other, *weights)
    return (
        final_rows,
        grad_rows,
        grad_weight_in.reshape(2 * width, hid),
        grad_weight_out.reshape(2 * width, hid),
        *(s.reshape(-1) for s in small),
    )


def solution(mesh):
    placed = (P("seq", None), P("seq", None), P(), P(), P(), P(), P(), P())
    return jax.shard_map(
        per_device,
        mesh=mesh,
        in_specs=placed,
        out_specs=(P("seq", None), P("seq", None), P(), P(), P(), P(), P(), P()),
        check_vma=False,
    )
```

time: 79.7 us -> 75.4 us (0.946)
  waiting for transfers between devices: 19.4 us -> 13.5 us
  local copies, waits for them, and re-layouts: 5.75 us -> 1.92 us
  blocking collectives: 29.2 us -> 32.4 us
  other arithmetic: 0.07 us -> 1.77 us
    all_to_all x1, waiting for transfers between devices: 12.4 us -> 7.69 us  [exchange(): return lax.all_to_all(value, 'seq', 0, 0, axis_index_groups=groups)]
    unnamed x20 -> x12, local copies, waits for them, and re-layouts: 5.75 us -> 1.92 us
    all_gather x0 -> x1, blocking collectives: none -> 2.17 us  [per_device(): lax.all_gather(rows, 'seq', axis=0, axis_index_groups=bit_groups(devices,...]
    concatenate x0 -> x2, other arithmetic: none -> 1.69 us  [the longest x1 0.97 us: per_device(): jnp.concatenate([tokens, cotangent], axis=-1).reshape(keys, own, 2 * width)]
    ppermute x2, waiting for transfers between devices: 6.96 us -> 5.78 us  [send(): return lax.ppermute(value, 'seq', [(i, i ^ mask) for i in range(devices)])]
    all_to_all x2, blocking collectives: 29.2 us -> 30.3 us  [exchange(): return lax.all_to_all(value, 'seq', 0, 0, axis_index_groups=groups)]
    all_to_all x1, starting transfers between devices: 7.3 us -> 8.31 us  [exchange(): return lax.all_to_all(value, 'seq', 0, 0, axis_index_groups=groups)]
  transfers between devices with their start and end apart: 3 -> 3, of which waited for: 3 -> 3; matrix products, arithmetic and copies ran while one was open for 0% -> 0% of each run, Pallas kernels for 0% -> 2%
where the time goes in v3:
time: 75.4 us; the launch traced here: 75 us
  blocking collectives  32.4 us (43%)
  Pallas kernels  15.3 us (20%)
  waiting for transfers between devices  13.5 us (18%)
  starting transfers between devices  9.42 us (12%)
  local copies, waits for them, and re-layouts  1.92 us (3%)
  other arithmetic  1.77 us (2%)
    all_to_all x2, blocking collectives, exchange(): return lax.all_to_all(value, 'seq', 0, 0, axis_index_groups=groups)  30.3 us
    pallas_call x1, Pallas kernels, compute(): pl.pallas_call(switch_kernel, out_shape=jax.ShapeDtypeStruct((keys, msg_r...  10.6 us
    all_to_all x1, starting transfers between devices, exchange(): return lax.all_to_all(value, 'seq', 0, 0, axis_index_groups=groups)  8.31 us
    all_to_all x1, waiting for transfers between devices, exchange(): return lax.all_to_all(value, 'seq', 0, 0, axis_index_groups=groups)  7.69 us
    ppermute x2, waiting for transfers between devices, send(): return lax.ppermute(value, 'seq', [(i, i ^ mask) for i in range(devices)])  5.78 us
    all_gather x1, blocking collectives, per_device(): lax.all_gather(rows, 'seq', axis=0, axis_index_groups=bit_groups(devices,...  2.17 us
    unnamed x12, local copies, waits for them, and re-layouts  1.92 us
    pallas_call x1, Pallas kernels, per_device(): pl.pallas_call(mine_kernel, out_shape=[ordered] * 2, in_specs=[SMEM, VMEM...  1.63 us
  transfers between devices with their start and end apart: 3, of which 3 were waited for; matrix products, arithmetic and copies ran while one was open for 0% of the time, Pallas kernels for 2%

profile of v3, /device:TPU:0, one launch (start us, length us, event | category | flops | bytes accessed | tf_op | source)
XLA Modules:
  0.0 75.0 jit_solution(6371731839883773354)
XLA Ops:
  0.6 0.0 copy-start
  0.6 1.0 %pad_maximum_fusion.1 = bf16[128,512]{1,0:T(8,128)(2,1)S(1)} fusion(bf16[128,256]{1,0:T(8,128)(2,1)} %param.9, bf16[128,256]{1,0:T(8,128)(2,1)} %param.8), kind=kLoop, calls=%fused_computation.1 | loop fusion | flops 262144 | bytes 262144 | tf_op jit(solution)/shard_map/concatenate | solution.py:422
  1.6 0.7 pad_maximum_fusion
  2.3 8.3 %all-to-all-start = ((bf16[16,16,512]{2,1,0:T(8,128)(2,1)}), bf16[16,16,512]{2,1,0:T(8,128)(2,1)S(1)}, u32[]{:S(2)}, u32[]{:S(2)}) async-start(bf16[16,16,512]{2,1,0:T(8,128)(2,1)} %pad_maximum_fusion), calls=%async_computation | async-start | bytes 524288 | tf_op jit(solution)/shard_map/all_to_all | solution.py:357
  10.7 0.0 copy-start.4
  10.7 0.0 copy-start.5
  10.7 0.0 copy-start.3
  10.7 0.0 copy-start.2
  10.7 0.0 copy-done
  10.7 0.6 copy-done.4
  11.3 0.0 copy-done.5
  11.4 0.0 copy-done.3
  11.4 0.0 copy-done.2
  11.4 0.0 copy-start.1
  11.4 1.2 %copy-done.1 = bf16[512,1024]{1,0:T(8,128)(2,1)S(1)} copy-done((bf16[512,1024]{1,0:T(8,128)(2,1)S(1)}, bf16[512,1024]{1,0:T(8,128)(2,1)}, u32[]{:S(2)}) %copy-start.1) | copy-done | bytes 1048600
  12.6 0.1 keep_weights.1
  12.8 0.1 pad_add_fusion.place_ref
  12.8 7.7 %all-to-all-done = bf16[16,16,512]{2,1,0:T(8,128)(2,1)S(1)} async-done(((bf16[16,16,512]{2,1,0:T(8,128)(2,1)}), bf16[16,16,512]{2,1,0:T(8,128)(2,1)S(1)}, u32[]{:S(2)}, u32[]{:S(2)}) %all-to-all-start) | async-done | bytes 262176 | tf_op jit(solution)/shard_map/all_to_all | solution.py:357
  20.5 2.2 %all-gather = bf16[32,16,512]{2,1,0:T(8,128)(2,1)S(1)} all-gather(bf16[16,16,512]{2,1,0:T(8,128)(2,1)S(1)} %all-to-all-done), channel_id=2, replica_groups={{0,1},{2,3},{4,5},{6,7},{8,9},{10,11},{12,13},{14,15},{16,17},{18,19},{..., dimensions={0}, use_global_device_ids=true | all-gather | bytes 786432 | tf_op jit(solution)/shard_map/all_gather | solution.py:424
  22.7 10.6 %switch_layers.1 = bf16[8,368,128]{2,1,0:T(8,128)(2,1)S(1)} custom-call(s32[2]{0:T(128)S(1)} %pad_add_fusion.place_ref, bf16[2,16,16,512]{3,2,1,0:T(8,128)(2,1)S(1)} %bitcast.15, bf16[512,1024]{1,0:T(8,128)(2,1)S(1)} %get-tuple-element.25.win_ref, f32[1,1024]{1,0:T(1,128)S(1)} %get-tuple-element.26.bin_ref, f32[1,1024]{1,0:T(1,128)S(1)} %get-tuple-element.27.gain_ref, ...), custom_call_target="tpu_custom_call" | custom-call | tf_op jit(solution)/shard_map/switch_layers/pallas_call | solution.py:380
  33.3 14.9 %all_to_all.15.got_ref = bf16[8,368,128]{2,1,0:T(8,128)(2,1)S(1)} all-to-all(bf16[8,368,128]{2,1,0:T(8,128)(2,1)S(1)} %switch_layers.1), channel_id=1, replica_groups={{0,2,4,6,8,10,12,14},{1,3,5,7,9,11,13,15},{16,18,20,22,24,26,28,30},{17..., dimensions={0} | all-to-all | bytes 1507328 | tf_op jit(solution)/shard_map/all_to_all | solution.py:357
  48.2 0.7 key_sum.1
  48.9 1.1 %collective-permute-start = (bf16[32,1024]{1,0:T(8,128)(2,1)S(1)}, bf16[32,1024]{1,0:T(8,128)(2,1)S(1)}, u32[]{:S(2)}, u32[]{:S(2)}) collective-permute-start(bf16[32,1024]{1,0:T(8,128)(2,1)S(1)} %get-tuple-element.33.mine_ref), channel_id=1, source_target_pairs={{0,16},{1,17},{2,18},{3,19},{4,20},{5,21},{6,22},{7,23},{8,24},{9,... | collective-permute-start | bytes 196616 | tf_op jit(solution)/shard_map/ppermute | solution.py:361
  50.0 4.8 %collective-permute-done.other_ref = bf16[32,1024]{1,0:T(8,128)(2,1)S(1)} collective-permute-done((bf16[32,1024]{1,0:T(8,128)(2,1)S(1)}, bf16[32,1024]{1,0:T(8,128)(2,1)S(1)}, u32[]{:S(2)}, u32[]{:S(2)}) %collective-permute-start) | collective-permute-done | bytes 65568 | tf_op jit(solution)/shard_map/ppermute | solution.py:361
  54.8 0.6 copy_gather.1
  55.4 15.3 %all_to_all.16.mine_ref = bf16[8,2,32,1024]{3,2,1,0:T(8,128)(2,1)S(1)} all-to-all(bf16[8,2,32,1024]{3,2,1,0:T(8,128)(2,1)S(1)} %copy_gather.1), channel_id=1, replica_groups={{0,2,4,6,8,10,12,14},{1,3,5,7,9,11,13,15},{16,18,20,22,24,26,28,30},{17..., dimensions={0} | all-to-all | bytes 2097152 | tf_op jit(solution)/shard_map/all_to_all | solution.py:357
  70.7 0.0 collective-permute-start.1
  70.7 1.6 %mine_out.1 = (bf16[2,8,32,1024]{3,2,1,0:T(8,128)(2,1)}, bf16[2,8,32,1024]{3,2,1,0:T(8,128)(2,1)}) custom-call(s32[2]{0:T(128)S(1)} %pad_add_fusion.place_ref, bf16[8,2,32,1024]{3,2,1,0:T(8,128)(2,1)S(1)} %all_to_all.16.mine_ref), custom_call_target="tpu_custom_call" | custom-call | tf_op jit(solution)/shard_map/mine_out/pallas_call | solution.py:460
  72.4 1.0 %collective-permute-done.1.other_ref = bf16[8,2,32,1024]{3,2,1,0:T(8,128)(2,1)S(1)} collective-permute-done((bf16[8,2,32,1024]{3,2,1,0:T(8,128)(2,1)S(1)}, bf16[8,2,32,1024]{3,2,1,0:T(8,128)(2,1)S(1)}, u32[]{:S(2)}, u32[]{:S(2)}) %collective-permute-start.1) | collective-permute-done | bytes 1048608 | tf_op jit(solution)/shard_map/ppermute | solution.py:361
  73.4 1.6 %other_out.1 = (bf16[2,8,32,1024]{3,2,1,0:T(8,128)(2,1)}, bf16[2,8,32,1024]{3,2,1,0:T(8,128)(2,1)}) custom-call(s32[2]{0:T(128)S(1)} %pad_add_fusion.place_ref, bf16[8,2,32,1024]{3,2,1,0:T(8,128)(2,1)S(1)} %collective-permute-done.1.other_ref, bf16[2,8,32,1024]{3,2,1,0:T(8,128)(2,1)} %get-tuple-element.34.first_in, ...), custom_call_target="tpu_custom_call", output_to_operand_aliasing={{0}: (2, {}), {1}: (3, {})} | custom-call | tf_op jit(solution)/shard_map/other_out/pallas_call | solution.py:469
Async XLA Ops:
  0.6 10.1 %copy-start = (bf16[512,1024]{1,0:T(8,128)(2,1)S(1)}, bf16[512,1024]{1,0:T(8,128)(2,1)}, u32[]{:S(2)}) copy-start(bf16[512,1024]{1,0:T(8,128)(2,1)} %refs_0_.1) | copy-start | bytes 3145732
  2.3 18.2 %all-to-all-start = ((bf16[16,16,512]{2,1,0:T(8,128)(2,1)}), bf16[16,16,512]{2,1,0:T(8,128)(2,1)S(1)}, u32[]{:S(2)}, u32[]{:S(2)}) async-start(bf16[16,16,512]{2,1,0:T(8,128)(2,1)} %pad_maximum_fusion), calls=%async_computation | async-start | bytes 524288 | tf_op jit(solution)/shard_map/all_to_all | solution.py:357
  10.7 0.7 copy-start.4
  10.7 0.7 copy-start.5
  10.7 0.7 copy-start.3
  10.7 0.7 copy-start.2
  11.4 1.2 %copy-start.1 = (bf16[512,1024]{1,0:T(8,128)(2,1)S(1)}, bf16[512,1024]{1,0:T(8,128)(2,1)}, u32[]{:S(2)}) copy-start(bf16[512,1024]{1,0:T(8,128)(2,1)} %refs_3_.1) | copy-start | bytes 3145732
  48.9 5.9 %collective-permute-start = (bf16[32,1024]{1,0:T(8,128)(2,1)S(1)}, bf16[32,1024]{1,0:T(8,128)(2,1)S(1)}, u32[]{:S(2)}, u32[]{:S(2)}) collective-permute-start(bf16[32,1024]{1,0:T(8,128)(2,1)S(1)} %get-tuple-element.33.mine_ref), channel_id=1, source_target_pairs={{0,16},{1,17},{2,18},{3,19},{4,20},{5,21},{6,22},{7,23},{8,24},{9,... | collective-permute-start | bytes 196616 | tf_op jit(solution)/shard_map/ppermute | solution.py:361
  70.7 2.7 %collective-permute-start.1 = (bf16[8,2,32,1024]{3,2,1,0:T(8,128)(2,1)S(1)}, bf16[8,2,32,1024]{3,2,1,0:T(8,128)(2,1)S(1)}, u32[]{:S(2)}, u32[]{:S(2)}) collective-permute-start(bf16[8,2,32,1024]{3,2,1,0:T(8,128)(2,1)S(1)} %all_to_all.16.mine_ref), channel_id=1, source_target_pairs={{0,1},{1,0},{2,3},{3,2},{4,5},{5,4},{6,7},{7,6},{8,9},{9,8},{10,11... | collective-permute-start | bytes 3145736 | tf_op jit(solution)/shard_map/ppermute | solution.py:361

commit v4 on v3

--- a/solution.py
+++ b/solution.py
@@ -68,17 +68,17 @@
 
 
 def switch_kernel(
-    place_ref, rows_ref, win_ref, bin_ref, gain_ref, wout_ref, bout_ref, gate_ref, msg_ref,
-    pre_s, normed_s, slope_s, inv_s, stat_s, both_s, side_s, small_s, ends_s,
+    place_ref, rows_ref, win_ref, bin_ref, gain_ref, wout_ref, bout_ref, gate_ref,
+    mine_ref, send_ref, tail_ref, small_ref,
+    pre_s, normed_s, slope_s, inv_s, stat_s, both_s, side_s, ends_s,
 ):
     core = place_ref[0]
     copy = place_ref[1]
-    twins, count, own, double = rows_ref.shape
+    count, height, double = rows_ref.shape
     width = double // 2
-    height = twins * own
     pairs = count * height // 2
     hid = win_ref.shape[1]
-    keys = msg_ref.shape[0]
+    keys = tail_ref.shape[0]
     columns = [slice(c, c + TILE) for c in range(0, hid, TILE)]
     chunks = [slice(r, r + CHUNK) for r in range(0, pairs, CHUNK)]
     gate = 1.0 / (1.0 + jnp.exp(-gate_ref[...]))
@@ -87,10 +87,7 @@
     def below(layer, here):
         return slice(layer * pairs + here.start, layer * pairs + here.stop)
 
-    blocks = [
-        jnp.concatenate([rows_ref[twin, b, :, :width] for twin in range(twins)], axis=0)
-        for b in range(count)
-    ]
+    blocks = [rows_ref[b, :, :width] for b in range(count)]
     for layer in range(LAYERS):
         paired, lower, upper = layer_halves(blocks, layer)
         span = slice(layer * pairs, (layer + 1) * pairs)
@@ -160,10 +157,7 @@
     for b in range(count):
         ends_s[0, b * height : (b + 1) * height, :] = blocks[b]
 
-    blocks = [
-        jnp.concatenate([rows_ref[twin, b, :, width:] for twin in range(twins)], axis=0)
-        for b in range(count)
-    ]
+    blocks = [rows_ref[b, :, width:] for b in range(count)]
     sum_pre = [jnp.zeros((1, TILE), F32) for _ in columns]
     sum_gain = [jnp.zeros((1, TILE), F32) for _ in columns]
     sum_mix = jnp.zeros((1, 2 * width), F32)
@@ -242,34 +236,47 @@
         ends_s[1, b * height : (b + 1) * height, :] = blocks[b]
 
     share = width // keys
-    for piece in range(width // LANES):
-        part = lax.dot_general(
-            side_s[core, copy, :, piece * LANES : (piece + 1) * LANES], both_s[core],
-            (((0,), (0,)), ((), ())), preferred_element_type=F32,
-        ).astype(BF16)
-        for i in range(LANES // share):
-            key = piece * (LANES // share) + i
-            for k in range(hid // LANES):
-                msg_ref[key, k * share : (k + 1) * share, :] = part[
-                    i * share : (i + 1) * share, k * LANES : (k + 1) * LANES
-                ]
+    slab = share * hid // LANES
+    for weight, out_ref in ((1 - core, send_ref), (core, mine_ref)):
+        for piece in range(width // LANES):
+            part = lax.dot_general(
+                side_s[weight, copy, :, piece * LANES : (piece + 1) * LANES], both_s[weight],
+                (((0,), (0,)), ((), ())), preferred_element_type=F32,
+            ).astype(out_ref.dtype)
+            for i in range(LANES // share):
+                for k in range(hid // LANES):
+                    start = (piece * (LANES // share) + i) * slab + k * share
+                    out_ref[start : start + share, :] = part[
+                        i * share : (i + 1) * share, k * LANES : (k + 1) * LANES
+                    ]
 
     row = 0
     for total in (*sum_pre, *sum_gain, sum_mix, sum_gate):
         for k in range(total.shape[1] // LANES):
-            small_s[row : row + 1, :] = total[:, k * LANES : (k + 1) * LANES]
+            small_ref[row : row + 1, :] = total[:, k * LANES : (k + 1) * LANES]
             row += 1
-    packed = split_small(small_s[...])
+    send_ref[keys * slab :, :] = split_small(small_ref[...])
     for key in range(keys):
-        start = share * hid // LANES
-        rows = pl.ds(pl.multiple_of((copy * keys + key) * height + core * own, own), own)
+        start = 0
+        rows = pl.ds(pl.multiple_of((copy * keys + key) * height, height), height)
         for t in range(2):
             for k in range(width // LANES):
-                msg_ref[key, start : start + own, :] = ends_s[
+                tail_ref[key, start : start + height, :] = ends_s[
                     t, rows, k * LANES : (k + 1) * LANES
                 ]
-                start += own
-        msg_ref[key, start:, :] = packed
+                start += height
+
+
+def core_kernel(mine_ref, tail_ref, small_ref, other_ref, msg_ref):
+    keys, tail = tail_ref.shape[:2]
+    slab = mine_ref.shape[0] // keys
+    small = join_small(split_small(small_ref[...])) + join_small(other_ref[keys * slab :, :])
+    packed = split_small(small)
+    for key in range(keys):
+        here = slice(key * slab, (key + 1) * slab)
+        msg_ref[key, :slab, :] = (mine_ref[here, :] + other_ref[here, :].astype(F32)).astype(BF16)
+        msg_ref[key, slab : slab + tail, :] = tail_ref[key]
+        msg_ref[key, slab + tail :, :] = packed
 
 
 def sum_kernel(
@@ -370,18 +377,23 @@
 
 def compute(place, rows, kept):
     hid = kept[0].shape[1]
-    twins, count, own, double = rows.shape
+    count, own, double = rows.shape
     width = double // 2
     keys = count // 2
-    pairs = twins * count * own // 2
-    share = width // keys
+    pairs = count * own // 2
+    slab = width // keys * hid // LANES
+    tail = 2 * own * width // LANES
     small_rows = (2 * hid + 4 * width) // LANES
-    msg_rows = share * hid // LANES + 2 * own * width // LANES + 2 * small_rows
     return pl.pallas_call(
         switch_kernel,
-        out_shape=jax.ShapeDtypeStruct((keys, msg_rows, LANES), BF16),
+        out_shape=[
+            jax.ShapeDtypeStruct((keys * slab, LANES), F32),
+            jax.ShapeDtypeStruct((keys * slab + 2 * small_rows, LANES), BF16),
+            jax.ShapeDtypeStruct((keys, tail, LANES), BF16),
+            jax.ShapeDtypeStruct((small_rows, LANES), F32),
+        ],
         in_specs=[SMEM] + [VMEM] * 7,
-        out_specs=VMEM,
+        out_specs=[VMEM] * 4,
         scratch_shapes=[
             pltpu.VMEM((pairs, hid), F32),
             pltpu.VMEM((LAYERS * pairs, hid), F32),
@@ -390,7 +402,6 @@
             pltpu.VMEM((3, pairs, LANES), F32),
             pltpu.VMEM((2, LAYERS * pairs, hid), BF16),
             pltpu.VMEM((2, 2, LAYERS * pairs, width), BF16),
-            pltpu.VMEM((small_rows, LANES), F32),
             pltpu.VMEM((2, 2 * pairs, width), BF16),
         ],
         compiler_params=WIDE,
@@ -421,9 +432,18 @@
     )(*kept)
     both = jnp.concatenate([tokens, cotangent], axis=-1).reshape(keys, own, 2 * width)
     rows = exchange(jnp.concatenate([both, both], axis=0), devices, top_bits)
-    rows = lax.all_gather(rows, "seq", axis=0, axis_index_groups=bit_groups(devices, [0]))
-
-    message = compute(place, rows, kept)
+
+    mine, sent, tail, small = compute(place, rows, kept)
+    message = pl.pallas_call(
+        core_kernel,
+        out_shape=jax.ShapeDtypeStruct(
+            (keys, mine.shape[0] // keys + tail.shape[1] + 2 * small.shape[0], LANES), BF16
+        ),
+        in_specs=[VMEM] * 4,
+        out_specs=VMEM,
+        compiler_params=PARAMS,
+        name="core_sum",
+    )(mine, tail, small, send(sent, devices, 1))
     share = width // keys
     got = exchange(message, devices, key_bits)
     scaling = float(rows_dev * devices // 2) ** (-0.5)

time: 75.4 us -> 72.9 us (0.967)
  Pallas kernels: 15.3 us -> 12.9 us
  blocking collectives: 32.4 us -> 30.3 us
  waiting for transfers between devices: 13.5 us -> 15.4 us
    pallas_call x1 -> x2, Pallas kernels: 10.6 us -> 8.22 us  [the longest x1 8.09 us: compute(): pl.pallas_call(switch_kernel, out_shape=[jax.ShapeDtypeStruct((keys * sla...]
    all_gather x1 -> x0, blocking collectives: 2.17 us -> none  [per_device(): lax.all_gather(rows, 'seq', axis=0, axis_index_groups=bit_groups(devices,...]
    ppermute x2 -> x3, waiting for transfers between devices: 5.78 us -> 7.69 us  [send(): return lax.ppermute(value, 'seq', [(i, i ^ mask) for i in range(devices)])]
  transfers between devices with their start and end apart: 3 -> 4, of which waited for: 3 -> 4; matrix products, arithmetic and copies ran while one was open for 0% -> 0% of each run, Pallas kernels for 2% -> 2%
where the time goes in v4:
time: 72.9 us; the launch traced here: 72.5 us
  blocking collectives  30.3 us (42%)
  waiting for transfers between devices  15.4 us (21%)
  Pallas kernels  12.9 us (18%)
  starting transfers between devices  9.5 us (13%)
  local copies, waits for them, and re-layouts  1.92 us (3%)
  other arithmetic  1.77 us (2%)
  between operations  0.74 us (1%)
    all_to_all x2, blocking collectives, exchange(): return lax.all_to_all(value, 'seq', 0, 0, axis_index_groups=groups)  30.3 us
    all_to_all x1, starting transfers between devices, exchange(): return lax.all_to_all(value, 'seq', 0, 0, axis_index_groups=groups)  8.31 us
    pallas_call x1, Pallas kernels, compute(): pl.pallas_call(switch_kernel, out_shape=[jax.ShapeDtypeStruct((keys * sla...  8.09 us
    ppermute x3, waiting for transfers between devices, send(): return lax.ppermute(value, 'seq', [(i, i ^ mask) for i in range(devices)])  7.69 us
    all_to_all x1, waiting for transfers between devices, exchange(): return lax.all_to_all(value, 'seq', 0, 0, axis_index_groups=groups)  7.69 us
    unnamed x12, local copies, waits for them, and re-layouts  1.92 us
    pallas_call x1, Pallas kernels, per_device(): pl.pallas_call(mine_kernel, out_shape=[ordered] * 2, in_specs=[SMEM, VMEM...  1.63 us
    pallas_call x1, Pallas kernels, per_device(): pl.pallas_call(other_kernel, out_shape=[ordered] * 2, in_specs=[SMEM, VME...  1.63 us
  transfers between devices with their start and end apart: 4, of which 4 were waited for; matrix products, arithmetic and copies ran while one was open for 0% of the time, Pallas kernels for 2%

profile of v4, /device:TPU:0, one launch (start us, length us, event | category | flops | bytes accessed | tf_op | source)
XLA Modules:
  0.0 72.5 jit_solution(1644023155540390222)
XLA Ops:
  0.6 0.0 copy-start
  0.6 1.0 %pad_maximum_fusion.1 = bf16[128,512]{1,0:T(8,128)(2,1)S(1)} fusion(bf16[128,256]{1,0:T(8,128)(2,1)} %param.9, bf16[128,256]{1,0:T(8,128)(2,1)} %param.8), kind=kLoop, calls=%fused_computation.1 | loop fusion | flops 262144 | bytes 262144 | tf_op jit(solution)/shard_map/concatenate | solution.py:433
  1.6 0.7 pad_maximum_fusion
  2.3 8.3 %all-to-all-start = ((bf16[16,16,512]{2,1,0:T(8,128)(2,1)}), bf16[16,16,512]{2,1,0:T(8,128)(2,1)S(1)}, u32[]{:S(2)}, u32[]{:S(2)}) async-start(bf16[16,16,512]{2,1,0:T(8,128)(2,1)} %pad_maximum_fusion), calls=%async_computation | async-start | bytes 524288 | tf_op jit(solution)/shard_map/all_to_all | solution.py:364
  10.7 0.0 copy-start.4
  10.7 0.0 copy-start.5
  10.7 0.0 copy-start.3
  10.7 0.0 copy-start.2
  10.7 0.0 copy-done
  10.7 0.6 copy-done.4
  11.3 0.0 copy-done.5
  11.4 0.0 copy-done.3
  11.4 0.0 copy-done.2
  11.4 0.0 copy-start.1
  11.4 1.2 %copy-done.1 = bf16[512,1024]{1,0:T(8,128)(2,1)S(1)} copy-done((bf16[512,1024]{1,0:T(8,128)(2,1)S(1)}, bf16[512,1024]{1,0:T(8,128)(2,1)}, u32[]{:S(2)}) %copy-start.1) | copy-done | bytes 1048600
  12.6 0.1 keep_weights.1
  12.8 0.1 pad_add_fusion.place_ref
  12.8 7.7 %all-to-all-done.rows_ref = bf16[16,16,512]{2,1,0:T(8,128)(2,1)S(1)} async-done(((bf16[16,16,512]{2,1,0:T(8,128)(2,1)}), bf16[16,16,512]{2,1,0:T(8,128)(2,1)S(1)}, u32[]{:S(2)}, u32[]{:S(2)}) %all-to-all-start) | async-done | bytes 262176 | tf_op jit(solution)/shard_map/all_to_all | solution.py:364
  20.5 8.1 %switch_layers.1 = (f32[2048,128]{1,0:T(8,128)S(1)}, bf16[2096,128]{1,0:T(8,128)(2,1)S(1)}, bf16[8,64,128]{2,1,0:T(8,128)(2,1)S(1)}, f32[24,128]{1,0:T(8,128)S(1)}) custom-call(s32[2]{0:T(128)S(1)} %pad_add_fusion.place_ref, bf16[16,16,512]{2,1,0:T(8,128)(2,1)S(1)} %all-to-all-done.rows_ref, bf16[512,1024]{1,0:T(8,128)(2,1)S(1)} %get-tuple-element.29.win_ref, ...), custom_call_target="tpu_custom_call" | custom-call | tf_op jit(solution)/shard_map/switch_layers/pallas_call | solution.py:387
  28.6 0.1 collective-permute-start
  28.7 1.9 %collective-permute-done.other_ref = bf16[2096,128]{1,0:T(8,128)(2,1)S(1)} collective-permute-done((bf16[2096,128]{1,0:T(8,128)(2,1)S(1)}, bf16[2096,128]{1,0:T(8,128)(2,1)S(1)}, u32[]{:S(2)}, u32[]{:S(2)}) %collective-permute-start) | collective-permute-done | bytes 536608 | tf_op jit(solution)/shard_map/ppermute | solution.py:368
  30.6 0.1 core_sum.1
  30.8 14.9 %all_to_all.15.got_ref = bf16[8,368,128]{2,1,0:T(8,128)(2,1)S(1)} all-to-all(bf16[8,368,128]{2,1,0:T(8,128)(2,1)S(1)} %core_sum.1), channel_id=1, replica_groups={{0,2,4,6,8,10,12,14},{1,3,5,7,9,11,13,15},{16,18,20,22,24,26,28,30},{17..., dimensions={0} | all-to-all | bytes 1507328 | tf_op jit(solution)/shard_map/all_to_all | solution.py:364
  45.7 0.7 key_sum.1
  46.4 1.1 %collective-permute-start.1 = (bf16[32,1024]{1,0:T(8,128)(2,1)S(1)}, bf16[32,1024]{1,0:T(8,128)(2,1)S(1)}, u32[]{:S(2)}, u32[]{:S(2)}) collective-permute-start(bf16[32,1024]{1,0:T(8,128)(2,1)S(1)} %get-tuple-element.41.mine_ref), channel_id=1, source_target_pairs={{0,16},{1,17},{2,18},{3,19},{4,20},{5,21},{6,22},{7,23},{8,24},{9,... | collective-permute-start | bytes 196616 | tf_op jit(solution)/shard_map/ppermute | solution.py:368
  47.5 4.8 %collective-permute-done.1.other_ref = bf16[32,1024]{1,0:T(8,128)(2,1)S(1)} collective-permute-done((bf16[32,1024]{1,0:T(8,128)(2,1)S(1)}, bf16[32,1024]{1,0:T(8,128)(2,1)S(1)}, u32[]{:S(2)}, u32[]{:S(2)}) %collective-permute-start.1) | collective-permute-done | bytes 65568 | tf_op jit(solution)/shard_map/ppermute | solution.py:368
  52.2 0.6 copy_gather.1
  52.9 15.3 %all_to_all.16.mine_ref = bf16[8,2,32,1024]{3,2,1,0:T(8,128)(2,1)S(1)} all-to-all(bf16[8,2,32,1024]{3,2,1,0:T(8,128)(2,1)S(1)} %copy_gather.1), channel_id=1, replica_groups={{0,2,4,6,8,10,12,14},{1,3,5,7,9,11,13,15},{16,18,20,22,24,26,28,30},{17..., dimensions={0} | all-to-all | bytes 2097152 | tf_op jit(solution)/shard_map/all_to_all | solution.py:364
  68.2 0.0 collective-permute-start.2
  68.2 1.6 %mine_out.1 = (bf16[2,8,32,1024]{3,2,1,0:T(8,128)(2,1)}, bf16[2,8,32,1024]{3,2,1,0:T(8,128)(2,1)}) custom-call(s32[2]{0:T(128)S(1)} %pad_add_fusion.place_ref, bf16[8,2,32,1024]{3,2,1,0:T(8,128)(2,1)S(1)} %all_to_all.16.mine_ref), custom_call_target="tpu_custom_call" | custom-call | tf_op jit(solution)/shard_map/mine_out/pallas_call | solution.py:480
  69.8 1.0 %collective-permute-done.2.other_ref = bf16[8,2,32,1024]{3,2,1,0:T(8,128)(2,1)S(1)} collective-permute-done((bf16[8,2,32,1024]{3,2,1,0:T(8,128)(2,1)S(1)}, bf16[8,2,32,1024]{3,2,1,0:T(8,128)(2,1)S(1)}, u32[]{:S(2)}, u32[]{:S(2)}) %collective-permute-start.2) | collective-permute-done | bytes 1048608 | tf_op jit(solution)/shard_map/ppermute | solution.py:368
  70.9 1.6 %other_out.1 = (bf16[2,8,32,1024]{3,2,1,0:T(8,128)(2,1)}, bf16[2,8,32,1024]{3,2,1,0:T(8,128)(2,1)}) custom-call(s32[2]{0:T(128)S(1)} %pad_add_fusion.place_ref, bf16[8,2,32,1024]{3,2,1,0:T(8,128)(2,1)S(1)} %collective-permute-done.2.other_ref, bf16[2,8,32,1024]{3,2,1,0:T(8,128)(2,1)} %get-tuple-element.42.first_in, ...), custom_call_target="tpu_custom_call", output_to_operand_aliasing={{0}: (2, {}), {1}: (3, {})} | custom-call | tf_op jit(solution)/shard_map/other_out/pallas_call | solution.py:489
Async XLA Ops:
  0.6 10.1 %copy-start = (bf16[512,1024]{1,0:T(8,128)(2,1)S(1)}, bf16[512,1024]{1,0:T(8,128)(2,1)}, u32[]{:S(2)}) copy-start(bf16[512,1024]{1,0:T(8,128)(2,1)} %refs_0_.1) | copy-start | bytes 3145732
  2.3 18.2 %all-to-all-start = ((bf16[16,16,512]{2,1,0:T(8,128)(2,1)}), bf16[16,16,512]{2,1,0:T(8,128)(2,1)S(1)}, u32[]{:S(2)}, u32[]{:S(2)}) async-start(bf16[16,16,512]{2,1,0:T(8,128)(2,1)} %pad_maximum_fusion), calls=%async_computation | async-start | bytes 524288 | tf_op jit(solution)/shard_map/all_to_all | solution.py:364
  10.7 0.7 copy-start.4
  10.7 0.7 copy-start.5
  10.7 0.7 copy-start.3
  10.7 0.7 copy-start.2
  11.4 1.2 %copy-start.1 = (bf16[512,1024]{1,0:T(8,128)(2,1)S(1)}, bf16[512,1024]{1,0:T(8,128)(2,1)}, u32[]{:S(2)}) copy-start(bf16[512,1024]{1,0:T(8,128)(2,1)} %refs_3_.1) | copy-start | bytes 3145732
  28.6 2.0 %collective-permute-start = (bf16[2096,128]{1,0:T(8,128)(2,1)S(1)}, bf16[2096,128]{1,0:T(8,128)(2,1)S(1)}, u32[]{:S(2)}, u32[]{:S(2)}) collective-permute-start(bf16[2096,128]{1,0:T(8,128)(2,1)S(1)} %get-tuple-element.38), channel_id=1, source_target_pairs={{0,1},{1,0},{2,3},{3,2},{4,5},{5,4},{6,7},{7,6},{8,9},{9,8},{10,11... | collective-permute-start | bytes 1609736 | tf_op jit(solution)/shard_map/ppermute | solution.py:368
  46.4 5.9 %collective-permute-start.1 = (bf16[32,1024]{1,0:T(8,128)(2,1)S(1)}, bf16[32,1024]{1,0:T(8,128)(2,1)S(1)}, u32[]{:S(2)}, u32[]{:S(2)}) collective-permute-start(bf16[32,1024]{1,0:T(8,128)(2,1)S(1)} %get-tuple-element.41.mine_ref), channel_id=1, source_target_pairs={{0,16},{1,17},{2,18},{3,19},{4,20},{5,21},{6,22},{7,23},{8,24},{9,... | collective-permute-start | bytes 196616 | tf_op jit(solution)/shard_map/ppermute | solution.py:368
  68.2 2.7 %collective-permute-start.2 = (bf16[8,2,32,1024]{3,2,1,0:T(8,128)(2,1)S(1)}, bf16[8,2,32,1024]{3,2,1,0:T(8,128)(2,1)S(1)}, u32[]{:S(2)}, u32[]{:S(2)}) collective-permute-start(bf16[8,2,32,1024]{3,2,1,0:T(8,128)(2,1)S(1)} %all_to_all.16.mine_ref), channel_id=1, source_target_pairs={{0,1},{1,0},{2,3},{3,2},{4,5},{5,4},{6,7},{7,6},{8,9},{9,8},{10,11... | collective-permute-start | bytes 3145736 | tf_op jit(solution)/shard_map/ppermute | solution.py:368

commit v5 on v4

--- a/solution.py
+++ b/solution.py
@@ -67,18 +67,25 @@
     return jnp.sum(folded, axis=-1, keepdims=True)
 
 
+def core_place():
+    return lax.axis_index("seq") & 1
+
+
+def copy_place():
+    return lax.axis_index("seq") >> (lax.axis_size("seq").bit_length() - 2) & 1
+
+
 def switch_kernel(
-    place_ref, rows_ref, win_ref, bin_ref, gain_ref, wout_ref, bout_ref, gate_ref,
-    mine_ref, send_ref, tail_ref, small_ref,
-    pre_s, normed_s, slope_s, inv_s, stat_s, both_s, side_s, ends_s,
+    rows_ref, win_ref, bin_ref, gain_ref, wout_ref, bout_ref, gate_ref,
+    send_ref, both_s, side_s, ends_s, small_ref,
+    pre_s, normed_s, slope_s, inv_s, stat_s,
 ):
-    core = place_ref[0]
-    copy = place_ref[1]
+    core, copy = core_place(), copy_place()
     count, height, double = rows_ref.shape
     width = double // 2
     pairs = count * height // 2
     hid = win_ref.shape[1]
-    keys = tail_ref.shape[0]
+    keys = count // 2
     columns = [slice(c, c + TILE) for c in range(0, hid, TILE)]
     chunks = [slice(r, r + CHUNK) for r in range(0, pairs, CHUNK)]
     gate = 1.0 / (1.0 + jnp.exp(-gate_ref[...]))
@@ -235,33 +242,44 @@
     for b in range(count):
         ends_s[1, b * height : (b + 1) * height, :] = blocks[b]
 
-    share = width // keys
-    slab = share * hid // LANES
-    for weight, out_ref in ((1 - core, send_ref), (core, mine_ref)):
-        for piece in range(width // LANES):
-            part = lax.dot_general(
-                side_s[weight, copy, :, piece * LANES : (piece + 1) * LANES], both_s[weight],
-                (((0,), (0,)), ((), ())), preferred_element_type=F32,
-            ).astype(out_ref.dtype)
-            for i in range(LANES // share):
-                for k in range(hid // LANES):
-                    start = (piece * (LANES // share) + i) * slab + k * share
-                    out_ref[start : start + share, :] = part[
-                        i * share : (i + 1) * share, k * LANES : (k + 1) * LANES
-                    ]
-
+    weight_part(side_s.at[1 - core, copy], both_s.at[1 - core], send_ref)
     row = 0
     for total in (*sum_pre, *sum_gain, sum_mix, sum_gate):
         for k in range(total.shape[1] // LANES):
             small_ref[row : row + 1, :] = total[:, k * LANES : (k + 1) * LANES]
             row += 1
-    send_ref[keys * slab :, :] = split_small(small_ref[...])
+    packed = split_small(small_ref[...])
+    send_ref[send_ref.shape[0] - packed.shape[0] :, :] = packed
+
+
+def weight_part(left_ref, right_ref, out_ref):
+    width, hid = left_ref.shape[1], right_ref.shape[1]
+    share = 2 * width // 2**LAYERS
+    for piece in range(width // LANES):
+        part = lax.dot_general(
+            left_ref[:, piece * LANES : (piece + 1) * LANES], right_ref[...],
+            (((0,), (0,)), ((), ())), preferred_element_type=F32,
+        ).astype(out_ref.dtype)
+        for i in range(LANES // share):
+            for k in range(hid // LANES):
+                start = ((piece * (LANES // share) + i) * hid // LANES + k) * share
+                out_ref[start : start + share, :] = part[
+                    i * share : (i + 1) * share, k * LANES : (k + 1) * LANES
+                ]
+
+
+def own_kernel(both_ref, side_ref, ends_ref, mine_ref, tail_ref):
+    core, copy = core_place(), copy_place()
+    keys = tail_ref.shape[0]
+    width = ends_ref.shape[2]
+    height = ends_ref.shape[1] // (2 * keys)
+    weight_part(side_ref.at[core, copy], both_ref.at[core], mine_ref)
     for key in range(keys):
         start = 0
         rows = pl.ds(pl.multiple_of((copy * keys + key) * height, height), height)
         for t in range(2):
             for k in range(width // LANES):
-                tail_ref[key, start : start + height, :] = ends_s[
+                tail_ref[key, start : start + height, :] = ends_ref[
                     t, rows, k * LANES : (k + 1) * LANES
                 ]
                 start += height
@@ -279,22 +297,23 @@
         msg_ref[key, slab + tail :, :] = packed
 
 
-def sum_kernel(
-    sizes, scaling, got_ref, gate_ref,
-    slice_ref, final_ref, grad_ref, pre_ref, gain_ref, mix_ref, gout_ref,
-):
-    share, own, width = sizes
-    keys = got_ref.shape[0]
-    hid = slice_ref.shape[1]
+def slice_kernel(scaling, got_ref, slice_ref):
+    share, hid = slice_ref.shape
     for k in range(hid // LANES):
         here = slice(k * share, (k + 1) * share)
         total = got_ref[0, here, :].astype(F32)
-        for key in range(1, keys):
+        for key in range(1, got_ref.shape[0]):
             total += got_ref[key, here, :].astype(F32)
         slice_ref[:, k * LANES : (k + 1) * LANES] = (total * scaling).astype(slice_ref.dtype)
-    start = share * hid // LANES
+
+
+def rows_kernel(
+    start, scaling, got_ref, gate_ref, final_ref, grad_ref, pre_ref, gain_ref, mix_ref, gout_ref
+):
+    keys = got_ref.shape[0]
+    own = final_ref.shape[0] // keys
     for out_ref in (final_ref, grad_ref):
-        for k in range(width // LANES):
+        for k in range(final_ref.shape[1] // LANES):
             for key in range(keys):
                 out_ref[key * own : (key + 1) * own, k * LANES : (k + 1) * LANES] = got_ref[
                     key, start : start + own, :
@@ -315,11 +334,11 @@
         first += count
 
 
-def gather_kernel(place_ref, mine_ref, other_ref, out_ref):
-    copy = place_ref[1]
+def spread_kernel(flip, slice_ref, *refs):
+    out_ref = refs[-1]
+    copy = copy_place()
     for key in range(out_ref.shape[0]):
-        out_ref[key, copy] = mine_ref[...]
-        out_ref[key, 1 - copy] = other_ref[...]
+        out_ref[key, 1 - copy if flip else copy] = slice_ref[...]
 
 
 def move_weight(source_ref, target_ref, sems):
@@ -337,18 +356,18 @@
         move.wait()
 
 
-def mine_kernel(place_ref, mine_ref, first_ref, second_ref, sems):
+def mine_kernel(mine_ref, first_ref, second_ref, sems):
     for core, out_ref in enumerate((first_ref, second_ref)):
 
-        @pl.when(place_ref[0] == core)
+        @pl.when(core_place() == core)
         def _():
             move_weight(mine_ref, out_ref, sems)
 
 
-def other_kernel(place_ref, other_ref, first_in, second_in, first_ref, second_ref, sems):
+def other_kernel(other_ref, first_in, second_in, first_ref, second_ref, sems):
     for core, out_ref in enumerate((second_ref, first_ref)):
 
-        @pl.when(place_ref[0] == core)
+        @pl.when(core_place() == core)
         def _():
             move_weight(other_ref, out_ref, sems)
 
@@ -369,44 +388,38 @@
 
 
 VMEM = pl.BlockSpec(memory_space=pltpu.VMEM)
-SMEM = pl.BlockSpec(memory_space=pltpu.SMEM)
 HBM = pl.BlockSpec(memory_space=pltpu.HBM)
 PARAMS = pltpu.CompilerParams(vmem_limit_bytes=4 * 1024 * 1024)
 WIDE = pltpu.CompilerParams(vmem_limit_bytes=32 * 1024 * 1024)
 
 
-def compute(place, rows, kept):
+def compute(rows, kept):
     hid = kept[0].shape[1]
     count, own, double = rows.shape
     width = double // 2
-    keys = count // 2
     pairs = count * own // 2
-    slab = width // keys * hid // LANES
-    tail = 2 * own * width // LANES
     small_rows = (2 * hid + 4 * width) // LANES
     return pl.pallas_call(
         switch_kernel,
         out_shape=[
-            jax.ShapeDtypeStruct((keys * slab, LANES), F32),
-            jax.ShapeDtypeStruct((keys * slab + 2 * small_rows, LANES), BF16),
-            jax.ShapeDtypeStruct((keys, tail, LANES), BF16),
+            jax.ShapeDtypeStruct((width * hid // LANES + 2 * small_rows, LANES), BF16),
+            jax.ShapeDtypeStruct((2, LAYERS * pairs, hid), BF16),
+            jax.ShapeDtypeStruct((2, 2, LAYERS * pairs, width), BF16),
+            jax.ShapeDtypeStruct((2, 2 * pairs, width), BF16),
             jax.ShapeDtypeStruct((small_rows, LANES), F32),
         ],
-        in_specs=[SMEM] + [VMEM] * 7,
-        out_specs=[VMEM] * 4,
+        in_specs=[VMEM] * 7,
+        out_specs=[VMEM] * 5,
         scratch_shapes=[
             pltpu.VMEM((pairs, hid), F32),
             pltpu.VMEM((LAYERS * pairs, hid), F32),
             pltpu.VMEM((LAYERS * pairs, hid), F32),
             pltpu.VMEM((LAYERS * pairs, LANES), F32),
             pltpu.VMEM((3, pairs, LANES), F32),
-            pltpu.VMEM((2, LAYERS * pairs, hid), BF16),
-            pltpu.VMEM((2, 2, LAYERS * pairs, width), BF16),
-            pltpu.VMEM((2, 2 * pairs, width), BF16),
         ],
         compiler_params=WIDE,
         name="switch_layers",
-    )(place, rows, *kept)
+    )(rows, *kept)
 
 
 def per_device(tokens, cotangent, weight_in, bias_in, norm_gain, weight_out, bias_out, gate_logit):
@@ -414,12 +427,10 @@
     hid = weight_in.shape[1]
     devices = lax.axis_size("seq")
     top_bit = devices.bit_length() - 1
-    index = lax.axis_index("seq").astype(jnp.int32)
     top_bits = list(range(top_bit - LAYERS, top_bit))
     key_bits, copy_bit = top_bits[:-1], top_bits[-1]
     keys = 2 ** len(key_bits)
     own = rows_dev // keys
-    place = jnp.stack([index & 1, index >> copy_bit & 1])
 
     kept = (weight_in, bias_in[None], norm_gain[None], weight_out, bias_out[None], gate_logit[None])
     kept = pl.pallas_call(
@@ -433,7 +444,19 @@
     both = jnp.concatenate([tokens, cotangent], axis=-1).reshape(keys, own, 2 * width)
     rows = exchange(jnp.concatenate([both, both], axis=0), devices, top_bits)
 
-    mine, sent, tail, small = compute(place, rows, kept)
+    sent, both_sides, sides, ends, small = compute(rows, kept)
+    received = send(sent, devices, 1)
+    mine, tail = pl.pallas_call(
+        own_kernel,
+        out_shape=[
+            jax.ShapeDtypeStruct((width * hid // LANES, LANES), F32),
+            jax.ShapeDtypeStruct((keys, 2 * own * width // LANES, LANES), BF16),
+        ],
+        in_specs=[VMEM] * 3,
+        out_specs=[VMEM] * 2,
+        compiler_params=PARAMS,
+        name="own_part",
+    )(both_sides, sides, ends)
     message = pl.pallas_call(
         core_kernel,
         out_shape=jax.ShapeDtypeStruct(
@@ -443,22 +466,29 @@
         out_specs=VMEM,
         compiler_params=PARAMS,
         name="core_sum",
-    )(mine, tail, small, send(sent, devices, 1))
+    )(mine, tail, small, received)
     share = width // keys
     got = exchange(message, devices, key_bits)
     scaling = float(rows_dev * devices // 2) ** (-0.5)
     rest = list(range(1, top_bit - LAYERS))
     rows_shape = jax.ShapeDtypeStruct((rows_dev, width), BF16)
     tall, short = hid // LANES, 2 * width // LANES
-    owned, final_rows, grad_rows, *small = pl.pallas_call(
-        functools.partial(sum_kernel, (share, own, width), scaling),
-        out_shape=[jax.ShapeDtypeStruct((share, hid), F32 if rest else BF16)]
-        + [rows_shape] * 2
+    owned = pl.pallas_call(
+        functools.partial(slice_kernel, scaling),
+        out_shape=jax.ShapeDtypeStruct((share, hid), F32 if rest else BF16),
+        in_specs=[VMEM],
+        out_specs=VMEM,
+        compiler_params=PARAMS,
+        name="slice_sum",
+    )(got)
+    final_rows, grad_rows, *small = pl.pallas_call(
+        functools.partial(rows_kernel, share * hid // LANES, scaling),
+        out_shape=[rows_shape] * 2
         + [jax.ShapeDtypeStruct((n, LANES), F32) for n in (tall, tall, short, short)],
         in_specs=[VMEM] * 2,
-        out_specs=[VMEM] * 7,
-        compiler_params=PARAMS,
-        name="key_sum",
+        out_specs=[VMEM] * 6,
+        compiler_params=PARAMS,
+        name="rows_out",
     )(got, kept[5].reshape(-1, LANES))
     if rest:
         owned, *small = lax.psum(
@@ -466,36 +496,47 @@
         )
         owned = owned.astype(BF16)
 
+    twin = send(owned, devices, 1 << copy_bit)
+    spread_shape = jax.ShapeDtypeStruct((keys, 2, share, hid), BF16)
     spread = pl.pallas_call(
-        gather_kernel,
-        out_shape=jax.ShapeDtypeStruct((keys, 2, share, hid), BF16),
-        in_specs=[SMEM, VMEM, VMEM],
+        functools.partial(spread_kernel, False),
+        out_shape=spread_shape,
+        in_specs=[VMEM],
         out_specs=VMEM,
         compiler_params=PARAMS,
-        name="copy_gather",
-    )(place, owned, send(owned, devices, 1 << copy_bit))
+        name="spread_own",
+    )(owned)
+    spread = pl.pallas_call(
+        functools.partial(spread_kernel, True),
+        out_shape=spread_shape,
+        in_specs=[VMEM, VMEM],
+        out_specs=VMEM,
+        input_output_aliases={1: 0},
+        compiler_params=PARAMS,
+        name="spread_twin",
+    )(twin, spread)
     whole = exchange(spread, devices, key_bits)
     other = send(whole, devices, 1)
     ordered = jax.ShapeDtypeStruct((2, keys, share, hid), BF16)
     weights = pl.pallas_call(
         mine_kernel,
         out_shape=[ordered] * 2,
-        in_specs=[SMEM, VMEM],
+        in_specs=[VMEM],
         out_specs=[HBM] * 2,
         scratch_shapes=[pltpu.SemaphoreType.DMA((2 * keys,))],
         compiler_params=PARAMS,
         name="mine_out",
-    )(place, whole)
+    )(whole)
     grad_weight_in, grad_weight_out = pl.pallas_call(
         other_kernel,
         out_shape=[ordered] * 2,
-        in_specs=[SMEM, VMEM, HBM, HBM],
+        in_specs=[VMEM, HBM, HBM],
         out_specs=[HBM] * 2,
         scratch_shapes=[pltpu.SemaphoreType.DMA((2 * keys,))],
-        input_output_aliases={2: 0, 3: 1},
+        input_output_aliases={1: 0, 2: 1},
         compiler_params=PARAMS,
         name="other_out",
-    )(place, other, *weights)
+    )(other, *weights)
     return (
         final_rows,
         grad_rows,

time: 72.9 us -> 70.5 us (0.967)
  waiting for transfers between devices: 15.4 us -> 11.5 us
  local copies, waits for them, and re-layouts: 1.92 us -> 5.18 us
  Pallas kernels: 12.9 us -> 11.1 us
    unnamed x12, local copies, waits for them, and re-layouts: 1.92 us -> 5.18 us
    all_to_all x1, waiting for transfers between devices: 7.69 us -> 4.54 us  [exchange(): return lax.all_to_all(value, 'seq', 0, 0, axis_index_groups=groups)]
    pallas_call x5 -> x8, Pallas kernels: 12.7 us -> 10.9 us  [the longest x1 7.36 us: compute(): pl.pallas_call(switch_kernel, out_shape=[jax.ShapeDtypeStruct((width * hi...]
  transfers between devices with their start and end apart: 4 -> 4, of which waited for: 4 -> 4; matrix products, arithmetic and copies ran while one was open for 0% -> 0% of each run, Pallas kernels for 2% -> 3%
where the time goes in v5:
time: 70.5 us; the launch traced here: 70 us
  blocking collectives  30.3 us (43%)
  waiting for transfers between devices  11.5 us (16%)
  Pallas kernels  11.1 us (16%)
  starting transfers between devices  9.55 us (14%)
  local copies, waits for them, and re-layouts  5.18 us (7%)
  other arithmetic  1.6 us (2%)
  between operations  0.71 us (1%)
    all_to_all x2, blocking collectives, exchange(): return lax.all_to_all(value, 'seq', 0, 0, axis_index_groups=groups)  30.3 us
    all_to_all x1, starting transfers between devices, exchange(): return lax.all_to_all(value, 'seq', 0, 0, axis_index_groups=groups)  8.31 us
    pallas_call x1, Pallas kernels, compute(): pl.pallas_call(switch_kernel, out_shape=[jax.ShapeDtypeStruct((width * hi...  7.36 us
    ppermute x3, waiting for transfers between devices, send(): return lax.ppermute(value, 'seq', [(i, i ^ mask) for i in range(devices)])  7.01 us
    unnamed x12, local copies, waits for them, and re-layouts  5.18 us
    all_to_all x1, waiting for transfers between devices, exchange(): return lax.all_to_all(value, 'seq', 0, 0, axis_index_groups=groups)  4.54 us
  transfers between devices with their start and end apart: 4, of which 4 were waited for; matrix products, arithmetic and copies ran while one was open for 0% of the time, Pallas kernels for 3%

profile of v5, /device:TPU:0, one launch (start us, length us, event | category | flops | bytes accessed | tf_op | source)
XLA Modules:
  0.0 70.0 jit_solution(5154055934040432095)
XLA Ops:
  0.6 0.9 %pad_maximum_fusion.1 = bf16[128,512]{1,0:T(8,128)(2,1)S(1)} fusion(bf16[128,256]{1,0:T(8,128)(2,1)} %param.9, bf16[128,256]{1,0:T(8,128)(2,1)} %param.8), kind=kLoop, calls=%fused_computation.1 | loop fusion | flops 262144 | bytes 262144 | tf_op jit(solution)/shard_map/concatenate | solution.py:444
  1.5 0.7 %pad_maximum_fusion = bf16[16,16,512]{2,1,0:T(8,128)(2,1)} fusion(bf16[8,16,512]{2,1,0:T(8,128)(2,1)S(1)} %bitcast.19), kind=kLoop, calls=%fused_computation | loop fusion | flops 131072 | bytes 393216 | tf_op jit(solution)/shard_map/concatenate | solution.py:445
  2.2 8.3 %all-to-all-start = ((bf16[16,16,512]{2,1,0:T(8,128)(2,1)}), bf16[16,16,512]{2,1,0:T(8,128)(2,1)S(1)}, u32[]{:S(2)}, u32[]{:S(2)}) async-start(bf16[16,16,512]{2,1,0:T(8,128)(2,1)} %pad_maximum_fusion), calls=%async_computation | async-start | bytes 524288 | tf_op jit(solution)/shard_map/all_to_all | solution.py:383
  10.6 0.0 copy-start
  10.6 1.2 %copy-done = bf16[512,1024]{1,0:T(8,128)(2,1)S(1)} copy-done((bf16[512,1024]{1,0:T(8,128)(2,1)S(1)}, bf16[512,1024]{1,0:T(8,128)(2,1)}, u32[]{:S(2)}) %copy-start) | copy-done | bytes 1048600
  11.8 0.0 copy-start.1
  11.8 1.2 %copy-done.1 = bf16[512,1024]{1,0:T(8,128)(2,1)S(1)} copy-done((bf16[512,1024]{1,0:T(8,128)(2,1)S(1)}, bf16[512,1024]{1,0:T(8,128)(2,1)}, u32[]{:S(2)}) %copy-start.1) | copy-done | bytes 1048600
  13.0 0.0 copy-start.2
  13.0 0.7 copy-done.2
  13.7 0.0 copy-start.3
  13.7 0.7 copy-done.3
  14.4 0.0 copy-start.4
  14.4 0.7 copy-done.4
  15.1 0.0 copy-start.5
  15.1 0.7 copy-done.5
  15.8 0.1 keep_weights.1
  15.9 4.5 %all-to-all-done.rows_ref = bf16[16,16,512]{2,1,0:T(8,128)(2,1)S(1)} async-done(((bf16[16,16,512]{2,1,0:T(8,128)(2,1)}), bf16[16,16,512]{2,1,0:T(8,128)(2,1)S(1)}, u32[]{:S(2)}, u32[]{:S(2)}) %all-to-all-start) | async-done | bytes 262176 | tf_op jit(solution)/shard_map/all_to_all | solution.py:383
  20.4 7.4 %switch_layers.1 = (bf16[2096,128]{1,0:T(8,128)(2,1)S(1)}, bf16[2,512,1024]{2,1,0:T(8,128)(2,1)S(1)}, bf16[2,2,512,256]{3,2,1,0:T(8,128)(2,1)S(1)}, bf16[2,256,256]{2,1,0:T(8,128)(2,1)S(1)}, f32[24,128]{1,0:T(8,128)S(1)}) custom-call(bf16[16,16,512]{2,1,0:T(8,128)(2,1)S(1)} %all-to-all-done.rows_ref, bf16[512,1024]{1,0:T(8,128)(2,1)S(1)} %get-tuple-element.31.win_ref, ...), custom_call_target="tpu_custom_call" | custom-call | tf_op jit(solution)/shard_map/switch_layers/pallas_call | solution.py:402
  27.8 0.1 collective-permute-start
  27.9 0.5 own_part.1
  28.4 1.4 %collective-permute-done.other_ref = bf16[2096,128]{1,0:T(8,128)(2,1)S(1)} collective-permute-done((bf16[2096,128]{1,0:T(8,128)(2,1)S(1)}, bf16[2096,128]{1,0:T(8,128)(2,1)S(1)}, u32[]{:S(2)}, u32[]{:S(2)}) %collective-permute-start) | collective-permute-done | bytes 536608 | tf_op jit(solution)/shard_map/ppermute | solution.py:387
  29.8 0.1 core_sum.1
  29.9 14.9 %all_to_all.15.got_ref = bf16[8,368,128]{2,1,0:T(8,128)(2,1)S(1)} all-to-all(bf16[8,368,128]{2,1,0:T(8,128)(2,1)S(1)} %core_sum.1), channel_id=1, replica_groups={{0,2,4,6,8,10,12,14},{1,3,5,7,9,11,13,15},{16,18,20,22,24,26,28,30},{17..., dimensions={0} | all-to-all | bytes 1507328 | tf_op jit(solution)/shard_map/all_to_all | solution.py:383
  44.8 0.1 slice_sum.1.slice_ref
  44.9 1.2 %collective-permute-start.1 = (bf16[32,1024]{1,0:T(8,128)(2,1)S(1)}, bf16[32,1024]{1,0:T(8,128)(2,1)S(1)}, u32[]{:S(2)}, u32[]{:S(2)}) collective-permute-start(bf16[32,1024]{1,0:T(8,128)(2,1)S(1)} %slice_sum.1.slice_ref), channel_id=1, source_target_pairs={{0,16},{1,17},{2,18},{3,19},{4,20},{5,21},{6,22},{7,23},{8,24},{9,... | collective-permute-start | bytes 196616 | tf_op jit(solution)/shard_map/ppermute | solution.py:387
  46.1 4.7 %collective-permute-done.1.slice_ref = bf16[32,1024]{1,0:T(8,128)(2,1)S(1)} collective-permute-done((bf16[32,1024]{1,0:T(8,128)(2,1)S(1)}, bf16[32,1024]{1,0:T(8,128)(2,1)S(1)}, u32[]{:S(2)}, u32[]{:S(2)}) %collective-permute-start.1) | collective-permute-done | bytes 65568 | tf_op jit(solution)/shard_map/ppermute | solution.py:387
  50.9 15.3 %all_to_all.16.mine_ref = bf16[8,2,32,1024]{3,2,1,0:T(8,128)(2,1)S(1)} all-to-all(bf16[8,2,32,1024]{3,2,1,0:T(8,128)(2,1)S(1)} %spread_twin.1), channel_id=1, replica_groups={{0,2,4,6,8,10,12,14},{1,3,5,7,9,11,13,15},{16,18,20,22,24,26,28,30},{17..., dimensions={0} | all-to-all | bytes 2097152 | tf_op jit(solution)/shard_map/all_to_all | solution.py:383
  66.2 0.0 collective-permute-start.2
  66.2 0.7 rows_out.1
  66.9 1.1 %mine_out.1 = (bf16[2,8,32,1024]{3,2,1,0:T(8,128)(2,1)}, bf16[2,8,32,1024]{3,2,1,0:T(8,128)(2,1)}) custom-call(bf16[8,2,32,1024]{3,2,1,0:T(8,128)(2,1)S(1)} %all_to_all.16.mine_ref), custom_call_target="tpu_custom_call" | custom-call | tf_op jit(solution)/shard_map/mine_out/pallas_call | solution.py:521
  68.0 0.9 %collective-permute-done.2.other_ref = bf16[8,2,32,1024]{3,2,1,0:T(8,128)(2,1)S(1)} collective-permute-done((bf16[8,2,32,1024]{3,2,1,0:T(8,128)(2,1)S(1)}, bf16[8,2,32,1024]{3,2,1,0:T(8,128)(2,1)S(1)}, u32[]{:S(2)}, u32[]{:S(2)}) %collective-permute-start.2) | collective-permute-done | bytes 1048608 | tf_op jit(solution)/shard_map/ppermute | solution.py:387
  68.9 1.1 %other_out.1 = (bf16[2,8,32,1024]{3,2,1,0:T(8,128)(2,1)}, bf16[2,8,32,1024]{3,2,1,0:T(8,128)(2,1)}) custom-call(bf16[8,2,32,1024]{3,2,1,0:T(8,128)(2,1)S(1)} %collective-permute-done.2.other_ref, bf16[2,8,32,1024]{3,2,1,0:T(8,128)(2,1)} %get-tuple-element.46.first_in, ...), custom_call_target="tpu_custom_call", output_to_operand_aliasing={{0}: (1, {}), {1}: (2, {})} | custom-call | tf_op jit(solution)/shard_map/other_out/pallas_call | solution.py:530
  (2 shorter events, 0.1 us)
Async XLA Ops:
  2.2 18.2 %all-to-all-start = ((bf16[16,16,512]{2,1,0:T(8,128)(2,1)}), bf16[16,16,512]{2,1,0:T(8,128)(2,1)S(1)}, u32[]{:S(2)}, u32[]{:S(2)}) async-start(bf16[16,16,512]{2,1,0:T(8,128)(2,1)} %pad_maximum_fusion), calls=%async_computation | async-start | bytes 524288 | tf_op jit(solution)/shard_map/all_to_all | solution.py:383
  10.6 1.2 %copy-start = (bf16[512,1024]{1,0:T(8,128)(2,1)S(1)}, bf16[512,1024]{1,0:T(8,128)(2,1)}, u32[]{:S(2)}) copy-start(bf16[512,1024]{1,0:T(8,128)(2,1)} %refs_0_.1) | copy-start | bytes 3145732
  11.8 1.2 %copy-start.1 = (bf16[512,1024]{1,0:T(8,128)(2,1)S(1)}, bf16[512,1024]{1,0:T(8,128)(2,1)}, u32[]{:S(2)}) copy-start(bf16[512,1024]{1,0:T(8,128)(2,1)} %refs_3_.1) | copy-start | bytes 3145732
  13.0 0.7 copy-start.2
  13.7 0.7 copy-start.3
  14.4 0.7 copy-start.4
  15.1 0.7 copy-start.5
  27.8 2.0 %collective-permute-start = (bf16[2096,128]{1,0:T(8,128)(2,1)S(1)}, bf16[2096,128]{1,0:T(8,128)(2,1)S(1)}, u32[]{:S(2)}, u32[]{:S(2)}) collective-permute-start(bf16[2096,128]{1,0:T(8,128)(2,1)S(1)} %get-tuple-element.43), channel_id=1, source_target_pairs={{0,1},{1,0},{2,3},{3,2},{4,5},{5,4},{6,7},{7,6},{8,9},{9,8},{10,11... | collective-permute-start | bytes 1609736 | tf_op jit(solution)/shard_map/ppermute | solution.py:387
  44.9 5.9 %collective-permute-start.1 = (bf16[32,1024]{1,0:T(8,128)(2,1)S(1)}, bf16[32,1024]{1,0:T(8,128)(2,1)S(1)}, u32[]{:S(2)}, u32[]{:S(2)}) collective-permute-start(bf16[32,1024]{1,0:T(8,128)(2,1)S(1)} %slice_sum.1.slice_ref), channel_id=1, source_target_pairs={{0,16},{1,17},{2,18},{3,19},{4,20},{5,21},{6,22},{7,23},{8,24},{9,... | collective-permute-start | bytes 196616 | tf_op jit(solution)/shard_map/ppermute | solution.py:387
  66.2 2.7 %collective-permute-start.2 = (bf16[8,2,32,1024]{3,2,1,0:T(8,128)(2,1)S(1)}, bf16[8,2,32,1024]{3,2,1,0:T(8,128)(2,1)S(1)}, u32[]{:S(2)}, u32[]{:S(2)}) collective-permute-start(bf16[8,2,32,1024]{3,2,1,0:T(8,128)(2,1)S(1)} %all_to_all.16.mine_ref), channel_id=1, source_target_pairs={{0,1},{1,0},{2,3},{3,2},{4,5},{5,4},{6,7},{7,6},{8,9},{9,8},{10,11... | collective-permute-start | bytes 3145736 | tf_op jit(solution)/shard_map/ppermute | solution.py:387

commit v6 on v5

--- a/solution.py
+++ b/solution.py
@@ -75,9 +75,29 @@
     return lax.axis_index("seq") >> (lax.axis_size("seq").bit_length() - 2) & 1
 
 
+def output_vectors(vectors_ref, width):
+    begin = vectors_ref.shape[1] - 4 * width
+    bias_out = vectors_ref[:, begin : begin + 2 * width]
+    return bias_out, 1.0 / (1.0 + jnp.exp(-vectors_ref[:, begin + 2 * width :]))
+
+
+def layer_result(paired, hidden_ref, wout_ref, gate, bias_out):
+    mixed = lax.dot_general(
+        hidden_ref[...], wout_ref[...], (((1,), (1,)), ((), ())), preferred_element_type=F32
+    )
+    return (gate * paired.astype(F32) + branch_scale * (mixed + bias_out)).astype(BF16)
+
+
+def layer_grads(grad_out, cast_ref, win_ref, gate):
+    back_in = lax.dot_general(
+        cast_ref[...], win_ref[...], (((1,), (1,)), ((), ())), preferred_element_type=F32
+    )
+    return (gate * grad_out.astype(F32) + back_in).astype(BF16)
+
+
 def switch_kernel(
-    rows_ref, win_ref, bin_ref, gain_ref, wout_ref, bout_ref, gate_ref,
-    send_ref, both_s, side_s, ends_s, small_ref,
+    rows_ref, win_ref, wout_ref, vectors_ref,
+    send_ref, both_s, side_s, first_ref, small_ref,
     pre_s, normed_s, slope_s, inv_s, stat_s,
 ):
     core, copy = core_place(), copy_place()
@@ -88,8 +108,8 @@
     keys = count // 2
     columns = [slice(c, c + TILE) for c in range(0, hid, TILE)]
     chunks = [slice(r, r + CHUNK) for r in range(0, pairs, CHUNK)]
-    gate = 1.0 / (1.0 + jnp.exp(-gate_ref[...]))
-    bias_out = bout_ref[...]
+    bin_ref, gain_ref = vectors_ref.at[:, :hid], vectors_ref.at[:, hid : 2 * hid]
+    bias_out, gate = output_vectors(vectors_ref, width)
 
     def below(layer, here):
         return slice(layer * pairs + here.start, layer * pairs + here.stop)
@@ -147,22 +167,11 @@
                 )
                 normed_s[there, column] = normed
 
-        activate(columns[0])
-        mixed = None
-        for i, column in enumerate(columns):
-            if i + 1 < len(columns):
-                activate(columns[i + 1])
-            part = lax.dot_general(
-                both_s[1, span, column], wout_ref[:, column], (((1,), (1,)), ((), ())),
-                preferred_element_type=F32,
-            )
-            mixed = part if mixed is None else mixed + part
-        result = (
-            gate * paired.astype(F32) + branch_scale * (mixed + bias_out)
-        ).astype(BF16)
-        blocks = layer_blocks(result, lower, upper, height, width)
-    for b in range(count):
-        ends_s[0, b * height : (b + 1) * height, :] = blocks[b]
+        for column in columns:
+            activate(column)
+        if layer + 1 < LAYERS:
+            result = layer_result(paired, both_s.at[1, span], wout_ref, gate, bias_out)
+            blocks = layer_blocks(result, lower, upper, height, width)
 
     blocks = [rows_ref[b, :, width:] for b in range(count)]
     sum_pre = [jnp.zeros((1, TILE), F32) for _ in columns]
@@ -227,20 +236,12 @@
                 both_s[0, there, column] = pre_grads.astype(BF16)
             sum_pre[i] += jnp.sum(total, axis=0, keepdims=True)
 
-        finish(0, columns[0])
-        back_in = None
         for i, column in enumerate(columns):
-            if i + 1 < len(columns):
-                finish(i + 1, columns[i + 1])
-            part = lax.dot_general(
-                both_s[0, span, column], win_ref[:, column], (((1,), (1,)), ((), ())),
-                preferred_element_type=F32,
-            )
-            back_in = part if back_in is None else back_in + part
-        result = (gate * out_grads + back_in).astype(BF16)
-        blocks = layer_blocks(result, lower, upper, height, width)
-    for b in range(count):
-        ends_s[1, b * height : (b + 1) * height, :] = blocks[b]
+            finish(i, column)
+        if layer:
+            result = layer_grads(grad_out, both_s.at[0, span], win_ref, gate)
+            blocks = layer_blocks(result, lower, upper, height, width)
+    first_ref[...] = grad_out
 
     weight_part(side_s.at[1 - core, copy], both_s.at[1 - core], send_ref)
     row = 0
@@ -268,18 +269,31 @@
                 ]
 
 
-def own_kernel(both_ref, side_ref, ends_ref, mine_ref, tail_ref):
+def own_kernel(
+    both_ref, side_ref, first_ref, win_ref, wout_ref, vectors_ref, mine_ref, tail_ref, ends_s
+):
     core, copy = core_place(), copy_place()
     keys = tail_ref.shape[0]
-    width = ends_ref.shape[2]
-    height = ends_ref.shape[1] // (2 * keys)
+    width = ends_s.shape[2]
+    height = ends_s.shape[1] // (2 * keys)
+    pairs = first_ref.shape[0]
     weight_part(side_ref.at[core, copy], both_ref.at[core], mine_ref)
+    bias_out, gate = output_vectors(vectors_ref, width)
+    last = slice((LAYERS - 1) * pairs, LAYERS * pairs)
+    paired = jnp.concatenate([side_ref[0, side, last, :] for side in range(2)], axis=1)
+    result = layer_result(paired, both_ref.at[1, last], wout_ref, gate, bias_out)
+    grads = layer_grads(first_ref[...], both_ref.at[0, :pairs], win_ref, gate)
+    for t, layer, joined in ((0, LAYERS - 1, result), (1, 0, grads)):
+        lower = [b for b in range(2 * keys) if not b >> layer & 1]
+        upper = [b for b in range(2 * keys) if b >> layer & 1]
+        for b, block in enumerate(layer_blocks(joined, lower, upper, height, width)):
+            ends_s[t, b * height : (b + 1) * height, :] = block
     for key in range(keys):
         start = 0
         rows = pl.ds(pl.multiple_of((copy * keys + key) * height, height), height)
         for t in range(2):
             for k in range(width // LANES):
-                tail_ref[key, start : start + height, :] = ends_ref[
+                tail_ref[key, start : start + height, :] = ends_s[
                     t, rows, k * LANES : (k + 1) * LANES
                 ]
                 start += height
@@ -308,7 +322,7 @@
 
 
 def rows_kernel(
-    start, scaling, got_ref, gate_ref, final_ref, grad_ref, pre_ref, gain_ref, mix_ref, gout_ref
+    start, scaling, got_ref, vectors_ref, final_ref, grad_ref, pre_ref, gain_ref, mix_ref, gout_ref
 ):
     keys = got_ref.shape[0]
     own = final_ref.shape[0] // keys
@@ -323,7 +337,10 @@
     for key in range(1, keys):
         small = small + join_small(got_ref[key, start:, :])
     small = small * scaling
-    gate = 1.0 / (1.0 + jnp.exp(-gate_ref[...]))
+    count = gout_ref.shape[0]
+    begin = vectors_ref.shape[1] - count * LANES
+    logit = [vectors_ref[:, begin + k * LANES : begin + (k + 1) * LANES] for k in range(count)]
+    gate = 1.0 / (1.0 + jnp.exp(-jnp.concatenate(logit, axis=0)))
     first = 0
     for out_ref in (pre_ref, gain_ref, mix_ref, gout_ref):
         count = out_ref.shape[0]
@@ -405,10 +422,10 @@
             jax.ShapeDtypeStruct((width * hid // LANES + 2 * small_rows, LANES), BF16),
             jax.ShapeDtypeStruct((2, LAYERS * pairs, hid), BF16),
             jax.ShapeDtypeStruct((2, 2, LAYERS * pairs, width), BF16),
-            jax.ShapeDtypeStruct((2, 2 * pairs, width), BF16),
+            jax.ShapeDtypeStruct((pairs, 2 * width), BF16),
             jax.ShapeDtypeStruct((small_rows, LANES), F32),
         ],
-        in_specs=[VMEM] * 7,
+        in_specs=[VMEM] * 4,
         out_specs=[VMEM] * 5,
         scratch_shapes=[
             pltpu.VMEM((pairs, hid), F32),
@@ -432,7 +449,8 @@
     keys = 2 ** len(key_bits)
     own = rows_dev // keys
 
-    kept = (weight_in, bias_in[None], norm_gain[None], weight_out, bias_out[None], gate_logit[None])
+    vectors = jnp.concatenate([bias_in, norm_gain, bias_out, gate_logit])[None]
+    kept = (weight_in, weight_out, vectors)
     kept = pl.pallas_call(
         keep_kernel,
         out_shape=[jax.ShapeDtypeStruct(k.shape, k.dtype) for k in kept],
@@ -444,7 +462,7 @@
     both = jnp.concatenate([tokens, cotangent], axis=-1).reshape(keys, own, 2 * width)
     rows = exchange(jnp.concatenate([both, both], axis=0), devices, top_bits)
 
-    sent, both_sides, sides, ends, small = compute(rows, kept)
+    sent, both_sides, sides, first, small = compute(rows, kept)
     received = send(sent, devices, 1)
     mine, tail = pl.pallas_call(
         own_kernel,
@@ -452,11 +470,12 @@
             jax.ShapeDtypeStruct((width * hid // LANES, LANES), F32),
             jax.ShapeDtypeStruct((keys, 2 * own * width // LANES, LANES), BF16),
         ],
-        in_specs=[VMEM] * 3,
+        in_specs=[VMEM] * 6,
         out_specs=[VMEM] * 2,
-        compiler_params=PARAMS,
+        scratch_shapes=[pltpu.VMEM((2, 2 * keys * own, width), BF16)],
+        compiler_params=WIDE,
         name="own_part",
-    )(both_sides, sides, ends)
+    )(both_sides, sides, first, *kept)
     message = pl.pallas_call(
         core_kernel,
         out_shape=jax.ShapeDtypeStruct(
@@ -489,7 +508,7 @@
         out_specs=[VMEM] * 6,
         compiler_params=PARAMS,
         name="rows_out",
-    )(got, kept[5].reshape(-1, LANES))
+    )(got, kept[2])
     if rest:
         owned, *small = lax.psum(
             (owned, *small), "seq", axis_index_groups=bit_groups(devices, rest)

time: 70.5 us -> 69.8 us (0.990)
  local copies, waits for them, and re-layouts: 5.18 us -> 2.45 us
  waiting for transfers between devices: 11.5 us -> 12.8 us
  other arithmetic: 1.6 us -> 2.35 us
    unnamed x12 -> x4, local copies, waits for them, and re-layouts: 5.18 us -> 2.45 us
    all_to_all x1, waiting for transfers between devices: 4.54 us -> 6.53 us  [exchange(): return lax.all_to_all(value, 'seq', 0, 0, axis_index_groups=groups)]
    concatenate x0 -> x1, other arithmetic: none -> 0.75 us  [per_device(): vectors = jnp.concatenate([bias_in, norm_gain, bias_out, gate_logit])[None]]
    ppermute x3, waiting for transfers between devices: 7.01 us -> 6.3 us  [send(): return lax.ppermute(value, 'seq', [(i, i ^ mask) for i in range(devices)])]
    pallas_call x1, Pallas kernels: 0.5 us -> 1.21 us  [per_device(): pl.pallas_call(own_kernel, out_shape=[jax.ShapeDtypeStruct((width * hid /...]
  transfers between devices with their start and end apart: 4 -> 4, of which waited for: 4 -> 4; matrix products, arithmetic and copies ran while one was open for 0% -> 1% of each run, Pallas kernels for 3% -> 5%
where the time goes in v6:
time: 69.8 us; the launch traced here: 69.4 us
  blocking collectives  30.3 us (43%)
  waiting for transfers between devices  12.8 us (18%)
  Pallas kernels  11.3 us (16%)
  starting transfers between devices  9.55 us (14%)
  local copies, waits for them, and re-layouts  2.45 us (4%)
  other arithmetic  2.35 us (3%)
  between operations  0.7 us (1%)
    all_to_all x2, blocking collectives, exchange(): return lax.all_to_all(value, 'seq', 0, 0, axis_index_groups=groups)  30.3 us
    all_to_all x1, starting transfers between devices, exchange(): return lax.all_to_all(value, 'seq', 0, 0, axis_index_groups=groups)  8.31 us
    pallas_call x1, Pallas kernels, compute(): pl.pallas_call(switch_kernel, out_shape=[jax.ShapeDtypeStruct((width * hi...  6.8 us
    all_to_all x1, waiting for transfers between devices, exchange(): return lax.all_to_all(value, 'seq', 0, 0, axis_index_groups=groups)  6.53 us
    ppermute x3, waiting for transfers between devices, send(): return lax.ppermute(value, 'seq', [(i, i ^ mask) for i in range(devices)])  6.3 us
    unnamed x4, local copies, waits for them, and re-layouts  2.45 us
  transfers between devices with their start and end apart: 4, of which 4 were waited for; matrix products, arithmetic and copies ran while one was open for 1% of the time, Pallas kernels for 5%

profile of v6, /device:TPU:0, one launch (start us, length us, event | category | flops | bytes accessed | tf_op | source)
XLA Modules:
  0.0 69.4 jit_solution(16106221814548019649)
XLA Ops:
  0.6 0.9 %pad_maximum_fusion.1 = bf16[128,512]{1,0:T(8,128)(2,1)S(1)} fusion(bf16[128,256]{1,0:T(8,128)(2,1)} %param.9, bf16[128,256]{1,0:T(8,128)(2,1)} %param.8), kind=kLoop, calls=%fused_computation.1 | loop fusion | flops 262144 | bytes 262144 | tf_op jit(solution)/shard_map/concatenate | solution.py:462
  1.5 0.7 %pad_maximum_fusion = bf16[16,16,512]{2,1,0:T(8,128)(2,1)} fusion(bf16[8,16,512]{2,1,0:T(8,128)(2,1)S(1)} %bitcast.11), kind=kLoop, calls=%fused_computation | loop fusion | flops 131072 | bytes 393216 | tf_op jit(solution)/shard_map/concatenate | solution.py:463
  2.2 8.3 %all-to-all-start = ((bf16[16,16,512]{2,1,0:T(8,128)(2,1)}), bf16[16,16,512]{2,1,0:T(8,128)(2,1)S(1)}, u32[]{:S(2)}, u32[]{:S(2)}) async-start(bf16[16,16,512]{2,1,0:T(8,128)(2,1)} %pad_maximum_fusion), calls=%async_computation | async-start | bytes 524288 | tf_op jit(solution)/shard_map/all_to_all | solution.py:400
  10.6 0.7 %pad_maximum_fusion.2 = f32[3072]{0:T(1024)S(1)} fusion(f32[512]{0:T(512)} %param.15, f32[512]{0:T(512)} %param.14, f32[1024]{0:T(1024)} %param.12, f32[1024]{0:T(1024)} %param.11), kind=kLoop, calls=%fused_computation.2 | loop fusion | flops 9216 | bytes 24576 | tf_op jit(solution)/shard_map/concatenate | solution.py:452
  11.3 0.0 copy-start
  11.3 1.2 %copy-done = bf16[512,1024]{1,0:T(8,128)(2,1)S(1)} copy-done((bf16[512,1024]{1,0:T(8,128)(2,1)S(1)}, bf16[512,1024]{1,0:T(8,128)(2,1)}, u32[]{:S(2)}) %copy-start) | copy-done | bytes 1048600
  12.5 0.0 copy-start.1
  12.5 1.2 %copy-done.1 = bf16[512,1024]{1,0:T(8,128)(2,1)S(1)} copy-done((bf16[512,1024]{1,0:T(8,128)(2,1)S(1)}, bf16[512,1024]{1,0:T(8,128)(2,1)}, u32[]{:S(2)}) %copy-start.1) | copy-done | bytes 1048600
  13.8 0.1 keep_weights.1
  13.9 6.5 %all-to-all-done.rows_ref = bf16[16,16,512]{2,1,0:T(8,128)(2,1)S(1)} async-done(((bf16[16,16,512]{2,1,0:T(8,128)(2,1)}), bf16[16,16,512]{2,1,0:T(8,128)(2,1)S(1)}, u32[]{:S(2)}, u32[]{:S(2)}) %all-to-all-start) | async-done | bytes 262176 | tf_op jit(solution)/shard_map/all_to_all | solution.py:400
  20.4 6.8 %switch_layers.1 = (bf16[2096,128]{1,0:T(8,128)(2,1)S(1)}, bf16[2,512,1024]{2,1,0:T(8,128)(2,1)S(1)}, bf16[2,2,512,256]{3,2,1,0:T(8,128)(2,1)S(1)}, bf16[128,512]{1,0:T(8,128)(2,1)S(1)}, f32[24,128]{1,0:T(8,128)S(1)}) custom-call(bf16[16,16,512]{2,1,0:T(8,128)(2,1)S(1)} %all-to-all-done.rows_ref, bf16[512,1024]{1,0:T(8,128)(2,1)S(1)} %get-tuple-element.28.win_ref, ...), custom_call_target="tpu_custom_call" | custom-call | tf_op jit(solution)/shard_map/switch_layers/pallas_call | solution.py:419
  27.2 0.1 collective-permute-start
  27.3 1.2 %own_part.1 = (f32[2048,128]{1,0:T(8,128)S(1)}, bf16[8,64,128]{2,1,0:T(8,128)(2,1)S(1)}) custom-call(bf16[2,512,1024]{2,1,0:T(8,128)(2,1)S(1)} %get-tuple-element.31.both_ref, bf16[2,2,512,256]{3,2,1,0:T(8,128)(2,1)S(1)} %get-tuple-element.32.side_ref, bf16[128,512]{1,0:T(8,128)(2,1)S(1)} %get-tuple-element.33.first_ref, ...), custom_call_target="tpu_custom_call" | custom-call | tf_op jit(solution)/shard_map/own_part/pallas_call | solution.py:467
  28.5 0.7 %collective-permute-done.other_ref = bf16[2096,128]{1,0:T(8,128)(2,1)S(1)} collective-permute-done((bf16[2096,128]{1,0:T(8,128)(2,1)S(1)}, bf16[2096,128]{1,0:T(8,128)(2,1)S(1)}, u32[]{:S(2)}, u32[]{:S(2)}) %collective-permute-start) | collective-permute-done | bytes 536608 | tf_op jit(solution)/shard_map/ppermute | solution.py:404
  29.2 0.1 core_sum.1
  29.3 14.9 %all_to_all.15.got_ref = bf16[8,368,128]{2,1,0:T(8,128)(2,1)S(1)} all-to-all(bf16[8,368,128]{2,1,0:T(8,128)(2,1)S(1)} %core_sum.1), channel_id=1, replica_groups={{0,2,4,6,8,10,12,14},{1,3,5,7,9,11,13,15},{16,18,20,22,24,26,28,30},{17..., dimensions={0} | all-to-all | bytes 1507328 | tf_op jit(solution)/shard_map/all_to_all | solution.py:400
  44.2 0.1 slice_sum.1.slice_ref
  44.3 1.2 %collective-permute-start.1 = (bf16[32,1024]{1,0:T(8,128)(2,1)S(1)}, bf16[32,1024]{1,0:T(8,128)(2,1)S(1)}, u32[]{:S(2)}, u32[]{:S(2)}) collective-permute-start(bf16[32,1024]{1,0:T(8,128)(2,1)S(1)} %slice_sum.1.slice_ref), channel_id=1, source_target_pairs={{0,16},{1,17},{2,18},{3,19},{4,20},{5,21},{6,22},{7,23},{8,24},{9,... | collective-permute-start | bytes 196616 | tf_op jit(solution)/shard_map/ppermute | solution.py:404
  45.5 4.7 %collective-permute-done.1.slice_ref = bf16[32,1024]{1,0:T(8,128)(2,1)S(1)} collective-permute-done((bf16[32,1024]{1,0:T(8,128)(2,1)S(1)}, bf16[32,1024]{1,0:T(8,128)(2,1)S(1)}, u32[]{:S(2)}, u32[]{:S(2)}) %collective-permute-start.1) | collective-permute-done | bytes 65568 | tf_op jit(solution)/shard_map/ppermute | solution.py:404
  50.3 15.3 %all_to_all.16.mine_ref = bf16[8,2,32,1024]{3,2,1,0:T(8,128)(2,1)S(1)} all-to-all(bf16[8,2,32,1024]{3,2,1,0:T(8,128)(2,1)S(1)} %spread_twin.1), channel_id=1, replica_groups={{0,2,4,6,8,10,12,14},{1,3,5,7,9,11,13,15},{16,18,20,22,24,26,28,30},{17..., dimensions={0} | all-to-all | bytes 2097152 | tf_op jit(solution)/shard_map/all_to_all | solution.py:400
  65.7 0.0 collective-permute-start.2
  65.7 0.7 rows_out.1
  66.3 1.1 %mine_out.1 = (bf16[2,8,32,1024]{3,2,1,0:T(8,128)(2,1)}, bf16[2,8,32,1024]{3,2,1,0:T(8,128)(2,1)}) custom-call(bf16[8,2,32,1024]{3,2,1,0:T(8,128)(2,1)S(1)} %all_to_all.16.mine_ref), custom_call_target="tpu_custom_call" | custom-call | tf_op jit(solution)/shard_map/mine_out/pallas_call | solution.py:540
  67.4 0.9 %collective-permute-done.2.other_ref = bf16[8,2,32,1024]{3,2,1,0:T(8,128)(2,1)S(1)} collective-permute-done((bf16[8,2,32,1024]{3,2,1,0:T(8,128)(2,1)S(1)}, bf16[8,2,32,1024]{3,2,1,0:T(8,128)(2,1)S(1)}, u32[]{:S(2)}, u32[]{:S(2)}) %collective-permute-start.2) | collective-permute-done | bytes 1048608 | tf_op jit(solution)/shard_map/ppermute | solution.py:404
  68.3 1.1 %other_out.1 = (bf16[2,8,32,1024]{3,2,1,0:T(8,128)(2,1)}, bf16[2,8,32,1024]{3,2,1,0:T(8,128)(2,1)}) custom-call(bf16[8,2,32,1024]{3,2,1,0:T(8,128)(2,1)S(1)} %collective-permute-done.2.other_ref, bf16[2,8,32,1024]{3,2,1,0:T(8,128)(2,1)} %get-tuple-element.40.first_in, ...), custom_call_target="tpu_custom_call", output_to_operand_aliasing={{0}: (1, {}), {1}: (2, {})} | custom-call | tf_op jit(solution)/shard_map/other_out/pallas_call | solution.py:549
  (2 shorter events, 0.1 us)
Async XLA Ops:
  2.2 18.2 %all-to-all-start = ((bf16[16,16,512]{2,1,0:T(8,128)(2,1)}), bf16[16,16,512]{2,1,0:T(8,128)(2,1)S(1)}, u32[]{:S(2)}, u32[]{:S(2)}) async-start(bf16[16,16,512]{2,1,0:T(8,128)(2,1)} %pad_maximum_fusion), calls=%async_computation | async-start | bytes 524288 | tf_op jit(solution)/shard_map/all_to_all | solution.py:400
  11.3 1.2 %copy-start = (bf16[512,1024]{1,0:T(8,128)(2,1)S(1)}, bf16[512,1024]{1,0:T(8,128)(2,1)}, u32[]{:S(2)}) copy-start(bf16[512,1024]{1,0:T(8,128)(2,1)} %refs_0_.1) | copy-start | bytes 3145732
  12.5 1.2 %copy-start.1 = (bf16[512,1024]{1,0:T(8,128)(2,1)S(1)}, bf16[512,1024]{1,0:T(8,128)(2,1)}, u32[]{:S(2)}) copy-start(bf16[512,1024]{1,0:T(8,128)(2,1)} %refs_1_.1) | copy-start | bytes 3145732
  27.2 2.0 %collective-permute-start = (bf16[2096,128]{1,0:T(8,128)(2,1)S(1)}, bf16[2096,128]{1,0:T(8,128)(2,1)S(1)}, u32[]{:S(2)}, u32[]{:S(2)}) collective-permute-start(bf16[2096,128]{1,0:T(8,128)(2,1)S(1)} %get-tuple-element.37), channel_id=1, source_target_pairs={{0,1},{1,0},{2,3},{3,2},{4,5},{5,4},{6,7},{7,6},{8,9},{9,8},{10,11... | collective-permute-start | bytes 1609736 | tf_op jit(solution)/shard_map/ppermute | solution.py:404
  44.3 5.9 %collective-permute-start.1 = (bf16[32,1024]{1,0:T(8,128)(2,1)S(1)}, bf16[32,1024]{1,0:T(8,128)(2,1)S(1)}, u32[]{:S(2)}, u32[]{:S(2)}) collective-permute-start(bf16[32,1024]{1,0:T(8,128)(2,1)S(1)} %slice_sum.1.slice_ref), channel_id=1, source_target_pairs={{0,16},{1,17},{2,18},{3,19},{4,20},{5,21},{6,22},{7,23},{8,24},{9,... | collective-permute-start | bytes 196616 | tf_op jit(solution)/shard_map/ppermute | solution.py:404
  65.7 2.7 %collective-permute-start.2 = (bf16[8,2,32,1024]{3,2,1,0:T(8,128)(2,1)S(1)}, bf16[8,2,32,1024]{3,2,1,0:T(8,128)(2,1)S(1)}, u32[]{:S(2)}, u32[]{:S(2)}) collective-permute-start(bf16[8,2,32,1024]{3,2,1,0:T(8,128)(2,1)S(1)} %all_to_all.16.mine_ref), channel_id=1, source_target_pairs={{0,1},{1,0},{2,3},{3,2},{4,5},{5,4},{6,7},{7,6},{8,9},{9,8},{10,11... | collective-permute-start | bytes 3145736 | tf_op jit(solution)/shard_map/ppermute | solution.py:404

commit v7 on v6

--- a/solution.py
+++ b/solution.py
@@ -19,6 +19,10 @@
 
 BF16 = jnp.bfloat16
 F32 = jnp.float32
+
+
+def slot_order(count):
+    return [j // 2 if j % 2 == 0 else count - 1 - j // 2 for j in range(count)]
 
 
 def split_small(total):
@@ -304,11 +308,11 @@
     slab = mine_ref.shape[0] // keys
     small = join_small(split_small(small_ref[...])) + join_small(other_ref[keys * slab :, :])
     packed = split_small(small)
-    for key in range(keys):
+    for slot, key in enumerate(slot_order(keys)):
         here = slice(key * slab, (key + 1) * slab)
-        msg_ref[key, :slab, :] = (mine_ref[here, :] + other_ref[here, :].astype(F32)).astype(BF16)
-        msg_ref[key, slab : slab + tail, :] = tail_ref[key]
-        msg_ref[key, slab + tail :, :] = packed
+        msg_ref[slot, :slab, :] = (mine_ref[here, :] + other_ref[here, :].astype(F32)).astype(BF16)
+        msg_ref[slot, slab : slab + tail, :] = tail_ref[key]
+        msg_ref[slot, slab + tail :, :] = packed
 
 
 def slice_kernel(scaling, got_ref, slice_ref):
@@ -328,9 +332,9 @@
     own = final_ref.shape[0] // keys
     for out_ref in (final_ref, grad_ref):
         for k in range(final_ref.shape[1] // LANES):
-            for key in range(keys):
+            for slot, key in enumerate(slot_order(keys)):
                 out_ref[key * own : (key + 1) * own, k * LANES : (k + 1) * LANES] = got_ref[
-                    key, start : start + own, :
+                    slot, start : start + own, :
                 ]
             start += own
     small = join_small(got_ref[0, start:, :])
@@ -362,9 +366,9 @@
     keys, copies = source_ref.shape[:2]
     moves = [
         pltpu.make_async_copy(
-            source_ref.at[key, copy], target_ref.at[copy, key], sems.at[copies * key + copy]
+            source_ref.at[slot, copy], target_ref.at[copy, key], sems.at[copies * key + copy]
         )
-        for key in range(keys)
+        for slot, key in enumerate(slot_order(keys))
         for copy in range(copies)
     ]
     for move in moves:
@@ -395,8 +399,7 @@
     return [[base | m for m in masks] for base in range(devices) if not base & every]
 
 
-def exchange(value, devices, bits):
-    groups = None if 2 ** len(bits) == devices else bit_groups(devices, bits)
+def exchange(value, groups):
     return lax.all_to_all(value, "seq", 0, 0, axis_index_groups=groups)
 
 
@@ -460,7 +463,7 @@
         name="keep_weights",
     )(*kept)
     both = jnp.concatenate([tokens, cotangent], axis=-1).reshape(keys, own, 2 * width)
-    rows = exchange(jnp.concatenate([both, both], axis=0), devices, top_bits)
+    rows = exchange(jnp.concatenate([both, both], axis=0), bit_groups(devices, top_bits))
 
     sent, both_sides, sides, first, small = compute(rows, kept)
     received = send(sent, devices, 1)
@@ -487,7 +490,10 @@
         name="core_sum",
     )(mine, tail, small, received)
     share = width // keys
-    got = exchange(message, devices, key_bits)
+    key_groups = [
+        [group[key] for key in slot_order(keys)] for group in bit_groups(devices, key_bits)
+    ]
+    got = exchange(message, key_groups)
     scaling = float(rows_dev * devices // 2) ** (-0.5)
     rest = list(range(1, top_bit - LAYERS))
     rows_shape = jax.ShapeDtypeStruct((rows_dev, width), BF16)
@@ -534,7 +540,7 @@
         compiler_params=PARAMS,
         name="spread_twin",
     )(twin, spread)
-    whole = exchange(spread, devices, key_bits)
+    whole = exchange(spread, key_groups)
     other = send(whole, devices, 1)
     ordered = jax.ShapeDtypeStruct((2, keys, share, hid), BF16)
     weights = pl.pallas_call(

time: 69.8 us -> 69.3 us (level)
  waiting for transfers between devices: 12.8 us -> 12.1 us
    ppermute x3, waiting for transfers between devices: 6.3 us -> 5.59 us  [send(): return lax.ppermute(value, 'seq', [(i, i ^ mask) for i in range(devices)])]
where the time goes in v7:
time: 69.3 us; the launch traced here: 68.8 us
  blocking collectives  30.4 us (44%)
  waiting for transfers between devices  12.1 us (17%)
  Pallas kernels  11.3 us (16%)
  starting transfers between devices  9.55 us (14%)
  local copies, waits for them, and re-layouts  2.45 us (4%)
  other arithmetic  2.35 us (3%)
  between operations  0.7 us (1%)
    all_to_all x2, blocking collectives, exchange(): return lax.all_to_all(value, 'seq', 0, 0, axis_index_groups=groups)  30.4 us
    all_to_all x1, starting transfers between devices, exchange(): return lax.all_to_all(value, 'seq', 0, 0, axis_index_groups=groups)  8.31 us
    pallas_call x1, Pallas kernels, compute(): pl.pallas_call(switch_kernel, out_shape=[jax.ShapeDtypeStruct((width * hi...  6.8 us
    all_to_all x1, waiting for transfers between devices, exchange(): return lax.all_to_all(value, 'seq', 0, 0, axis_index_groups=groups)  6.53 us
    ppermute x3, waiting for transfers between devices, send(): return lax.ppermute(value, 'seq', [(i, i ^ mask) for i in range(devices)])  5.59 us
    unnamed x4, local copies, waits for them, and re-layouts  2.45 us
  transfers between devices with their start and end apart: 4, of which 4 were waited for; matrix products, arithmetic and copies ran while one was open for 1% of the time, Pallas kernels for 5%

profile of v7, /device:TPU:0, one launch (start us, length us, event | category | flops | bytes accessed | tf_op | source)
XLA Modules:
  0.0 68.8 jit_solution(6756870972111695087)
XLA Ops:
  0.6 0.9 %pad_maximum_fusion.1 = bf16[128,512]{1,0:T(8,128)(2,1)S(1)} fusion(bf16[128,256]{1,0:T(8,128)(2,1)} %param.9, bf16[128,256]{1,0:T(8,128)(2,1)} %param.8), kind=kLoop, calls=%fused_computation.1 | loop fusion | flops 262144 | bytes 262144 | tf_op jit(solution)/shard_map/concatenate | solution.py:465
  1.5 0.7 %pad_maximum_fusion = bf16[16,16,512]{2,1,0:T(8,128)(2,1)} fusion(bf16[8,16,512]{2,1,0:T(8,128)(2,1)S(1)} %bitcast.11), kind=kLoop, calls=%fused_computation | loop fusion | flops 131072 | bytes 393216 | tf_op jit(solution)/shard_map/concatenate | solution.py:466
  2.2 8.3 %all-to-all-start = ((bf16[16,16,512]{2,1,0:T(8,128)(2,1)}), bf16[16,16,512]{2,1,0:T(8,128)(2,1)S(1)}, u32[]{:S(2)}, u32[]{:S(2)}) async-start(bf16[16,16,512]{2,1,0:T(8,128)(2,1)} %pad_maximum_fusion), calls=%async_computation | async-start | bytes 524288 | tf_op jit(solution)/shard_map/all_to_all | solution.py:403
  10.6 0.7 %pad_maximum_fusion.2 = f32[3072]{0:T(1024)S(1)} fusion(f32[512]{0:T(512)} %param.15, f32[512]{0:T(512)} %param.14, f32[1024]{0:T(1024)} %param.12, f32[1024]{0:T(1024)} %param.11), kind=kLoop, calls=%fused_computation.2 | loop fusion | flops 9216 | bytes 24576 | tf_op jit(solution)/shard_map/concatenate | solution.py:455
  11.3 0.0 copy-start
  11.3 1.2 %copy-done = bf16[512,1024]{1,0:T(8,128)(2,1)S(1)} copy-done((bf16[512,1024]{1,0:T(8,128)(2,1)S(1)}, bf16[512,1024]{1,0:T(8,128)(2,1)}, u32[]{:S(2)}) %copy-start) | copy-done | bytes 1048600
  12.5 0.0 copy-start.1
  12.5 1.2 %copy-done.1 = bf16[512,1024]{1,0:T(8,128)(2,1)S(1)} copy-done((bf16[512,1024]{1,0:T(8,128)(2,1)S(1)}, bf16[512,1024]{1,0:T(8,128)(2,1)}, u32[]{:S(2)}) %copy-start.1) | copy-done | bytes 1048600
  13.8 0.1 keep_weights.1
  13.9 6.5 %all-to-all-done.rows_ref = bf16[16,16,512]{2,1,0:T(8,128)(2,1)S(1)} async-done(((bf16[16,16,512]{2,1,0:T(8,128)(2,1)}), bf16[16,16,512]{2,1,0:T(8,128)(2,1)S(1)}, u32[]{:S(2)}, u32[]{:S(2)}) %all-to-all-start) | async-done | bytes 262176 | tf_op jit(solution)/shard_map/all_to_all | solution.py:403
  20.4 6.8 %switch_layers.1 = (bf16[2096,128]{1,0:T(8,128)(2,1)S(1)}, bf16[2,512,1024]{2,1,0:T(8,128)(2,1)S(1)}, bf16[2,2,512,256]{3,2,1,0:T(8,128)(2,1)S(1)}, bf16[128,512]{1,0:T(8,128)(2,1)S(1)}, f32[24,128]{1,0:T(8,128)S(1)}) custom-call(bf16[16,16,512]{2,1,0:T(8,128)(2,1)S(1)} %all-to-all-done.rows_ref, bf16[512,1024]{1,0:T(8,128)(2,1)S(1)} %get-tuple-element.28.win_ref, ...), custom_call_target="tpu_custom_call" | custom-call | tf_op jit(solution)/shard_map/switch_layers/pallas_call | solution.py:422
  27.2 0.1 collective-permute-start
  27.3 1.2 %own_part.1 = (f32[2048,128]{1,0:T(8,128)S(1)}, bf16[8,64,128]{2,1,0:T(8,128)(2,1)S(1)}) custom-call(bf16[2,512,1024]{2,1,0:T(8,128)(2,1)S(1)} %get-tuple-element.31.both_ref, bf16[2,2,512,256]{3,2,1,0:T(8,128)(2,1)S(1)} %get-tuple-element.32.side_ref, bf16[128,512]{1,0:T(8,128)(2,1)S(1)} %get-tuple-element.33.first_ref, ...), custom_call_target="tpu_custom_call" | custom-call | tf_op jit(solution)/shard_map/own_part/pallas_call | solution.py:470
  28.5 0.7 %collective-permute-done.other_ref = bf16[2096,128]{1,0:T(8,128)(2,1)S(1)} collective-permute-done((bf16[2096,128]{1,0:T(8,128)(2,1)S(1)}, bf16[2096,128]{1,0:T(8,128)(2,1)S(1)}, u32[]{:S(2)}, u32[]{:S(2)}) %collective-permute-start) | collective-permute-done | bytes 536608 | tf_op jit(solution)/shard_map/ppermute | solution.py:407
  29.2 0.1 core_sum.1
  29.3 14.3 %all_to_all.15.got_ref = bf16[8,368,128]{2,1,0:T(8,128)(2,1)S(1)} all-to-all(bf16[8,368,128]{2,1,0:T(8,128)(2,1)S(1)} %core_sum.1), channel_id=1, replica_groups={{0,14,2,12,4,10,6,8},{1,15,3,13,5,11,7,9},{16,30,18,28,20,26,22,24},{17..., dimensions={0} | all-to-all | bytes 1507328 | tf_op jit(solution)/shard_map/all_to_all | solution.py:403
  43.7 0.1 slice_sum.1.slice_ref
  43.7 1.2 %collective-permute-start.1 = (bf16[32,1024]{1,0:T(8,128)(2,1)S(1)}, bf16[32,1024]{1,0:T(8,128)(2,1)S(1)}, u32[]{:S(2)}, u32[]{:S(2)}) collective-permute-start(bf16[32,1024]{1,0:T(8,128)(2,1)S(1)} %slice_sum.1.slice_ref), channel_id=1, source_target_pairs={{0,16},{1,17},{2,18},{3,19},{4,20},{5,21},{6,22},{7,23},{8,24},{9,... | collective-permute-start | bytes 196616 | tf_op jit(solution)/shard_map/ppermute | solution.py:407
  44.9 4.0 %collective-permute-done.1.slice_ref = bf16[32,1024]{1,0:T(8,128)(2,1)S(1)} collective-permute-done((bf16[32,1024]{1,0:T(8,128)(2,1)S(1)}, bf16[32,1024]{1,0:T(8,128)(2,1)S(1)}, u32[]{:S(2)}, u32[]{:S(2)}) %collective-permute-start.1) | collective-permute-done | bytes 65568 | tf_op jit(solution)/shard_map/ppermute | solution.py:407
  49.0 16.1 %all_to_all.16.mine_ref = bf16[8,2,32,1024]{3,2,1,0:T(8,128)(2,1)S(1)} all-to-all(bf16[8,2,32,1024]{3,2,1,0:T(8,128)(2,1)S(1)} %spread_twin.1), channel_id=1, replica_groups={{0,14,2,12,4,10,6,8},{1,15,3,13,5,11,7,9},{16,30,18,28,20,26,22,24},{17..., dimensions={0} | all-to-all | bytes 2097152 | tf_op jit(solution)/shard_map/all_to_all | solution.py:403
  65.1 0.0 collective-permute-start.2
  65.1 0.7 rows_out.1
  65.8 1.1 %mine_out.1 = (bf16[2,8,32,1024]{3,2,1,0:T(8,128)(2,1)}, bf16[2,8,32,1024]{3,2,1,0:T(8,128)(2,1)}) custom-call(bf16[8,2,32,1024]{3,2,1,0:T(8,128)(2,1)S(1)} %all_to_all.16.mine_ref), custom_call_target="tpu_custom_call" | custom-call | tf_op jit(solution)/shard_map/mine_out/pallas_call | solution.py:546
  66.9 0.9 %collective-permute-done.2.other_ref = bf16[8,2,32,1024]{3,2,1,0:T(8,128)(2,1)S(1)} collective-permute-done((bf16[8,2,32,1024]{3,2,1,0:T(8,128)(2,1)S(1)}, bf16[8,2,32,1024]{3,2,1,0:T(8,128)(2,1)S(1)}, u32[]{:S(2)}, u32[]{:S(2)}) %collective-permute-start.2) | collective-permute-done | bytes 1048608 | tf_op jit(solution)/shard_map/ppermute | solution.py:407
  67.8 1.1 %other_out.1 = (bf16[2,8,32,1024]{3,2,1,0:T(8,128)(2,1)}, bf16[2,8,32,1024]{3,2,1,0:T(8,128)(2,1)}) custom-call(bf16[8,2,32,1024]{3,2,1,0:T(8,128)(2,1)S(1)} %collective-permute-done.2.other_ref, bf16[2,8,32,1024]{3,2,1,0:T(8,128)(2,1)} %get-tuple-element.40.first_in, ...), custom_call_target="tpu_custom_call", output_to_operand_aliasing={{0}: (1, {}), {1}: (2, {})} | custom-call | tf_op jit(solution)/shard_map/other_out/pallas_call | solution.py:555
  (2 shorter events, 0.1 us)
Async XLA Ops:
  2.2 18.2 %all-to-all-start = ((bf16[16,16,512]{2,1,0:T(8,128)(2,1)}), bf16[16,16,512]{2,1,0:T(8,128)(2,1)S(1)}, u32[]{:S(2)}, u32[]{:S(2)}) async-start(bf16[16,16,512]{2,1,0:T(8,128)(2,1)} %pad_maximum_fusion), calls=%async_computation | async-start | bytes 524288 | tf_op jit(solution)/shard_map/all_to_all | solution.py:403
  11.3 1.2 %copy-start = (bf16[512,1024]{1,0:T(8,128)(2,1)S(1)}, bf16[512,1024]{1,0:T(8,128)(2,1)}, u32[]{:S(2)}) copy-start(bf16[512,1024]{1,0:T(8,128)(2,1)} %refs_0_.1) | copy-start | bytes 3145732
  12.5 1.2 %copy-start.1 = (bf16[512,1024]{1,0:T(8,128)(2,1)S(1)}, bf16[512,1024]{1,0:T(8,128)(2,1)}, u32[]{:S(2)}) copy-start(bf16[512,1024]{1,0:T(8,128)(2,1)} %refs_1_.1) | copy-start | bytes 3145732
  27.2 2.0 %collective-permute-start = (bf16[2096,128]{1,0:T(8,128)(2,1)S(1)}, bf16[2096,128]{1,0:T(8,128)(2,1)S(1)}, u32[]{:S(2)}, u32[]{:S(2)}) collective-permute-start(bf16[2096,128]{1,0:T(8,128)(2,1)S(1)} %get-tuple-element.37), channel_id=1, source_target_pairs={{0,1},{1,0},{2,3},{3,2},{4,5},{5,4},{6,7},{7,6},{8,9},{9,8},{10,11... | collective-permute-start | bytes 1609736 | tf_op jit(solution)/shard_map/ppermute | solution.py:407
  43.7 5.2 %collective-permute-start.1 = (bf16[32,1024]{1,0:T(8,128)(2,1)S(1)}, bf16[32,1024]{1,0:T(8,128)(2,1)S(1)}, u32[]{:S(2)}, u32[]{:S(2)}) collective-permute-start(bf16[32,1024]{1,0:T(8,128)(2,1)S(1)} %slice_sum.1.slice_ref), channel_id=1, source_target_pairs={{0,16},{1,17},{2,18},{3,19},{4,20},{5,21},{6,22},{7,23},{8,24},{9,... | collective-permute-start | bytes 196616 | tf_op jit(solution)/shard_map/ppermute | solution.py:407
  65.1 2.7 %collective-permute-start.2 = (bf16[8,2,32,1024]{3,2,1,0:T(8,128)(2,1)S(1)}, bf16[8,2,32,1024]{3,2,1,0:T(8,128)(2,1)S(1)}, u32[]{:S(2)}, u32[]{:S(2)}) collective-permute-start(bf16[8,2,32,1024]{3,2,1,0:T(8,128)(2,1)S(1)} %all_to_all.16.mine_ref), channel_id=1, source_target_pairs={{0,1},{1,0},{2,3},{3,2},{4,5},{5,4},{6,7},{7,6},{8,9},{9,8},{10,11... | collective-permute-start | bytes 3145736 | tf_op jit(solution)/shard_map/ppermute | solution.py:407

commit v8 on v7

--- a/solution.py
+++ b/solution.py
@@ -366,9 +366,9 @@
     keys, copies = source_ref.shape[:2]
     moves = [
         pltpu.make_async_copy(
-            source_ref.at[slot, copy], target_ref.at[copy, key], sems.at[copies * key + copy]
+            source_ref.at[key, copy], target_ref.at[copy, key], sems.at[copies * key + copy]
         )
-        for slot, key in enumerate(slot_order(keys))
+        for key in range(keys)
         for copy in range(copies)
     ]
     for move in moves:
@@ -540,7 +540,7 @@
         compiler_params=PARAMS,
         name="spread_twin",
     )(twin, spread)
-    whole = exchange(spread, key_groups)
+    whole = exchange(spread, bit_groups(devices, key_bits))
     other = send(whole, devices, 1)
     ordered = jax.ShapeDtypeStruct((2, keys, share, hid), BF16)
     weights = pl.pallas_call(

time: 69.3 us -> 69.8 us (level)
  no operation moved by 1% of the time
where the time goes in v8:
time: 69.8 us; the launch traced here: 69.3 us
  blocking collectives  30.9 us (44%)
  waiting for transfers between devices  12.1 us (17%)
  Pallas kernels  11.3 us (16%)
  starting transfers between devices  9.55 us (14%)
  local copies, waits for them, and re-layouts  2.45 us (4%)
  other arithmetic  2.35 us (3%)
  between operations  0.7 us (1%)
    all_to_all x2, blocking collectives, exchange(): return lax.all_to_all(value, 'seq', 0, 0, axis_index_groups=groups)  30.9 us
    all_to_all x1, starting transfers between devices, exchange(): return lax.all_to_all(value, 'seq', 0, 0, axis_index_groups=groups)  8.31 us
    pallas_call x1, Pallas kernels, compute(): pl.pallas_call(switch_kernel, out_shape=[jax.ShapeDtypeStruct((width * hi...  6.8 us
    all_to_all x1, waiting for transfers between devices, exchange(): return lax.all_to_all(value, 'seq', 0, 0, axis_index_groups=groups)  6.53 us
    ppermute x3, waiting for transfers between devices, send(): return lax.ppermute(value, 'seq', [(i, i ^ mask) for i in range(devices)])  5.59 us
    unnamed x4, local copies, waits for them, and re-layouts  2.45 us
  transfers between devices with their start and end apart: 4, of which 4 were waited for; matrix products, arithmetic and copies ran while one was open for 1% of the time, Pallas kernels for 5%

profile of v8, /device:TPU:0, one launch (start us, length us, event | category | flops | bytes accessed | tf_op | source)
XLA Modules:
  0.0 69.3 jit_solution(7862670972206205649)
XLA Ops:
  0.6 0.9 %pad_maximum_fusion.1 = bf16[128,512]{1,0:T(8,128)(2,1)S(1)} fusion(bf16[128,256]{1,0:T(8,128)(2,1)} %param.9, bf16[128,256]{1,0:T(8,128)(2,1)} %param.8), kind=kLoop, calls=%fused_computation.1 | loop fusion | flops 262144 | bytes 262144 | tf_op jit(solution)/shard_map/concatenate | solution.py:465
  1.5 0.7 %pad_maximum_fusion = bf16[16,16,512]{2,1,0:T(8,128)(2,1)} fusion(bf16[8,16,512]{2,1,0:T(8,128)(2,1)S(1)} %bitcast.11), kind=kLoop, calls=%fused_computation | loop fusion | flops 131072 | bytes 393216 | tf_op jit(solution)/shard_map/concatenate | solution.py:466
  2.2 8.3 %all-to-all-start = ((bf16[16,16,512]{2,1,0:T(8,128)(2,1)}), bf16[16,16,512]{2,1,0:T(8,128)(2,1)S(1)}, u32[]{:S(2)}, u32[]{:S(2)}) async-start(bf16[16,16,512]{2,1,0:T(8,128)(2,1)} %pad_maximum_fusion), calls=%async_computation | async-start | bytes 524288 | tf_op jit(solution)/shard_map/all_to_all | solution.py:403
  10.6 0.7 %pad_maximum_fusion.2 = f32[3072]{0:T(1024)S(1)} fusion(f32[512]{0:T(512)} %param.15, f32[512]{0:T(512)} %param.14, f32[1024]{0:T(1024)} %param.12, f32[1024]{0:T(1024)} %param.11), kind=kLoop, calls=%fused_computation.2 | loop fusion | flops 9216 | bytes 24576 | tf_op jit(solution)/shard_map/concatenate | solution.py:455
  11.3 0.0 copy-start
  11.3 1.2 %copy-done = bf16[512,1024]{1,0:T(8,128)(2,1)S(1)} copy-done((bf16[512,1024]{1,0:T(8,128)(2,1)S(1)}, bf16[512,1024]{1,0:T(8,128)(2,1)}, u32[]{:S(2)}) %copy-start) | copy-done | bytes 1048600
  12.5 0.0 copy-start.1
  12.5 1.2 %copy-done.1 = bf16[512,1024]{1,0:T(8,128)(2,1)S(1)} copy-done((bf16[512,1024]{1,0:T(8,128)(2,1)S(1)}, bf16[512,1024]{1,0:T(8,128)(2,1)}, u32[]{:S(2)}) %copy-start.1) | copy-done | bytes 1048600
  13.8 0.1 keep_weights.1
  13.9 6.5 %all-to-all-done.rows_ref = bf16[16,16,512]{2,1,0:T(8,128)(2,1)S(1)} async-done(((bf16[16,16,512]{2,1,0:T(8,128)(2,1)}), bf16[16,16,512]{2,1,0:T(8,128)(2,1)S(1)}, u32[]{:S(2)}, u32[]{:S(2)}) %all-to-all-start) | async-done | bytes 262176 | tf_op jit(solution)/shard_map/all_to_all | solution.py:403
  20.4 6.8 %switch_layers.1 = (bf16[2096,128]{1,0:T(8,128)(2,1)S(1)}, bf16[2,512,1024]{2,1,0:T(8,128)(2,1)S(1)}, bf16[2,2,512,256]{3,2,1,0:T(8,128)(2,1)S(1)}, bf16[128,512]{1,0:T(8,128)(2,1)S(1)}, f32[24,128]{1,0:T(8,128)S(1)}) custom-call(bf16[16,16,512]{2,1,0:T(8,128)(2,1)S(1)} %all-to-all-done.rows_ref, bf16[512,1024]{1,0:T(8,128)(2,1)S(1)} %get-tuple-element.28.win_ref, ...), custom_call_target="tpu_custom_call" | custom-call | tf_op jit(solution)/shard_map/switch_layers/pallas_call | solution.py:422
  27.2 0.1 collective-permute-start
  27.3 1.2 %own_part.1 = (f32[2048,128]{1,0:T(8,128)S(1)}, bf16[8,64,128]{2,1,0:T(8,128)(2,1)S(1)}) custom-call(bf16[2,512,1024]{2,1,0:T(8,128)(2,1)S(1)} %get-tuple-element.31.both_ref, bf16[2,2,512,256]{3,2,1,0:T(8,128)(2,1)S(1)} %get-tuple-element.32.side_ref, bf16[128,512]{1,0:T(8,128)(2,1)S(1)} %get-tuple-element.33.first_ref, ...), custom_call_target="tpu_custom_call" | custom-call | tf_op jit(solution)/shard_map/own_part/pallas_call | solution.py:470
  28.5 0.7 %collective-permute-done.other_ref = bf16[2096,128]{1,0:T(8,128)(2,1)S(1)} collective-permute-done((bf16[2096,128]{1,0:T(8,128)(2,1)S(1)}, bf16[2096,128]{1,0:T(8,128)(2,1)S(1)}, u32[]{:S(2)}, u32[]{:S(2)}) %collective-permute-start) | collective-permute-done | bytes 536608 | tf_op jit(solution)/shard_map/ppermute | solution.py:407
  29.2 0.1 core_sum.1
  29.3 14.3 %all_to_all.15.got_ref = bf16[8,368,128]{2,1,0:T(8,128)(2,1)S(1)} all-to-all(bf16[8,368,128]{2,1,0:T(8,128)(2,1)S(1)} %core_sum.1), channel_id=1, replica_groups={{0,14,2,12,4,10,6,8},{1,15,3,13,5,11,7,9},{16,30,18,28,20,26,22,24},{17..., dimensions={0} | all-to-all | bytes 1507328 | tf_op jit(solution)/shard_map/all_to_all | solution.py:403
  43.7 0.1 slice_sum.1.slice_ref
  43.7 1.2 %collective-permute-start.1 = (bf16[32,1024]{1,0:T(8,128)(2,1)S(1)}, bf16[32,1024]{1,0:T(8,128)(2,1)S(1)}, u32[]{:S(2)}, u32[]{:S(2)}) collective-permute-start(bf16[32,1024]{1,0:T(8,128)(2,1)S(1)} %slice_sum.1.slice_ref), channel_id=1, source_target_pairs={{0,16},{1,17},{2,18},{3,19},{4,20},{5,21},{6,22},{7,23},{8,24},{9,... | collective-permute-start | bytes 196616 | tf_op jit(solution)/shard_map/ppermute | solution.py:407
  44.9 4.0 %collective-permute-done.1.slice_ref = bf16[32,1024]{1,0:T(8,128)(2,1)S(1)} collective-permute-done((bf16[32,1024]{1,0:T(8,128)(2,1)S(1)}, bf16[32,1024]{1,0:T(8,128)(2,1)S(1)}, u32[]{:S(2)}, u32[]{:S(2)}) %collective-permute-start.1) | collective-permute-done | bytes 65568 | tf_op jit(solution)/shard_map/ppermute | solution.py:407
  49.0 16.6 %all_to_all.16.mine_ref = bf16[8,2,32,1024]{3,2,1,0:T(8,128)(2,1)S(1)} all-to-all(bf16[8,2,32,1024]{3,2,1,0:T(8,128)(2,1)S(1)} %spread_twin.1), channel_id=1, replica_groups={{0,2,4,6,8,10,12,14},{1,3,5,7,9,11,13,15},{16,18,20,22,24,26,28,30},{17..., dimensions={0} | all-to-all | bytes 2097152 | tf_op jit(solution)/shard_map/all_to_all | solution.py:403
  65.6 0.0 collective-permute-start.2
  65.6 0.7 rows_out.1
  66.3 1.1 %mine_out.1 = (bf16[2,8,32,1024]{3,2,1,0:T(8,128)(2,1)}, bf16[2,8,32,1024]{3,2,1,0:T(8,128)(2,1)}) custom-call(bf16[8,2,32,1024]{3,2,1,0:T(8,128)(2,1)S(1)} %all_to_all.16.mine_ref), custom_call_target="tpu_custom_call" | custom-call | tf_op jit(solution)/shard_map/mine_out/pallas_call | solution.py:546
  67.4 0.9 %collective-permute-done.2.other_ref = bf16[8,2,32,1024]{3,2,1,0:T(8,128)(2,1)S(1)} collective-permute-done((bf16[8,2,32,1024]{3,2,1,0:T(8,128)(2,1)S(1)}, bf16[8,2,32,1024]{3,2,1,0:T(8,128)(2,1)S(1)}, u32[]{:S(2)}, u32[]{:S(2)}) %collective-permute-start.2) | collective-permute-done | bytes 1048608 | tf_op jit(solution)/shard_map/ppermute | solution.py:407
  68.3 1.1 %other_out.1 = (bf16[2,8,32,1024]{3,2,1,0:T(8,128)(2,1)}, bf16[2,8,32,1024]{3,2,1,0:T(8,128)(2,1)}) custom-call(bf16[8,2,32,1024]{3,2,1,0:T(8,128)(2,1)S(1)} %collective-permute-done.2.other_ref, bf16[2,8,32,1024]{3,2,1,0:T(8,128)(2,1)} %get-tuple-element.40.first_in, ...), custom_call_target="tpu_custom_call", output_to_operand_aliasing={{0}: (1, {}), {1}: (2, {})} | custom-call | tf_op jit(solution)/shard_map/other_out/pallas_call | solution.py:555
  (2 shorter events, 0.1 us)
Async XLA Ops:
  2.2 18.2 %all-to-all-start = ((bf16[16,16,512]{2,1,0:T(8,128)(2,1)}), bf16[16,16,512]{2,1,0:T(8,128)(2,1)S(1)}, u32[]{:S(2)}, u32[]{:S(2)}) async-start(bf16[16,16,512]{2,1,0:T(8,128)(2,1)} %pad_maximum_fusion), calls=%async_computation | async-start | bytes 524288 | tf_op jit(solution)/shard_map/all_to_all | solution.py:403
  11.3 1.2 %copy-start = (bf16[512,1024]{1,0:T(8,128)(2,1)S(1)}, bf16[512,1024]{1,0:T(8,128)(2,1)}, u32[]{:S(2)}) copy-start(bf16[512,1024]{1,0:T(8,128)(2,1)} %refs_0_.1) | copy-start | bytes 3145732
  12.5 1.2 %copy-start.1 = (bf16[512,1024]{1,0:T(8,128)(2,1)S(1)}, bf16[512,1024]{1,0:T(8,128)(2,1)}, u32[]{:S(2)}) copy-start(bf16[512,1024]{1,0:T(8,128)(2,1)} %refs_1_.1) | copy-start | bytes 3145732
  27.2 2.0 %collective-permute-start = (bf16[2096,128]{1,0:T(8,128)(2,1)S(1)}, bf16[2096,128]{1,0:T(8,128)(2,1)S(1)}, u32[]{:S(2)}, u32[]{:S(2)}) collective-permute-start(bf16[2096,128]{1,0:T(8,128)(2,1)S(1)} %get-tuple-element.37), channel_id=1, source_target_pairs={{0,1},{1,0},{2,3},{3,2},{4,5},{5,4},{6,7},{7,6},{8,9},{9,8},{10,11... | collective-permute-start | bytes 1609736 | tf_op jit(solution)/shard_map/ppermute | solution.py:407
  43.7 5.2 %collective-permute-start.1 = (bf16[32,1024]{1,0:T(8,128)(2,1)S(1)}, bf16[32,1024]{1,0:T(8,128)(2,1)S(1)}, u32[]{:S(2)}, u32[]{:S(2)}) collective-permute-start(bf16[32,1024]{1,0:T(8,128)(2,1)S(1)} %slice_sum.1.slice_ref), channel_id=1, source_target_pairs={{0,16},{1,17},{2,18},{3,19},{4,20},{5,21},{6,22},{7,23},{8,24},{9,... | collective-permute-start | bytes 196616 | tf_op jit(solution)/shard_map/ppermute | solution.py:407
  65.6 2.7 %collective-permute-start.2 = (bf16[8,2,32,1024]{3,2,1,0:T(8,128)(2,1)S(1)}, bf16[8,2,32,1024]{3,2,1,0:T(8,128)(2,1)S(1)}, u32[]{:S(2)}, u32[]{:S(2)}) collective-permute-start(bf16[8,2,32,1024]{3,2,1,0:T(8,128)(2,1)S(1)} %all_to_all.16.mine_ref), channel_id=1, source_target_pairs={{0,1},{1,0},{2,3},{3,2},{4,5},{5,4},{6,7},{7,6},{8,9},{9,8},{10,11... | collective-permute-start | bytes 3145736 | tf_op jit(solution)/shard_map/ppermute | solution.py:407
